TPU v7x, 32 devices: a whole 2x2x4 slice. The times are simulated.
32 devices in a mesh: dp: 4 (over z), ctx: 8 (over y, x, core).
Axes of the slice: x: 2, y: 2, z: 4, core: 2. Of those that a mesh axis runs over, the one named last changes fastest.
Arguments:
- inputs: bfloat16 [4, 4096, 1536], P(None, ('dp', 'ctx')), may hold values from -6 to 6
- doc_ids: int32 [4, 4096], P(None, ('dp', 'ctx')), may hold values from 1 to 3, as said below
- cotangent: bfloat16 [4, 4096, 1536], P(None, ('dp', 'ctx')), may hold values from -6 to 6
- attend_in: float32 [1536, 3072], P(('dp', 'ctx')), may hold values from -0.15625 to 0.15625
- attend_out: float32 [1536, 1536], P(('dp', 'ctx')), may hold values from -1.75 to 1.75
- gains: float32 [2, 1536], P(None, ('dp', 'ctx')), may hold values from 0.5 to 1.5
- expand: float32 [1536, 8192], P(('dp', 'ctx')), may hold values from -0.15625 to 0.15625
- contract: float32 [4096, 1536], P(('dp', 'ctx')), may hold values from -0.09375 to 0.09375
- attend_in_first: float32 [1536, 3072], P(('dp', 'ctx'))
- attend_in_second: float32 [1536, 3072], P(('dp', 'ctx')), as said below
- attend_out_first: float32 [1536, 1536], P(('dp', 'ctx'))
- attend_out_second: float32 [1536, 1536], P(('dp', 'ctx')), as said below
- gains_first: float32 [2, 1536], P(None, ('dp', 'ctx'))
- gains_second: float32 [2, 1536], P(None, ('dp', 'ctx')), as said below
- expand_first: float32 [1536, 8192], P(('dp', 'ctx'))
- expand_second: float32 [1536, 8192], P(('dp', 'ctx')), as said below
- contract_first: float32 [4096, 1536], P(('dp', 'ctx'))
- contract_second: float32 [4096, 1536], P(('dp', 'ctx')), as said below
Outputs:
- block_out: bfloat16 [4, 4096, 1536], P(None, ('dp', 'ctx'))
- grad_inputs: bfloat16 [4, 4096, 1536], P(None, ('dp', 'ctx'))
- new_attend_in: float32 [1536, 3072], P(('dp', 'ctx'))
- new_attend_in_first: float32 [1536, 3072], P(('dp', 'ctx'))
- new_attend_in_second: float32 [1536, 3072], P(('dp', 'ctx'))
- new_attend_out: float32 [1536, 1536], P(('dp', 'ctx'))
- new_attend_out_first: float32 [1536, 1536], P(('dp', 'ctx'))
- new_attend_out_second: float32 [1536, 1536], P(('dp', 'ctx'))
- new_gains: float32 [2, 1536], P(None, ('dp', 'ctx'))
- new_gains_first: float32 [2, 1536], P(None, ('dp', 'ctx'))
- new_gains_second: float32 [2, 1536], P(None, ('dp', 'ctx'))
- new_expand: float32 [1536, 8192], P(('dp', 'ctx'))
- new_expand_first: float32 [1536, 8192], P(('dp', 'ctx'))
- new_expand_second: float32 [1536, 8192], P(('dp', 'ctx'))
- new_contract: float32 [4096, 1536], P(('dp', 'ctx'))
- new_contract_first: float32 [4096, 1536], P(('dp', 'ctx'))
- new_contract_second: float32 [4096, 1536], P(('dp', 'ctx'))
Inputs may be any that keep to these rules, and one draw needn't show every extreme that they name: `doc_ids`: each row is 4 streams of 1024 tokens end to end. Within a stream the ids never fall and begin at 1. At each stream place, one of the 4 rows holds a single document that fills the whole stream; the other streams end at id 3. `attend_in_second`: positive. `attend_out_second`: positive. `gains_second`: positive. `expand_second`: positive. `contract_second`: positive.
All inputs are finite; a program needn't handle non-finite values.
Results may differ from a plain program's by a relative error of at most 0.019.
Values may be sent and summed in bfloat16 or wider, within the bound.
No kernel may reach another device: no remote copies, remote signals or barrier semaphores. Data moves between devices by JAX's collectives and lax.ppermute only.
A program may use at most 384 MiB of HBM per device.

v0:
```python
import math

import jax
import jax.numpy as jnp
from jax import lax
from jax.sharding import PartitionSpec as P

D = 1536
HEADS = 16
KV_HEADS = 8
HEAD_DIM = 96
FF = 4096
STEP = 10


EPSILON = 1e-06
ROPE_BASE = 100000.0
BETA_ONE = 0.9
BETA_TWO = 0.95
ADAM_EPSILON = 1e-08
DECAY = 0.1
RATE = 0.3
GAIN_RATE = 0.25


def rotate(values, cosine, sine):
    half = values.shape[-1] // 2
    first, second = (values[..., :half], values[..., half:])
    return jnp.concatenate(
        [first * cosine - second * sine, second * cosine + first * sine], axis=-1
    )


def unrotate(grads, cosine, sine):
    half = grads.shape[-1] // 2
    first, second = (grads[..., :half], grads[..., half:])
    return jnp.concatenate(
        [first * cosine + second * sine, second * cosine - first * sine], axis=-1
    )


def against(left, right):
    return lax.dot_general(
        left, right, (((1,), (1,)), ((), ())), preferred_element_type=jnp.float32
    )


def tokens_product(left, right):
    return lax.dot_general(
        left, right, (((0,), (0,)), ((), ())), preferred_element_type=jnp.float32
    )


def block_split(count):
    size = math.gcd(count, 512)
    return (size, count // size)


def adamw(weight, first, second, grad, rate):
    first_new = BETA_ONE * first + (1.0 - BETA_ONE) * grad
    second_new = BETA_TWO * second + (1.0 - BETA_TWO) * grad * grad
    ratio = (
        first_new
        / (1.0 - BETA_ONE**STEP)
        / (jnp.sqrt(second_new / (1.0 - BETA_TWO**STEP)) + ADAM_EPSILON)
    )
    return (weight - rate * (ratio + DECAY * weight), first_new, second_new)


def norm_back(grad_in, normed, inverse, gain):
    scaled = grad_in * gain
    return inverse * (scaled - normed * jnp.mean(scaled * normed, axis=-1, keepdims=True))


def local(
    inputs,
    doc_ids,
    cotangent,
    attend_in,
    attend_out,
    gains,
    expand,
    contract,
    attend_in_first,
    attend_in_second,
    attend_out_first,
    attend_out_second,
    gains_first,
    gains_second,
    expand_first,
    expand_second,
    contract_first,
    contract_second,
):
    batches, rows_local, width = inputs.shape
    total_rows = batches * rows_local
    place = lax.axis_index("ctx")
    groups = HEADS // KV_HEADS
    qwidth = HEADS * HEAD_DIM
    kwidth = KV_HEADS * HEAD_DIM
    scaling = HEAD_DIM ** (-0.5)
    all_ids = lax.all_gather(doc_ids, "ctx", axis=1, tiled=True)
    stream = all_ids.shape[1]
    query_pos = place * rows_local + jnp.arange(rows_local, dtype=jnp.int32)
    before = jnp.sum((all_ids[:, None, :] < doc_ids[:, :, None]).astype(jnp.int32), axis=-1)
    position = (query_pos[None, :] - before).astype(jnp.float32)
    half = HEAD_DIM // 2
    inverse = jnp.power(ROPE_BASE, -2.0 * jnp.arange(half, dtype=jnp.float32) / HEAD_DIM)
    angles = position.reshape(total_rows)[:, None, None] * inverse
    cosine = jnp.cos(angles)
    sine = jnp.sin(angles)
    in_low, out_low, gains_low = (
        lax.all_gather(attend_in.astype(jnp.bfloat16), ("dp", "ctx"), axis=0, tiled=True),
        lax.all_gather(attend_out.astype(jnp.bfloat16), ("dp", "ctx"), axis=0, tiled=True),
        lax.all_gather(gains.astype(jnp.bfloat16), ("dp", "ctx"), axis=1, tiled=True),
    )
    gain_one = gains_low[0].astype(jnp.float32)
    gain_two = gains_low[1].astype(jnp.float32)
    resid = inputs.astype(jnp.float32).reshape(total_rows, width)
    inv_one = lax.rsqrt(jnp.mean(resid * resid, axis=-1, keepdims=True) + EPSILON)
    normed_one = resid * inv_one
    first_in = (normed_one * gain_one).astype(jnp.bfloat16)
    joined = jnp.dot(first_in, in_low, preferred_element_type=jnp.float32)
    query = rotate(joined[:, :qwidth].reshape(total_rows, HEADS, HEAD_DIM), cosine, sine).astype(
        jnp.bfloat16
    )
    keys = rotate(
        joined[:, qwidth : qwidth + kwidth].reshape(total_rows, KV_HEADS, HEAD_DIM), cosine, sine
    ).astype(jnp.bfloat16)
    values = joined[:, qwidth + kwidth :].astype(jnp.bfloat16)
    query_grid = query.reshape(batches, rows_local, KV_HEADS, groups, HEAD_DIM).transpose(
        0, 2, 3, 1, 4
    )
    key_rows = keys.reshape(batches, rows_local, kwidth)
    value_rows = values.reshape(batches, rows_local, kwidth)

    def allowed(start, count):
        key_ids = lax.dynamic_slice_in_dim(all_ids, start, count, 1)
        key_pos = start + jnp.arange(count, dtype=jnp.int32)
        same = key_ids[:, None, :] == doc_ids[:, :, None]
        causal = key_pos[None, None, :] <= query_pos[None, :, None]
        return (same & causal)[:, None, None]

    def scores_of(key_block):
        count = key_block.shape[1]
        key_grid = key_block.reshape(batches, count, KV_HEADS, HEAD_DIM)
        return (
            jnp.einsum(
                "bkgqd,bckd->bkgqc", query_grid, key_grid, preferred_element_type=jnp.float32
            )
            * scaling
        )

    grid_shape = (batches, KV_HEADS, groups, rows_local)
    initial = (
        jnp.full(grid_shape, -1e30, jnp.float32),
        jnp.zeros(grid_shape, jnp.float32),
        jnp.zeros(grid_shape + (HEAD_DIM,), jnp.float32),
    )
    carry = initial
    key_piece = lax.all_gather(key_rows, "ctx", axis=1, tiled=True)
    value_piece = lax.all_gather(value_rows, "ctx", axis=1, tiled=True)
    size, number = block_split(key_piece.shape[1])

    def one_block(state, index):
        top, weight_sum, accum = state
        offset = index * size
        key_block = lax.dynamic_slice_in_dim(key_piece, offset, size, 1)
        value_block = lax.dynamic_slice_in_dim(value_piece, offset, size, 1)
        logits = scores_of(key_block)
        mask = allowed(offset, size)
        peak = jnp.maximum(top, jnp.max(jnp.where(mask, logits, -1e30), axis=-1))
        weights = jnp.where(mask, jnp.exp(logits - peak[..., None]), 0.0)
        factor = jnp.exp(top - peak)
        weight_sum = weight_sum * factor + jnp.sum(weights, axis=-1)
        value_grid = value_block.reshape(batches, size, KV_HEADS, HEAD_DIM).astype(jnp.float32)
        accum = accum * factor[..., None] + jnp.einsum(
            "bkgqc,bckd->bkgqd", weights, value_grid, precision=lax.Precision.HIGHEST
        )
        return ((peak, weight_sum, accum), None)

    carry, _ = lax.scan(one_block, carry, jnp.arange(number, dtype=jnp.int32))
    top, weight_sum, accum = carry
    attended = accum / weight_sum[..., None]
    logsum = top + jnp.log(weight_sum)
    att_low = attended.transpose(0, 3, 1, 2, 4).reshape(total_rows, qwidth).astype(jnp.bfloat16)
    hidden_res = resid + jnp.dot(att_low, out_low, preferred_element_type=jnp.float32)
    inv_two = lax.rsqrt(jnp.mean(hidden_res * hidden_res, axis=-1, keepdims=True) + EPSILON)
    normed_two = hidden_res * inv_two
    second_in = (normed_two * gain_two).astype(jnp.bfloat16)
    columns = second_in
    gate_up = jnp.dot(
        columns,
        lax.all_gather(expand.astype(jnp.bfloat16), ("dp", "ctx"), axis=0, tiled=True),
        preferred_element_type=jnp.float32,
    )
    gate = gate_up[:, :FF]
    upward = gate_up[:, FF:]
    sigmoid_gate = jax.nn.sigmoid(gate)
    activated = gate * sigmoid_gate
    mixed = (activated * upward).astype(jnp.bfloat16)
    columns = mixed
    contracted = jnp.dot(
        columns,
        lax.all_gather(contract.astype(jnp.bfloat16), ("dp", "ctx"), axis=0, tiled=True),
        preferred_element_type=jnp.float32,
    )
    block_out = (hidden_res + contracted).astype(jnp.bfloat16).reshape(batches, rows_local, width)
    upstream = cotangent.reshape(total_rows, width)
    in_back, out_back, gains_back = (
        lax.all_gather(attend_in.astype(jnp.bfloat16), ("dp", "ctx"), axis=0, tiled=True),
        lax.all_gather(attend_out.astype(jnp.bfloat16), ("dp", "ctx"), axis=0, tiled=True),
        lax.all_gather(gains.astype(jnp.bfloat16), ("dp", "ctx"), axis=1, tiled=True),
    )
    back_one = gains_back[0].astype(jnp.float32)
    back_two = gains_back[1].astype(jnp.float32)
    mixed_grad = against(
        upstream, lax.all_gather(contract.astype(jnp.bfloat16), ("dp", "ctx"), axis=0, tiled=True)
    )
    gate_grad = mixed_grad * upward * sigmoid_gate * (1.0 + gate * (1.0 - sigmoid_gate))
    up_grad = mixed_grad * activated
    gate_up_grad = jnp.concatenate([gate_grad, up_grad], axis=1).astype(jnp.bfloat16)
    second_grad = against(
        gate_up_grad, lax.all_gather(expand.astype(jnp.bfloat16), ("dp", "ctx"), axis=0, tiled=True)
    )
    gain_two_grad = jnp.sum(second_grad * normed_two, axis=0)
    hidden_grad = upstream.astype(jnp.float32) + norm_back(
        second_grad, normed_two, inv_two, back_two
    )
    branch_grad = hidden_grad.astype(jnp.bfloat16)
    att_grad = against(branch_grad, out_back).astype(jnp.bfloat16)
    out_grid = att_grad.reshape(batches, rows_local, KV_HEADS, groups, HEAD_DIM).transpose(
        0, 2, 3, 1, 4
    )
    out_float = out_grid.astype(jnp.float32)
    delta = jnp.sum(out_float * attended, axis=-1)
    key_all, value_all = (
        lax.all_gather(key_rows, "ctx", axis=1, tiled=True),
        lax.all_gather(value_rows, "ctx", axis=1, tiled=True),
    )

    def slopes(key_block, value_block, start):
        count = key_block.shape[1]
        logits = scores_of(key_block)
        mask = allowed(start, count)
        weights = jnp.where(mask, jnp.exp(logits - logsum[..., None]), 0.0)
        value_grid = value_block.reshape(batches, count, KV_HEADS, HEAD_DIM)
        weight_grad = jnp.einsum(
            "bkgqd,bckd->bkgqc", out_grid, value_grid, preferred_element_type=jnp.float32
        )
        logit_grad = (weights * (weight_grad - delta[..., None])).astype(jnp.bfloat16)
        return (weights, logit_grad)

    size_all, number_all = block_split(stream)

    def query_step(index, total):
        offset = index * size_all
        key_block = lax.dynamic_slice_in_dim(key_all, offset, size_all, 1)
        value_block = lax.dynamic_slice_in_dim(value_all, offset, size_all, 1)
        weights, logit_grad = slopes(key_block, value_block, offset)
        key_grid = key_block.reshape(batches, size_all, KV_HEADS, HEAD_DIM)
        return total + jnp.einsum(
            "bkgqc,bckd->bkgqd", logit_grad, key_grid, preferred_element_type=jnp.float32
        )

    query_grad = (
        lax.fori_loop(0, number_all, query_step, jnp.zeros(grid_shape + (HEAD_DIM,), jnp.float32))
        * scaling
    )

    def key_block_terms(index):
        offset = index * size_all
        key_block = lax.dynamic_slice_in_dim(key_all, offset, size_all, 1)
        value_block = lax.dynamic_slice_in_dim(value_all, offset, size_all, 1)
        weights, logit_grad = slopes(key_block, value_block, offset)
        key_part = (
            jnp.einsum(
                "bkgqc,bkgqd->bckd", logit_grad, query_grid, preferred_element_type=jnp.float32
            )
            * scaling
        )
        value_part = jnp.einsum(
            "bkgqc,bkgqd->bckd", weights, out_float, precision=lax.Precision.HIGHEST
        )
        return jnp.concatenate(
            [
                key_part.reshape(batches, size_all, kwidth),
                value_part.reshape(batches, size_all, kwidth),
            ],
            axis=-1,
        )

    stacked = lax.map(key_block_terms, jnp.arange(number_all, dtype=jnp.int32))
    pair_terms = stacked.transpose(0, 2, 1, 3).reshape(stream, batches, 2 * kwidth)
    pair_grads = lax.psum_scatter(
        pair_terms.astype(jnp.bfloat16), "ctx", scatter_dimension=0, tiled=True
    ).astype(jnp.float32)
    pair_grads = pair_grads.transpose(1, 0, 2).reshape(total_rows, 2 * kwidth)
    keys_grad = unrotate(
        pair_grads[:, :kwidth].reshape(total_rows, KV_HEADS, HEAD_DIM), cosine, sine
    )
    queries_grad = unrotate(
        query_grad.transpose(0, 3, 1, 2, 4).reshape(total_rows, HEADS, HEAD_DIM), cosine, sine
    )
    joined_grad = jnp.concatenate(
        [
            queries_grad.reshape(total_rows, qwidth),
            keys_grad.reshape(total_rows, kwidth),
            pair_grads[:, kwidth:],
        ],
        axis=1,
    ).astype(jnp.bfloat16)
    first_grad = against(joined_grad, in_back)
    gain_one_grad = jnp.sum(first_grad * normed_one, axis=0)
    resid_grad = hidden_grad + norm_back(first_grad, normed_one, inv_one, back_one)
    grad_inputs = resid_grad.astype(jnp.bfloat16).reshape(batches, rows_local, width)
    in_term = tokens_product(first_in, joined_grad)
    out_term = tokens_product(att_low, branch_grad)
    gain_term = jnp.stack([gain_one_grad, gain_two_grad])
    expand_term = tokens_product(second_in, gate_up_grad)
    contract_term = tokens_product(mixed, upstream)
    in_sum, out_sum, gain_sum, expand_sum, contract_sum = (
        lax.psum_scatter(in_term, ("dp", "ctx"), scatter_dimension=0, tiled=True),
        lax.psum_scatter(out_term, ("dp", "ctx"), scatter_dimension=0, tiled=True),
        lax.psum_scatter(gain_term, ("dp", "ctx"), scatter_dimension=1, tiled=True),
        lax.psum_scatter(expand_term, ("dp", "ctx"), scatter_dimension=0, tiled=True),
        lax.psum_scatter(contract_term, ("dp", "ctx"), scatter_dimension=0, tiled=True),
    )
    out_fan = max(1, HEADS * HEAD_DIM // (rows_local * lax.axis_size("ctx") // 8))
    new_in = adamw(attend_in, attend_in_first, attend_in_second, in_sum, RATE / math.sqrt(D))
    new_out = adamw(
        attend_out, attend_out_first, attend_out_second, out_sum, RATE / math.sqrt(out_fan)
    )
    new_gain = adamw(gains, gains_first, gains_second, gain_sum, GAIN_RATE)
    new_expand = adamw(expand, expand_first, expand_second, expand_sum, RATE / math.sqrt(D))
    new_contract = adamw(
        contract, contract_first, contract_second, contract_sum, RATE / math.sqrt(FF)
    )
    return (
        block_out,
        grad_inputs,
        new_in[0],
        new_in[1],
        new_in[2],
        new_out[0],
        new_out[1],
        new_out[2],
        new_gain[0],
        new_gain[1],
        new_gain[2],
        new_expand[0],
        new_expand[1],
        new_expand[2],
        new_contract[0],
        new_contract[1],
        new_contract[2],
    )


def solution(mesh):
    return jax.shard_map(
        local,
        mesh=mesh,
        in_specs=(
            P(None, ("dp", "ctx"), None),
            P(None, ("dp", "ctx")),
            P(None, ("dp", "ctx"), None),
            P(("dp", "ctx"), None),
            P(("dp", "ctx"), None),
            P(None, ("dp", "ctx")),
            P(("dp", "ctx"), None),
            P(("dp", "ctx"), None),
            P(("dp", "ctx"), None),
            P(("dp", "ctx"), None),
            P(("dp", "ctx"), None),
            P(("dp", "ctx"), None),
            P(None, ("dp", "ctx")),
            P(None, ("dp", "ctx")),
            P(("dp", "ctx"), None),
            P(("dp", "ctx"), None),
            P(("dp", "ctx"), None),
            P(("dp", "ctx"), None),
        ),
        out_specs=(
            P(None, ("dp", "ctx"), None),
            P(None, ("dp", "ctx"), None),
            P(("dp", "ctx"), None),
            P(("dp", "ctx"), None),
            P(("dp", "ctx"), None),
            P(("dp", "ctx"), None),
            P(("dp", "ctx"), None),
            P(("dp", "ctx"), None),
            P(None, ("dp", "ctx")),
            P(None, ("dp", "ctx")),
            P(None, ("dp", "ctx")),
            P(("dp", "ctx"), None),
            P(("dp", "ctx"), None),
            P(("dp", "ctx"), None),
            P(("dp", "ctx"), None),
            P(("dp", "ctx"), None),
            P(("dp", "ctx"), None),
        ),
        check_vma=False,
    )
```

profile of v0, /device:TPU:0, one launch (start us, length us, event | category | flops | bytes accessed | tf_op | source)
XLA Modules:
  0.0 1998.3 jit_solution(16975246588685114009)
XLA Ops:
  9.9 43.0 %all-gather = bf16[32,48,2]{1,2,0:T(2,128)(2,1)S(1)} all-gather(bf16[1,48,2]{1,2,0:T(2,128)(2,1)S(1)} %convert_bitcast_fusion.1), channel_id=1, replica_groups=mesh['dp'=4,'ctx'=8] {'dp','ctx'}, dimensions={0}, use_global_device_ids=true | all-gather | bytes 6336 | tf_op jit(solution)/shard_map/all_gather | solution.py:115
  66.0 30.4 %all-gather.8.cloned.1.call-done = bf16[1536,3072]{1,0:T(8,128)(2,1)} async-done(((bf16[48,3072]{1,0:T(8,128)(2,1)}), bf16[1536,3072]{1,0:T(8,128)(2,1)}) %all-gather.8.cloned.1.call-update) | async-done | bytes 9437200 | tf_op jit(solution)/shard_map/all_gather | solution.py:113
  128.0 50.9 %all-gather.10.cloned.1.call-done = bf16[4,1024,768]{1,0,2:T(4,128)(2,1)} async-done(((bf16[4,128,768]{1,0,2:T(4,128)(2,1)}), bf16[4,1024,768]{1,0,2:T(4,128)(2,1)}) %all-gather.10.cloned.1.call-update) | async-done | bytes 6291472 | tf_op jit(solution)/shard_map/all_gather | solution.py:161
  186.4 41.6 %all-gather.12.cloned.1.call-done = bf16[4,1024,768]{1,2,0:T(8,128)(2,1)} async-done(((bf16[4,128,768]{1,2,0:T(8,128)(2,1)}), bf16[4,1024,768]{1,2,0:T(8,128)(2,1)}) %all-gather.12.cloned.1.call-update) | async-done | bytes 6291472 | tf_op jit(solution)/shard_map/all_gather | solution.py:162
  228.0 77.8 %while.41 = (s32[]{:T(128)}, f32[4,8,2,128]{3,2,1,0:T(2,128)S(1)}, f32[4,8,2,128]{3,2,1,0:T(2,128)S(1)}, f32[4,8,2,128,96]{3,4,2,1,0:T(8,128)}, s32[2]{0:T(128)S...) while((s32[]{:T(128)}, f32[4,8,2,128]{3,2,1,0:T(2,128)S(1)}, ...), condition=%wide.region_5.6_spmd.clone, body=%wide.region_2.5_spmd.clone.sunk | while | flops 5682078208 | bytes 78806248 | solution.py:182
  252.0 14.4 fusion.141
  290.3 15.2 fusion.141
  319.1 132.7 %all-gather.16.cloned.1.call-done = bf16[1536,8192]{1,0:T(8,128)(2,1)} async-done(((bf16[48,8192]{1,0:T(8,128)(2,1)}), bf16[1536,8192]{1,0:T(8,128)(2,1)}) %all-gather.16.cloned.1.call-update) | async-done | bytes 25165840 | tf_op jit(solution)/shard_map/all_gather | solution.py:194
  451.8 22.3 %fusion.62 = f32[512,8192]{1,0:T(8,128)} fusion(bf16[1536,8192]{1,0:T(8,128)(2,1)} %all-gather.16.cloned.1.call-done, f32[512,1536]{1,0:T(8,128)} %get-tuple-element.685, f32[1536]{0:T(1024)S(1)} %copy-done.33, f32[512]{0:T(512)S(1)} %add_rsqrt_fusion), kind=kOutput, calls=%fused_computation.158 | convolution fusion | flops 12887261184 | bytes 45096960 | tf_op jit(solution)/shard_map/dot_general | solution.py:192
  474.0 75.2 %all-gather.18.cloned.1.call-done = bf16[4096,1536]{1,0:T(8,128)(2,1)} async-done(((bf16[128,1536]{1,0:T(8,128)(2,1)}), bf16[4096,1536]{1,0:T(8,128)(2,1)}) %all-gather.18.cloned.1.call-update) | async-done | bytes 12582928 | tf_op jit(solution)/shard_map/all_gather | solution.py:205
  549.3 22.1 %multiply_convert_fusion.1 = (bf16[512,4096]{1,0:T(8,128)(2,1)}, bf16[512,4096]{1,0:T(8,128)(2,1)}, bf16[512,4096]{1,0:T(8,128)(2,1)}) fusion(f32[512,8192]{1,0:T(8,128)} %fusion.62, bf16[512,1536]{1,0:T(8,128)(2,1)S(1)} %bitcast.287, bf16[4096,1536]{1,0:T(8,128)(2,1)} %all-gather.18.cloned.1.call-done), kind=kOutput, calls=%fused_computation.69 | convolution fusion | flops 6473908224 | bytes 43515904 | tf_op jit(solution)/shard_map/dot_general | solution.py:43
  571.3 21.7 %multiply_reduce_fusion = (f32[1536]{0:T(1024)}, f32[512]{0:T(512)S(1)}, f32[512,1536]{1,0:T(8,128)}) fusion(f32[512,1536]{1,0:T(8,128)} %get-tuple-element.685, f32[512]{0:T(512)S(1)} %add_rsqrt_fusion, f32[1536]{0:T(1024)S(1)} %copy-done.33, bf16[1536,8192]{1,0:T(8,128)(2,1)} %all-gather.16.cloned.1.call-done, bf16[512,4096]{1,0:T(8,128)(2,1)} %get-tuple-element.670, ...), kind=kOutput, calls=%fused_computation.80 | convolution fusion | flops 12906395648 | bytes 39862272 | tf_op jit(solution)/shard_map/dot_general | solution.py:43
  616.4 134.5 %while.40 = (s32[]{:T(128)}, bf16[2,4,512,1536]{3,2,0,1:T(8,128)(2,1)}, s32[2]{0:T(128)S(1)}, s32[4,1024]{1,0:T(4,128)S(1)}, s32[4,128]{1,0:T(4,128)S(1)}, /*ind...) while((s32[]{:T(128)}, ...), condition=%wide.region_12.13_spmd.clone, body=%wide.region_11.12_spmd.clone.sunk | while | flops 7301825024 | bytes 214433136 | solution.py:293
  627.6 23.1 %fusion.132 = bf16[4,8,512,96,1]{2,3,4,1,0:T(8,128)(2,1)} fusion(f32[4,8,2,128,96]{3,4,2,1,0:T(8,128)} %get-tuple-element.1011, f32[4,8,512,2,128]{4,2,3,1,0:T(8,128)S(1)} %fusion.131, f32[4,8,2,128]{3,2,1,0:T(2,128)S(1)} %get-tuple-element.1007, pred[4,128,512]{1,2,0:T(8,128)(4,1)S(1)} %compare_and_fusion.6), kind=kOutput, calls=%fused_computation.6.clone.1 | convolution fusion | flops 4844421120 | bytes 23363584 | tf_op jit(solution)/shard_map/while/body/eval_jaxpr/bkgqc,bkgqd->bckd/dot_general | solution.py:282
  694.5 23.1 %fusion.132 = bf16[4,8,512,96,1]{2,3,4,1,0:T(8,128)(2,1)} fusion(f32[4,8,2,128,96]{3,4,2,1,0:T(8,128)} %get-tuple-element.1011, f32[4,8,512,2,128]{4,2,3,1,0:T(8,128)S(1)} %fusion.131, f32[4,8,2,128]{3,2,1,0:T(2,128)S(1)} %get-tuple-element.1007, pred[4,128,512]{1,2,0:T(8,128)(4,1)S(1)} %compare_and_fusion.6), kind=kOutput, calls=%fused_computation.6.clone.1 | convolution fusion | flops 4844421120 | bytes 23363584 | tf_op jit(solution)/shard_map/while/body/eval_jaxpr/bkgqc,bkgqd->bckd/dot_general | solution.py:282
  762.2 55.7 %while.42 = (s32[]{:T(128)}, f32[4,8,2,128,96]{3,4,2,1,0:T(8,128)}, s32[4,1024]{1,0:T(4,128)S(1)}, s32[4,128]{1,0:T(4,128)S(1)}, bf16[4,1024,768]{1,2,0:T(8,128)...) while((s32[]{:T(128)}, f32[4,8,2,128,96]{3,4,2,1,0:T(8,128)}, ...), condition=%wide.region_10.11_spmd.clone, body=%wide.region_9.10_spmd.clone.sunk | while | flops 2443248128 | bytes 78347512 | solution.py:267
  828.3 13.4 reduce-scatter.9.cloned.1.call-done
  859.0 15.1 fusion.73
  888.9 25.4 %fusion.39 = f32[1536,8192]{1,0:T(8,128)} fusion(bf16[512,4096]{1,0:T(8,128)(2,1)} %get-tuple-element.670, bf16[512,4096]{1,0:T(8,128)(2,1)} %get-tuple-element.669, f32[512,1536]{1,0:T(8,128)S(1)} %copy-done.11, f32[1536]{0:T(1024)S(1)} %copy-done.34, f32[512]{0:T(512)S(1)} %copy-done.36), kind=kOutput, calls=%fused_computation.73 | convolution fusion | flops 12904038400 | bytes 61874176 | tf_op jit(solution)/shard_map/dot_general | solution.py:49
  926.8 56.4 %reduce-scatter.13.cloned.1.call-done = f32[48,1536]{1,0:T(8,128)} async-done(((f32[1536,1536]{1,0:T(8,128)}), f32[48,1536]{1,0:T(8,128)}) %reduce-scatter.13.cloned.1.call-update) | async-done | bytes 294928 | tf_op jit(solution)/shard_map/reduce_scatter | solution.py:324
  989.5 94.8 %reduce-scatter.19.cloned.1.call-done = f32[48,2]{1,0:T(8,128)} async-done(((f32[1536,2]{1,0:T(8,128)}), f32[48,2]{1,0:T(8,128)}) %reduce-scatter.19.cloned.1.call-update) | async-done | bytes 400
  1085.7 250.5 %reduce-scatter.17.cloned.1.call-done = f32[128,1536]{1,0:T(8,128)} async-done(((f32[4096,1536]{1,0:T(8,128)}), f32[128,1536]{1,0:T(8,128)}) %reduce-scatter.17.cloned.1.call-update) | async-done | bytes 786448 | tf_op jit(solution)/shard_map/reduce_scatter | solution.py:327
  1339.9 209.0 %reduce-scatter.11.cloned.1.call-done = f32[48,3072]{1,0:T(8,128)} async-done(((f32[1536,3072]{1,0:T(8,128)}), f32[48,3072]{1,0:T(8,128)}) %reduce-scatter.11.cloned.1.call-update) | async-done | bytes 589840 | tf_op jit(solution)/shard_map/reduce_scatter | solution.py:323
  1551.5 434.3 %reduce-scatter.15.cloned.1.call-done = f32[48,8192]{1,0:T(8,128)} async-done(((f32[1536,8192]{1,0:T(8,128)}), f32[48,8192]{1,0:T(8,128)}) %reduce-scatter.15.cloned.1.call-update) | async-done | bytes 1572880 | tf_op jit(solution)/shard_map/reduce_scatter | solution.py:326
  (271 shorter events, 364.4 us)
Async XLA Ops:
  7.2 89.2 %all-gather.8.cloned.1.call-start = ((), (), s32[]{:S(2)}) async-start(), calls=%async_computation.6 | async-start | bytes 9732096 | tf_op jit(solution)/shard_map/all_gather | solution.py:113
  9.2 169.7 %all-gather.10.cloned.1.call-start = ((), (), s32[]{:S(2)}) async-start(), calls=%async_computation.7 | async-start | bytes 7077888 | tf_op jit(solution)/shard_map/all_gather | solution.py:161
  108.7 119.3 %all-gather.12.cloned.1.call-start = ((), (), s32[]{:S(2)}) async-start(), calls=%async_computation.8 | async-start | bytes 7077888 | tf_op jit(solution)/shard_map/all_gather | solution.py:162
  111.5 200.2 %all-gather.14.cloned.1.call-start = ((), (), s32[]{:S(2)}) async-start(), calls=%async_computation.9 | async-start | bytes 4866048 | tf_op jit(solution)/shard_map/all_gather | solution.py:114
  113.2 338.6 %all-gather.16.cloned.1.call-start = ((), (), s32[]{:S(2)}) async-start(), calls=%async_computation.10 | async-start | bytes 25952256 | tf_op jit(solution)/shard_map/all_gather | solution.py:194
  114.2 435.0 %all-gather.18.cloned.1.call-start = ((), (), s32[]{:S(2)}) async-start(), calls=%async_computation.11 | async-start | bytes 12976128 | tf_op jit(solution)/shard_map/all_gather | solution.py:205
  115.1 726.7 %reduce-scatter.9.cloned.1.call-start = ((), (), s32[]{:S(2)}) async-start(), calls=%async_computation.12 | async-start | bytes 14155776 | tf_op jit(solution)/shard_map/reduce_scatter | solution.py:295
  128.0 100.0 %copy-start.30 = (s32[4,128]{1,0:T(4,128)S(1)}, s32[4,128]{1,0:T(4,128)}, u32[]{:S(2)}) copy-start(s32[4,128]{1,0:T(4,128)} %param.25) | copy-start | bytes 6148
  311.7 140.1 %copy-start.33 = (f32[1536]{0:T(1024)S(1)}, f32[1536]{0:T(1024)}, u32[]{:S(2)}) copy-start(f32[1536]{0:T(1024)} %get-tuple-element.572) | copy-start | bytes 18436
  319.0 274.0 %copy-start.35 = (f32[512]{0:T(512)}, f32[512]{0:T(512)S(1)}, u32[]{:S(2)}) copy-start(f32[512]{0:T(512)S(1)} %add_rsqrt_fusion) | copy-start | bytes 6148
  451.8 97.5 %copy-start.25 = (bf16[4,128,1536]{2,1,0:T(8,128)(2,1)S(1)}, bf16[4,128,1536]{2,1,0:T(8,128)(2,1)}, u32[]{:S(2)}) copy-start(bf16[4,128,1536]{2,1,0:T(8,128)(2,1)} %param.26) | copy-start | bytes 4718596
  750.9 232.2 %reduce-scatter.13.cloned.1.call-start = ((), (), s32[]{:S(2)}) async-start(), calls=%async_computation.14 | async-start | bytes 9732096 | tf_op jit(solution)/shard_map/reduce_scatter | solution.py:324
  760.4 323.9 %reduce-scatter.19.cloned.1.call-start = ((), (), s32[]{:S(2)}) async-start(), calls=%async_computation.17 | async-start | bytes 811008
  858.9 477.4 %reduce-scatter.17.cloned.1.call-start = ((), (), s32[]{:S(2)}) async-start(), calls=%async_computation.16 | async-start | bytes 25952256 | tf_op jit(solution)/shard_map/reduce_scatter | solution.py:327
  874.1 674.9 %reduce-scatter.11.cloned.1.call-start = ((), (), s32[]{:S(2)}) async-start(), calls=%async_computation.13 | async-start | bytes 19464192 | tf_op jit(solution)/shard_map/reduce_scatter | solution.py:323
  886.9 1098.9 %reduce-scatter.15.cloned.1.call-start = ((), (), s32[]{:S(2)}) async-start(), calls=%async_computation.15 | async-start | bytes 51904512 | tf_op jit(solution)/shard_map/reduce_scatter | solution.py:326
  914.3 71.2 %copy-start.6 = (f32[512,1536]{1,0:T(8,128)S(1)}, f32[512,1536]{1,0:T(8,128)}, u32[]{:S(2)}) copy-start(f32[512,1536]{1,0:T(8,128)} %copy-done.5) | copy-start | bytes 9437188
  985.5 99.6 %copy-start.42 = (f32[2,48]{1,0:T(2,128)S(1)}, f32[2,48]{1,0:T(2,128)}, u32[]{:S(2)}) copy-start(f32[2,48]{1,0:T(2,128)} %param.29) | copy-start | bytes 1156
  985.5 99.6 %copy-start.43 = (f32[2,48]{1,0:T(2,128)S(1)}, f32[2,48]{1,0:T(2,128)}, u32[]{:S(2)}) copy-start(f32[2,48]{1,0:T(2,128)} %param.36) | copy-start | bytes 1156
  985.5 99.6 %copy-start.44 = (f32[2,48]{1,0:T(2,128)S(1)}, f32[2,48]{1,0:T(2,128)}, u32[]{:S(2)}) copy-start(f32[2,48]{1,0:T(2,128)} %param.37) | copy-start | bytes 1156
  989.5 559.5 %copy-start.21 = (f32[48,3072]{1,0:T(8,128)S(1)}, f32[48,3072]{1,0:T(8,128)}, u32[]{:S(2)}) copy-start(f32[48,3072]{1,0:T(8,128)} %param.27) | copy-start | bytes 1769476
  989.5 559.5 %copy-start.31 = (f32[48,3072]{1,0:T(8,128)S(1)}, f32[48,3072]{1,0:T(8,128)}, u32[]{:S(2)}) copy-start(f32[48,3072]{1,0:T(8,128)} %param.32) | copy-start | bytes 1769476
  989.5 559.5 %copy-start.32 = (f32[48,3072]{1,0:T(8,128)S(1)}, f32[48,3072]{1,0:T(8,128)}, u32[]{:S(2)}) copy-start(f32[48,3072]{1,0:T(8,128)} %param.33) | copy-start | bytes 1769476
  1339.9 645.9 %copy-start.14 = (f32[48,8192]{1,0:T(8,128)S(1)}, f32[48,8192]{1,0:T(8,128)}, u32[]{:S(2)}) copy-start(f32[48,8192]{1,0:T(8,128)} %param.30) | copy-start | bytes 4718596
  (38 other events, 541.7 us)
Sparse Core Ops, SparseCore 0:
  11.5 84.8 all-gather.7
  108.9 69.9 all-gather.9
  181.3 46.6 all-gather.11
  231.3 63.6 all-gather.13
  298.3 153.4 all-gather.15
  455.1 94.1 all-gather.17
  751.1 90.6 reduce-scatter.8
  847.6 135.4 reduce-scatter.12
  989.6 94.6 reduce-scatter.18
  1091.7 244.5 reduce-scatter.16
  1342.7 206.2 reduce-scatter.10
  1555.2 430.4 reduce-scatter.14
where the time goes:
time: 2010 us; the launch traced here: 2000 us
  waiting for transfers between devices  1390 us (69%)
  matrix products  337 us (17%)
  local copies, waits for them, and re-layouts  118 us (6%)
  other arithmetic  82.8 us (4%)
  blocking collectives  51.1 us (3%)
    reduce_scatter x1, waiting for transfers between devices, local(): lax.psum_scatter(expand_term, ('dp', 'ctx'), scatter_dimension=0, tiled=T...  434 us
    reduce_scatter x1, waiting for transfers between devices, local(): lax.psum_scatter(contract_term, ('dp', 'ctx'), scatter_dimension=0, tiled...  251 us
    reduce_scatter x1, waiting for transfers between devices, local(): lax.psum_scatter(in_term, ('dp', 'ctx'), scatter_dimension=0, tiled=True)  209 us
    all_gather x1, waiting for transfers between devices, local(): lax.all_gather(expand.astype(jnp.bfloat16), ('dp', 'ctx'), axis=0, tiled=...  133 us
    unnamed x13, waiting for transfers between devices  95 us
    all_gather x1, waiting for transfers between devices, local(): lax.all_gather(contract.astype(jnp.bfloat16), ('dp', 'ctx'), axis=0, tile...  75.2 us
    dot_general x4, matrix products, tokens_product(): lax.dot_general(left, right, (((0,), (0,)), ((), ())), preferred_element_...  59.8 us
    dot_general x4, matrix products, against(): lax.dot_general(left, right, (((1,), (1,)), ((), ())), preferred_element_...  59.8 us
  transfers between devices with their start and end apart: 12, of which 11 were waited for; matrix products, arithmetic and copies ran while one was open for 16% of the time, Pallas kernels for 0%

commit v1 on v0

v1 whole, which is shorter than its diff:
```python
import functools
import math

import jax
import jax.numpy as jnp
import numpy as np
from jax import lax
from jax.experimental import pallas as pl
from jax.experimental.pallas import tpu as pltpu
from jax.sharding import PartitionSpec as P

D = 1536
HEADS = 16
KV_HEADS = 8
HEAD_DIM = 96
FF = 4096
STEP = 10

EPSILON = 1e-06
ROPE_BASE = 100000.0
BETA_ONE = 0.9
BETA_TWO = 0.95
ADAM_EPSILON = 1e-08
DECAY = 0.1
RATE = 0.3
GAIN_RATE = 0.25

HALF = HEAD_DIM // 2
SLOT = 128
SCALING = HEAD_DIM ** (-0.5)
LOG2E = math.log2(math.e)
VMEM_LIMIT = 60 * 1024 * 1024
BF16 = jnp.bfloat16
F32 = jnp.float32
SMALL_COST = pl.CostEstimate(flops=1 << 20, bytes_accessed=1 << 20, transcendentals=0)


def against(left, right):
    return lax.dot_general(left, right, (((1,), (1,)), ((), ())), preferred_element_type=F32)


def tokens_product(left, right):
    return lax.dot_general(left, right, (((0,), (0,)), ((), ())), preferred_element_type=F32)


def product(left, right):
    return jnp.dot(left, right, preferred_element_type=F32)


def adamw(weight, first, second, grad, rate):
    first_new = BETA_ONE * first + (1.0 - BETA_ONE) * grad
    second_new = BETA_TWO * second + (1.0 - BETA_TWO) * grad * grad
    ratio = (
        first_new
        / (1.0 - BETA_ONE**STEP)
        / (jnp.sqrt(second_new / (1.0 - BETA_TWO**STEP)) + ADAM_EPSILON)
    )
    return (weight - rate * (ratio + DECAY * weight), first_new, second_new)


def norm_back(grad_in, normed, inverse, gain):
    scaled = grad_in * gain
    return inverse * (scaled - normed * jnp.mean(scaled * normed, axis=-1, keepdims=True))


def exchange(value, axis, bit=1):
    count = lax.axis_size(axis)
    return lax.ppermute(value, axis, [(i, i ^ bit) for i in range(count)])


def shifted(value, step):
    count = lax.axis_size("dp")
    return lax.ppermute(value, "dp", [(i, (i + step) % count) for i in range(count)])


def total_of(terms):
    total = terms[0].astype(F32)
    for term in terms[1:]:
        total = total + term.astype(F32)
    return total


def taken(value, index, axis):
    return lax.dynamic_index_in_dim(value, index, axis, keepdims=True)


def axis_sum(terms, name, axis):
    mine = lax.axis_index(name)
    sent = total_of([taken(term, 1 - mine, axis) for term in terms]).astype(BF16)
    came = exchange(sent, name)
    return [taken(term, mine, axis) for term in terms] + [came]


def dp_sum(value, *ready):
    came = lax.all_to_all(value, "dp", split_axis=0, concat_axis=0, tiled=True)
    if ready:
        came = after(came, *ready)
    return jnp.sum(came.astype(F32), axis=0)


def column_sum(groups, *ready):
    sums = [total_of(terms).astype(BF16) for terms in groups]
    sums = [one.reshape(one.shape[:1] + one.shape[-2:]) for one in sums]
    return dp_sum(jnp.concatenate(sums, axis=2), *ready)


def after(value, *others):
    return lax.optimization_barrier((value,) + others)[0]


def put(whole, piece, *places):
    index = places + (0,) * (whole.ndim - len(places))
    return lax.dynamic_update_slice(whole, piece.reshape((1,) * len(places) + piece.shape), index)


def dp_gather(shard):
    n_dp = lax.axis_size("dp")
    place = lax.axis_index("dp")
    column = put(jnp.zeros((n_dp,) + shard.shape, shard.dtype), shard, place)
    pieces = [shifted(shard, step) for step in range(1, n_dp)]
    for step, piece in enumerate(pieces):
        column = put(column, piece, (place - step - 1) % n_dp)
    return column, pieces


def plane_parts(value):
    middle = value.shape[-1] // 2
    beside = exchange(value, "lo")
    across = exchange(value, "hi")
    corner = [exchange(beside[..., :middle], "hi"), exchange(across[..., middle:], "lo")]
    return [[value], [beside], [across], corner]


def pack_chunks(rows, width, columns):
    full, rest = divmod(width, columns)
    chunks = [(index * rows, rows, 0, 0, index * columns, columns) for index in range(full)]
    if rest:
        count = columns // rest
        part = rows // count
        chunks += [
            (full * rows, part, index * rest, index * part, full * columns, rest)
            for index in range(count)
        ]
    return chunks


def packed_rows(value, columns):
    rows, width = value.shape
    packed = jnp.zeros((rows * width // columns, columns), value.dtype)
    for to_row, count, to_column, row, column, size in pack_chunks(rows, width, columns):
        part = value[row : row + count, column : column + size]
        packed = lax.dynamic_update_slice(packed, part, (to_row, to_column))
    return packed


def unpacked_rows(packed, rows, width):
    columns = packed.shape[-1]
    whole = jnp.zeros(packed.shape[:-2] + (rows, width), packed.dtype)
    lead = (0,) * (packed.ndim - 2)
    for to_row, count, to_column, row, column, size in pack_chunks(rows, width, columns):
        part = packed[..., to_row : to_row + count, to_column : to_column + size]
        whole = lax.dynamic_update_slice(whole, part, lead + (row, column))
    return whole


def relative_gather(value):
    pieces = [value]
    bit = 1
    while bit < lax.axis_size("tp"):
        pieces = pieces + [exchange(piece, "tp", bit) for piece in pieces]
        bit *= 2
    return pieces


def relative_sum(pieces):
    pieces = list(pieces)
    bit = len(pieces) // 2
    while bit:
        for index in range(bit):
            came = exchange(pieces[index + bit].astype(BF16), "tp", bit)
            pieces[index] = pieces[index].astype(F32) + came.astype(F32)
        bit //= 2
    return pieces[0]


def group_gather(value):
    if lax.axis_size("tp") != 2:
        return lax.all_gather(value, "tp", axis=0, tiled=True)
    came = exchange(value, "tp")
    first = lax.axis_index("tp") == 0
    return jnp.concatenate([jnp.where(first, value, came), jnp.where(first, came, value)], axis=0)


def group_swap(value):
    if lax.axis_size("tp") != 2:
        return lax.all_to_all(value, "tp", split_axis=0, concat_axis=0, tiled=True)
    me = lax.axis_index("tp")
    mine = taken(value, me, 0)
    came = exchange(taken(value, 1 - me, 0), "tp")
    return jnp.concatenate([jnp.where(me == 0, mine, came), jnp.where(me == 0, came, mine)], axis=0)


CTX = ("hi", "lo", "tp")


def ctx_swap(value):
    return lax.all_to_all(value, CTX, split_axis=0, concat_axis=0, tiled=True)


def stream_moves(batches):
    group = lax.axis_size("tp")
    count = batches * group
    return [
        [(i, group * ((i + step) % batches) + i // batches) for i in range(count)]
        for step in range(batches)
    ]


def to_streams(value):
    batches = value.shape[0]
    me = lax.axis_index(CTX)
    stream = me // lax.axis_size("tp")
    whole = jnp.zeros_like(value)
    for step, pairs in enumerate(stream_moves(batches)):
        piece = lax.ppermute(taken(value, (me + step) % batches, 0), CTX, pairs)
        whole = lax.dynamic_update_slice_in_dim(whole, piece, (stream - step) % batches, 0)
    return whole


def from_streams(value):
    batches = value.shape[0]
    me = lax.axis_index(CTX)
    stream = me // lax.axis_size("tp")
    whole = jnp.zeros_like(value)
    for step, pairs in enumerate(stream_moves(batches)):
        back = [(b, a) for a, b in pairs]
        piece = lax.ppermute(taken(value, (stream - step) % batches, 0), CTX, back)
        whole = lax.dynamic_update_slice_in_dim(whole, piece, (me + step) % batches, 0)
    return whole


GROUP = HEADS // KV_HEADS
SLOTS = GROUP + 2
JOINED = SLOTS * HEAD_DIM
PAIR = 2


def placement(slots):
    matrix = np.zeros((slots * HEAD_DIM, slots * SLOT), np.float32)
    for slot in range(slots):
        for half in range(2):
            for m in range(HALF):
                matrix[slot * HEAD_DIM + half * HALF + m, slot * SLOT + half * (SLOT // 2) + m] = 1
    return matrix


def mask_of(start, first_row, rows, keys):
    row = first_row + lax.broadcasted_iota(jnp.int32, (rows, keys), 0)
    column = lax.broadcasted_iota(jnp.int32, (rows, keys), 1)
    return (column >= start) & (column <= row)


def columns_of(group, slot):
    first = (group * SLOTS + slot) * SLOT
    return slice(first, first + SLOT)


def forward_kernel(block, joined_ref, table_ref, start_ref, place_ref, back_ref,
                   out_ref, kept_ref, logsum_ref):
    length = joined_ref.shape[0]
    cosine = table_ref[:, :SLOT]
    sine = table_ref[:, SLOT:]
    for group in range(PAIR):
        joined = joined_ref[:, group * JOINED : (group + 1) * JOINED]
        placed = product(joined, place_ref[...])
        for slot in range(SLOTS):
            part = placed[:, slot * SLOT : (slot + 1) * SLOT]
            if slot <= GROUP:
                part = part * cosine + pltpu.roll(part, SLOT // 2, 1) * sine
            if slot < GROUP:
                part = part * (SCALING * LOG2E)
            kept_ref[:, columns_of(group, slot)] = part.astype(BF16)
    lane = lax.broadcasted_iota(jnp.int32, (block, SLOT), 1)
    for first in range(0, length, block):
        rows = slice(first, first + block)
        count = first + block
        mask = mask_of(start_ref[rows, :], first, block, count)
        outs = []
        logsums = jnp.zeros((block, SLOT), F32)
        for group in range(PAIR):
            keys = kept_ref[:count, columns_of(group, GROUP)]
            values = kept_ref[:count, columns_of(group, GROUP + 1)]
            for head in range(GROUP):
                logits = against(kept_ref[rows, columns_of(group, head)], keys)
                logits = jnp.where(mask, logits, -1e30)
                peak = jnp.max(logits, axis=-1, keepdims=True)
                weights = jnp.exp2(logits - peak)
                total = jnp.sum(weights, axis=-1, keepdims=True)
                outs.append((product(weights.astype(BF16), values) / total).astype(BF16))
                logsums = jnp.where(
                    lane == group * GROUP + head, peak + jnp.log2(total), logsums
                )
        logsum_ref[0, rows, :] = logsums
        out_ref[rows, :] = product(jnp.concatenate(outs, axis=1), back_ref[...]).astype(BF16)


def backward_kernel(block, kept_ref, table_ref, start_ref, logsum_ref, att_ref, grad_ref,
                    place_ref, back_ref, out_ref):
    length = kept_ref.shape[0]
    att = product(att_ref[...], place_ref[...])
    grad = product(grad_ref[...], place_ref[...])
    both = att * grad
    grad_low = grad.astype(BF16)
    blocks = length // block

    def add(store, index, value):
        store[index] = value if store[index] is None else store[index] + value

    for group in range(PAIR):
        key_grads = [None] * blocks
        value_grads = [None] * blocks
        query_grads = [[None] * blocks for _ in range(GROUP)]
        for step in range(blocks):
            first = step * block
            rows = slice(first, first + block)
            count = first + block
            mask = mask_of(start_ref[rows, :], first, block, count)
            keys = kept_ref[:count, columns_of(group, GROUP)]
            values = kept_ref[:count, columns_of(group, GROUP + 1)]
            for head in range(GROUP):
                index = group * GROUP + head
                columns = slice(index * SLOT, (index + 1) * SLOT)
                query = kept_ref[rows, columns_of(group, head)]
                delta = jnp.sum(both[rows, columns], axis=-1, keepdims=True)
                logits = against(query, keys)
                weights = jnp.where(
                    mask, jnp.exp2(logits - logsum_ref[0, rows, index : index + 1]), 0.0
                )
                weight_grad = against(grad_low[rows, columns], values)
                logit_grad = (weights * (weight_grad - delta)).astype(BF16)
                query_grads[head][step] = product(logit_grad, keys)
                key_part = tokens_product(logit_grad, query)
                value_part = tokens_product(weights.astype(BF16), grad_low[rows, columns])
                for other in range(step + 1):
                    piece = slice(other * block, (other + 1) * block)
                    add(key_grads, other, key_part[piece])
                    add(value_grads, other, value_part[piece])
        for step in range(blocks):
            rows = slice(step * block, (step + 1) * block)
            cosine = table_ref[rows, :SLOT]
            sine = table_ref[rows, SLOT:]

            def unrotated(value):
                return (value * cosine - pltpu.roll(value, SLOT // 2, 1) * sine).astype(BF16)

            parts = [unrotated(query_grads[head][step] * SCALING) for head in range(GROUP)]
            parts.append(unrotated(key_grads[step] * (1.0 / LOG2E)))
            parts.append(value_grads[step].astype(BF16))
            out_ref[rows, group * JOINED : (group + 1) * JOINED] = product(
                jnp.concatenate(parts, axis=1), back_ref[...]
            ).astype(BF16)


def attention_forward(joined, table, start):
    length, width = joined.shape
    steps = width // (PAIR * JOINED)
    out_width = PAIR * GROUP * HEAD_DIM
    kept_width = PAIR * SLOTS * SLOT
    place = jnp.asarray(placement(SLOTS), BF16)
    back = jnp.asarray(placement(PAIR * GROUP).T, BF16)
    block = min(256, length)
    flops = steps * PAIR * GROUP * length * (length // 2 + block // 2) * SLOT * 4
    return pl.pallas_call(
        functools.partial(forward_kernel, block),
        grid=(steps,),
        in_specs=[
            pl.BlockSpec((length, PAIR * JOINED), lambda s: (0, s)),
            pl.BlockSpec((length, 2 * SLOT), lambda s: (0, 0)),
            pl.BlockSpec((length, 1), lambda s: (0, 0)),
            pl.BlockSpec(place.shape, lambda s: (0, 0)),
            pl.BlockSpec(back.shape, lambda s: (0, 0)),
        ],
        out_specs=[
            pl.BlockSpec((length, out_width), lambda s: (0, s)),
            pl.BlockSpec((length, kept_width), lambda s: (0, s)),
            pl.BlockSpec((1, length, SLOT), lambda s: (s, 0, 0)),
        ],
        out_shape=[
            jax.ShapeDtypeStruct((length, steps * out_width), BF16),
            jax.ShapeDtypeStruct((length, steps * kept_width), BF16),
            jax.ShapeDtypeStruct((steps, length, SLOT), F32),
        ],
        compiler_params=pltpu.CompilerParams(vmem_limit_bytes=VMEM_LIMIT),
        cost_estimate=SMALL_COST,
        name="attention_forward",
    )(joined, table, start, place, back)


def attention_backward(kept, table, start, logsum, att, grad, first, steps):
    length = att.shape[0]
    out_width = PAIR * GROUP * HEAD_DIM
    kept_width = PAIR * SLOTS * SLOT
    place = jnp.asarray(placement(PAIR * GROUP), BF16)
    back = jnp.asarray(placement(SLOTS).T, BF16)
    block = min(256, length)
    flops = steps * PAIR * GROUP * length * (length // 2 + block // 2) * SLOT * 10
    return pl.pallas_call(
        functools.partial(backward_kernel, block),
        grid=(steps,),
        in_specs=[
            pl.BlockSpec((length, kept_width), lambda s: (0, s + first)),
            pl.BlockSpec((length, 2 * SLOT), lambda s: (0, 0)),
            pl.BlockSpec((length, 1), lambda s: (0, 0)),
            pl.BlockSpec((1, length, SLOT), lambda s: (s + first, 0, 0)),
            pl.BlockSpec((length, out_width), lambda s: (0, s + first)),
            pl.BlockSpec((length, out_width), lambda s: (0, s)),
            pl.BlockSpec(place.shape, lambda s: (0, 0)),
            pl.BlockSpec(back.shape, lambda s: (0, 0)),
        ],
        out_specs=pl.BlockSpec((length, PAIR * JOINED), lambda s: (0, s)),
        out_shape=jax.ShapeDtypeStruct((length, steps * PAIR * JOINED), BF16),
        compiler_params=pltpu.CompilerParams(vmem_limit_bytes=VMEM_LIMIT),
        cost_estimate=SMALL_COST,
        name="attention_backward",
    )(kept, table, start, logsum, att, grad, place, back)


def fetched(parts, c_refs, c_ref, sems):
    step = pl.program_id(0)

    def copies(index):
        first = sum(parts[:index])
        column = 0
        for part, ref in enumerate(c_refs[first : first + parts[index]]):
            size = ref.shape[1]
            target = c_ref.at[index % 2, :, pl.ds(column, size)]
            yield pltpu.make_async_copy(ref, target, sems.at[index % 2, part])
            column += size

    for index in range(len(parts)):

        @pl.when(step == index)
        def _():
            if index == 0:
                for copy in copies(0):
                    copy.start()
            if index + 1 < len(parts):
                for copy in copies(index + 1):
                    copy.start()
            for copy in copies(index):
                copy.wait()

    return c_ref[step % 2]


def feed_kernel(parts, residual, fresh, places_ref, *refs):
    c_refs, refs = refs[: sum(parts)], refs[sum(parts) :]
    (dy_ref, expand_ref, down_ref), refs = refs[:3], refs[3:]
    if residual:
        hidden_ref, refs = refs[0], refs[1:]
    if not fresh:
        refs = refs[2:]
    out_ref, terms_ref, dc_ref, c_buffer, sems = refs
    hidden = down_ref.shape[0]
    c = fetched(parts, c_refs, c_buffer, sems)
    gate = product(c, expand_ref[:, :hidden])
    up = product(c, expand_ref[:, hidden:])
    dm = against(dy_ref[0], down_ref[...])
    sigmoid = jax.nn.sigmoid(gate)
    active = gate * sigmoid
    mixed = (active * up).astype(BF16)
    dgate = (dm * up * sigmoid * (1.0 + gate * (1.0 - sigmoid))).astype(BF16)
    dup = (dm * active).astype(BF16)
    terms_ref[0, 0] = mixed
    terms_ref[0, 1] = dgate
    terms_ref[0, 2] = dup
    dc = against(dgate, expand_ref[:, :hidden]) + against(dup, expand_ref[:, hidden:])
    dc_ref[0] = dc.astype(BF16)
    out = product(mixed, down_ref[...])
    if residual:
        out_ref[0] = (out + jnp.where(pl.program_id(0) == 0, hidden_ref[...], 0.0)).astype(BF16)
    else:
        out_ref[0] = out.astype(BF16)


def c_scratch(own, width):
    return [pltpu.VMEM((2, own, width), BF16), pltpu.SemaphoreType.DMA((2, 2))]


def feed_forward(places, c, dy, expand, down, blocks, before=None, hidden_res=None):
    parts = tuple(len(block) for block in c)
    steps = len(c)
    own, width = dy.shape[1] // (blocks // 4), dy.shape[2]
    hidden = down.shape[0]
    residual = hidden_res is not None
    fresh = before is None
    single = pl.Buffered(1)
    whole = lambda s, p: (0, 0)
    token = pl.BlockSpec((1, own, width), lambda s, p: (p[s, 1], p[s, 2], 0))
    flat = [part for block in c for part in block]
    operands = [places, *flat, dy, expand, down]
    in_specs = [pl.BlockSpec(memory_space=pl.ANY)] * len(flat) + [
        token,
        pl.BlockSpec(expand.shape, whole, pipeline_mode=single),
        pl.BlockSpec(down.shape, whole, pipeline_mode=single),
    ]
    if residual:
        operands.append(hidden_res)
        in_specs.append(pl.BlockSpec((own, width), whole, pipeline_mode=single))
    aliases = {}
    if not fresh:
        aliases = {len(operands): 0, len(operands) + 1: 1}
        operands += list(before)
        in_specs += [pl.BlockSpec(memory_space=pl.ANY)] * 2
    return pl.pallas_call(
        functools.partial(feed_kernel, parts, residual, fresh),
        grid_spec=pltpu.PrefetchScalarGridSpec(
            num_scalar_prefetch=1,
            grid=(steps,),
            in_specs=in_specs,
            out_specs=[
                token,
                pl.BlockSpec((1, 3, own, hidden), lambda s, p: (p[s, 0], 0, 0, 0)),
                pl.BlockSpec((1, own, width), lambda s, p: (s, 0, 0)),
            ],
            scratch_shapes=c_scratch(own, width),
        ),
        out_shape=[
            jax.ShapeDtypeStruct(dy.shape, BF16),
            jax.ShapeDtypeStruct((blocks, 3, own, hidden), BF16),
            jax.ShapeDtypeStruct((steps, own, width), BF16),
        ],
        input_output_aliases=aliases,
        compiler_params=pltpu.CompilerParams(vmem_limit_bytes=VMEM_LIMIT),
        cost_estimate=SMALL_COST,
        name="feed_forward",
    )(*operands)


def accumulate(total_ref, value, columns=slice(None)):
    @pl.when(pl.program_id(0) == 0)
    def _():
        total_ref[:, columns] = value

    @pl.when(pl.program_id(0) > 0)
    def _():
        total_ref[:, columns] += value


def down_grad_kernel(rows, places_ref, dy_ref, mixed_ref, out_ref, total_ref):
    accumulate(total_ref, tokens_product(mixed_ref[0, 0], dy_ref[0]))
    width, columns = total_ref.shape[1], out_ref.shape[2]

    @pl.when(pl.program_id(0) == pl.num_programs(0) - 1)
    def _():
        for place in range(out_ref.shape[0]):
            for to_row, count, to_column, row, column, size in pack_chunks(rows, width, columns):
                first = place * rows + row
                out_ref[place, to_row : to_row + count, to_column : to_column + size] = total_ref[
                    first : first + count, column : column + size
                ].astype(BF16)


def expand_grad_kernel(parts, places_ref, *refs):
    c_refs, refs = refs[: sum(parts)], refs[sum(parts) :]
    dgate_ref, dup_ref, _, out_ref, total_ref, c_buffer, sems = refs
    hidden = dgate_ref.shape[3]
    c = fetched(parts, c_refs, c_buffer, sems)
    accumulate(total_ref, tokens_product(c, dgate_ref[0, 0]), slice(0, hidden))
    accumulate(total_ref, tokens_product(c, dup_ref[0, 0]), slice(hidden, None))

    @pl.when(pl.program_id(0) == pl.num_programs(0) - 1)
    def _():
        out_ref[...] = total_ref[...].astype(BF16).reshape(out_ref.shape)


def down_grads(places, dy, terms, n_dp, rows_before):
    blocks, _, own, hidden = terms.shape
    width = dy.shape[2]
    packed = hidden * width // (2 * hidden) // n_dp
    return pl.pallas_call(
        functools.partial(down_grad_kernel, hidden // n_dp),
        grid_spec=pltpu.PrefetchScalarGridSpec(
            num_scalar_prefetch=1,
            grid=(blocks,),
            in_specs=[
                pl.BlockSpec((1, own, width), lambda s, p: (p[s, 1], p[s, 2], 0)),
                pl.BlockSpec((1, 1, own, hidden), lambda s, p: (p[s, 0], 0, 0, 0)),
            ],
            out_specs=pl.BlockSpec(
                (n_dp, packed, 2 * hidden),
                lambda s, p: (0, rows_before // packed, 0),
                pipeline_mode=pl.Buffered(1),
            ),
            scratch_shapes=[pltpu.VMEM((hidden, width), F32)],
        ),
        out_shape=jax.ShapeDtypeStruct((n_dp, rows_before + packed, 2 * hidden), BF16),
        compiler_params=pltpu.CompilerParams(vmem_limit_bytes=VMEM_LIMIT),
        cost_estimate=SMALL_COST,
        name="down_grads",
    )(places, dy, terms)


def expand_grads(places, c, terms, packed, rows):
    parts = tuple(len(block) for block in c)
    blocks, _, own, hidden = terms.shape
    n_dp = packed.shape[0]
    width = n_dp * rows
    flat = [part for block in c for part in block]
    return pl.pallas_call(
        functools.partial(expand_grad_kernel, parts),
        grid_spec=pltpu.PrefetchScalarGridSpec(
            num_scalar_prefetch=1,
            grid=(blocks,),
            in_specs=[pl.BlockSpec(memory_space=pl.ANY)] * len(flat)
            + [
                pl.BlockSpec((1, 1, own, hidden), lambda s, p: (p[s, 0], 1, 0, 0)),
                pl.BlockSpec((1, 1, own, hidden), lambda s, p: (p[s, 0], 2, 0, 0)),
                pl.BlockSpec(memory_space=pl.ANY),
            ],
            out_specs=pl.BlockSpec(
                (n_dp, rows, 2 * hidden), lambda s, p: (0, 0, 0), pipeline_mode=pl.Buffered(1)
            ),
            scratch_shapes=[pltpu.VMEM((width, 2 * hidden), F32)] + c_scratch(own, width),
        ),
        out_shape=jax.ShapeDtypeStruct(packed.shape, BF16),
        input_output_aliases={1 + len(flat) + 2: 0},
        compiler_params=pltpu.CompilerParams(vmem_limit_bytes=VMEM_LIMIT),
        cost_estimate=SMALL_COST,
        name="expand_grads",
    )(places, *flat, terms, terms, packed)


def local(
    inputs,
    doc_ids,
    cotangent,
    attend_in,
    attend_out,
    gains,
    expand,
    contract,
    attend_in_first,
    attend_in_second,
    attend_out_first,
    attend_out_second,
    gains_first,
    gains_second,
    expand_first,
    expand_second,
    contract_first,
    contract_second,
):
    batches, rows_local, width = inputs.shape
    n_tp = lax.axis_size("tp")
    n_dp = lax.axis_size("dp")
    me = lax.axis_index("tp")
    stream_place = lax.axis_index(("hi", "lo")).astype(jnp.int32)
    stream = rows_local * batches * n_tp
    own = stream // n_tp
    qwidth = HEADS * HEAD_DIM
    kwidth = KV_HEADS * HEAD_DIM
    joined_width = qwidth + 2 * kwidth
    part_in = joined_width // n_tp
    part_out = width // n_tp
    row_in = attend_in.shape[0]
    row_down = contract.shape[0]

    def to_groups(value):
        rows = value.shape[0]
        return jnp.concatenate(
            [
                value[:, :qwidth].reshape(rows, KV_HEADS, -1),
                value[:, qwidth : qwidth + kwidth].reshape(rows, KV_HEADS, -1),
                value[:, qwidth + kwidth :].reshape(rows, KV_HEADS, -1),
            ],
            axis=2,
        ).reshape(rows, joined_width)

    def from_groups(value):
        rows = value.shape[0]
        grid = value.reshape(rows, KV_HEADS, JOINED)
        first, second = GROUP * HEAD_DIM, (GROUP + 1) * HEAD_DIM
        return jnp.concatenate(
            [
                grid[:, :, :first].reshape(rows, qwidth),
                grid[:, :, first:second].reshape(rows, kwidth),
                grid[:, :, second:].reshape(rows, kwidth),
            ],
            axis=1,
        )

    gain_columns = jnp.concatenate([gains.T, jnp.zeros((row_in, SLOT - 2), F32)], axis=1)
    attend_shard = jnp.concatenate([to_groups(attend_in), gain_columns, attend_out], axis=1)
    attend_all = lax.all_gather(
        attend_shard.astype(BF16), ("dp", "hi", "lo", "tp"), axis=0, tiled=True
    )

    n_ctx = 4 * n_tp
    expand_parts = expand.astype(BF16).reshape(row_in, 2, n_dp, n_ctx, row_down)
    expand_parts = expand_parts.transpose(3, 0, 1, 2, 4).reshape(n_ctx, row_in, -1)
    expand_shard = ctx_swap(expand_parts).reshape(n_ctx * row_in, -1)
    hidden_two = expand_shard.shape[1]
    rows_expand = n_ctx * row_in
    feed_shard = jnp.concatenate(
        [expand_shard, packed_rows(contract.astype(BF16), hidden_two)], axis=0
    )
    feed_all, feed_pieces = dp_gather(after(feed_shard, attend_all))
    expand_all = feed_all[:, :rows_expand].reshape(width, hidden_two)
    down_all = unpacked_rows(feed_all[:, rows_expand:], row_down, width).reshape(-1, width)

    ids_wide = jnp.broadcast_to(doc_ids[:, :, None].astype(BF16), (batches, rows_local, SLOT))
    moved = to_streams(jnp.concatenate([inputs, ids_wide], axis=2)).reshape(own, width + SLOT)
    resid = moved[:, :width]
    moved_all = group_gather(moved)
    resid_all = moved_all[:, :width].astype(F32)
    ids = moved_all[:, width].astype(jnp.int32)
    dy_all = lax.all_gather(after(cotangent, moved), CTX, axis=1, tiled=True)

    start = jnp.sum((ids[None, :] < ids[:, None]).astype(jnp.int32), axis=-1)
    position = (jnp.arange(stream, dtype=jnp.int32) - start).astype(F32)
    inverse = jnp.power(ROPE_BASE, -2.0 * jnp.arange(HALF, dtype=F32) / HEAD_DIM)
    angles = position[:, None] * inverse
    cosine = jnp.cos(angles)
    sine = jnp.sin(angles)
    gap = jnp.zeros((stream, SLOT // 2 - HALF), F32)
    table = jnp.concatenate([cosine, gap, cosine, gap, -sine, gap, sine, gap], axis=-1)
    start = start[:, None]

    in_low = lax.dynamic_slice(attend_all, (0, me * part_in), (width, part_in))
    gain_one = attend_all[:, joined_width].astype(F32)
    gain_two = attend_all[:, joined_width + 1].astype(F32)
    out_low = lax.dynamic_slice(
        attend_all, (me * (qwidth // n_tp), joined_width + SLOT), (qwidth // n_tp, width)
    )

    inv_all = lax.rsqrt(jnp.mean(resid_all * resid_all, axis=-1, keepdims=True) + EPSILON)
    first_in = (resid_all * inv_all * gain_one).astype(BF16)
    joined = product(first_in, in_low).astype(BF16)
    att_low, kept, logsum = attention_forward(joined, table, start)
    att_low = after(att_low, feed_pieces[0])

    def own_sum(value):
        grid = value.reshape(n_tp, own, width)
        if n_tp != 2:
            return lax.psum_scatter(grid, "tp", scatter_dimension=0, tiled=True)[0].astype(F32)
        came = exchange(lax.dynamic_index_in_dim(grid, 1 - me, 0, keepdims=False), "tp")
        mine = lax.dynamic_index_in_dim(grid, me, 0, keepdims=False)
        return mine.astype(F32) + came.astype(F32)

    resid = resid.astype(F32)
    hidden_res = resid + own_sum(product(att_low, out_low).astype(BF16))
    inv_two = lax.rsqrt(jnp.mean(hidden_res * hidden_res, axis=-1, keepdims=True) + EPSILON)
    normed_two = hidden_res * inv_two
    second_in = (normed_two * gain_two).astype(BF16)
    def place_row(relative, member):
        return jnp.stack(
            [jnp.int32(relative * n_tp + member), stream_place ^ relative, me ^ member]
        ).astype(jnp.int32)

    blocks = 4 * n_tp
    parts = [
        [relative_gather(part) for part in chip] for chip in plane_parts(second_in)
    ]

    def pieces_of(relative, member):
        return [part[member] for part in parts[relative]]

    def feed_call(order, before=None, residual=None):
        rows = jnp.stack([place_row(relative, member) for relative, member in order])
        c = [pieces_of(relative, member) for relative, member in order]
        return feed_forward(rows, c, dy_all, expand_all, down_all, blocks, before, residual)

    near_order = [(0, member) for member in range(n_tp)]
    first_order = [(r, member) for member in range(1, n_tp) for r in (1, 2, 3)]
    second_order = [(r, 0) for r in (1, 2, 3)]
    out_all, terms, first_dc = feed_call(first_order)
    first_dc = first_dc.reshape(n_tp - 1, 3, own, width)
    first_sent = [first_dc[member] for member in range(n_tp - 1)]
    out_all, terms, second_dc = feed_call(second_order, (out_all, terms))
    far_sum = relative_sum([second_dc] + first_sent).astype(BF16)
    middle = width // 2
    left_sent, right_sent = far_sum[0::2, :, :middle], far_sum[1:, :, middle:]
    out_all, terms, near_dc = feed_call(
        near_order, lax.optimization_barrier((out_all, terms, left_sent, right_sent))[:2], hidden_res
    )
    every_order = near_order + first_order + second_order
    every_rows = jnp.stack([place_row(relative, member) for relative, member in every_order])
    packed = down_grads(every_rows, dy_all, terms, n_dp, rows_expand)
    near = relative_sum([near_dc[member] for member in range(n_tp)])
    left_came = after(exchange(left_sent, "lo"), packed)
    right_came = after(exchange(right_sent, "hi"), packed)
    left = total_of([far_sum[1, :, :middle], left_came[1]]).astype(BF16)
    right = total_of([far_sum[0, :, middle:], right_came[1]]).astype(BF16)
    feed_terms = expand_grads(
        every_rows,
        [pieces_of(relative, member) for relative, member in every_order],
        terms,
        after(packed, left, right),
        rows_expand,
    )
    left = after(exchange(left, "hi"), feed_terms)
    right = after(exchange(right, "lo"), feed_terms)
    second_grad = near.astype(F32) + jnp.concatenate(
        [total_of([left_came[0], left]), total_of([right_came[0], right])], axis=1
    )
    out_all, second_grad = lax.optimization_barrier((out_all, second_grad))
    block_out = lax.psum_scatter(out_all, CTX, scatter_dimension=1, tiled=True)

    upstream = lax.dynamic_slice(dy_all, (stream_place, me * own, 0), (1, own, width))[0]
    upstream = upstream.astype(F32)
    hidden_grad = upstream + norm_back(second_grad, normed_two, inv_two, gain_two)
    branch_all = group_gather(hidden_grad.astype(BF16))
    att_steps = logsum.shape[0]
    cuts = [0, att_steps // 2, att_steps] if att_steps > 1 else [0, 1]
    heads_width = PAIR * GROUP * HEAD_DIM
    def plane_stage(terms, name):
        return axis_sum(terms, name, 1 if name == "hi" else 2)

    def plane_grid(value):
        return [value.reshape(n_dp, 2, 2, n_tp * row_in, -1)]

    def plane_terms(value, order):
        return plane_stage(plane_stage(plane_grid(value), order[0]), order[1])

    orders = (("hi", "lo"), ("lo", "hi"))

    def heads_grad(index):
        part = out_low[cuts[index] * heads_width : cuts[index + 1] * heads_width]
        return against(branch_all, part).astype(BF16)

    def heads_back(index, grad):
        begin, end = cuts[index], cuts[index + 1]
        return attention_backward(kept, table, start, logsum, att_low, grad, begin, end - begin)

    dp_place = lax.axis_index("dp")

    def feed_piece(step):
        return lax.dynamic_index_in_dim(feed_terms, (dp_place + step) % n_dp, 0, keepdims=False)

    feed_came = [shifted(feed_piece(step), step) for step in range(1, n_dp)]

    joined_parts = [heads_back(0, heads_grad(0))]
    in_parts = [tokens_product(first_in, joined_parts[0]).astype(BF16)]

    branch_late = after(branch_all, joined_parts[0])
    if n_tp == 2:
        heads_rows = qwidth // n_tp

        def out_columns(member):
            part = lax.dynamic_slice_in_dim(branch_late, member * part_out, part_out, 1)
            return tokens_product(att_low, part).astype(BF16)

        out_came = exchange(out_columns(1 - me), "tp")
        out_term = jnp.zeros((qwidth, part_out), BF16)
        out_term = lax.dynamic_update_slice_in_dim(out_term, out_columns(me), me * heads_rows, 0)
        out_term = lax.dynamic_update_slice_in_dim(out_term, out_came, (1 - me) * heads_rows, 0)
    else:
        out_term = tokens_product(att_low, branch_late).astype(BF16)
        out_term = out_term.reshape(qwidth // n_tp, n_tp, part_out).transpose(1, 0, 2)
        out_term = group_swap(out_term).reshape(qwidth, part_out)
    half = part_out // 2
    out_parts = [out_term[:, :half], out_term[:, half:]]

    if len(cuts) > 2:
        grad = after(heads_grad(1), in_parts[0], out_term)
        joined_parts.append(heads_back(1, grad))
    in_terms = [plane_stage(plane_grid(in_parts[0]), orders[0][0])]
    in_terms[0][-1] = after(in_terms[0][-1], feed_came[0])
    if len(cuts) > 2:
        in_parts.append(tokens_product(first_in, joined_parts[1]).astype(BF16))
        in_terms.append(plane_stage(plane_grid(in_parts[1]), orders[1][0]))
        in_terms[-1][-1] = after(in_terms[-1][-1], feed_came[1])
    out_terms = [
        plane_stage(plane_grid(after(part, in_parts[-1])), order[0])
        for part, order in zip(out_parts, orders)
    ]
    in_terms = [plane_stage(terms, order[1]) for terms, order in zip(in_terms, orders)]
    out_terms = [plane_stage(terms, order[1]) for terms, order in zip(out_terms, orders)]
    joined_all = after(jnp.concatenate(joined_parts, axis=1), in_parts[-1])
    first_part = against(joined_all, in_low).astype(BF16)

    ready = (first_part,) + tuple(terms[-1] for terms in in_terms)
    low = F32 if n_tp != 2 else BF16

    def owned(terms):
        rows = column_sum(terms).reshape(n_tp, row_in, -1)
        return group_swap(rows.astype(low)).astype(F32).transpose(1, 0, 2).reshape(row_in, -1)

    in_sum = owned(in_terms)
    out_terms[-1][-1] = after(out_terms[-1][-1], in_sum)
    out_sum = owned(out_terms)
    feed_sum = total_of([feed_piece(0)] + [after(came, in_sum) for came in feed_came])
    expand_rows = feed_sum[:rows_expand].astype(BF16).reshape(n_ctx, row_in, -1)
    expand_sum = ctx_swap(after(expand_rows, in_sum)).reshape(n_ctx, row_in, 2, n_dp, row_down)
    expand_sum = expand_sum.transpose(1, 2, 3, 0, 4).reshape(row_in, 2 * FF).astype(F32)
    contract_sum = unpacked_rows(feed_sum[rows_expand:], row_down, width)

    inv_one = lax.rsqrt(jnp.mean(resid * resid, axis=-1, keepdims=True) + EPSILON)
    first_grad = own_sum(first_part)
    first_grad = after(first_grad, *ready[1:])
    resid_grad = hidden_grad + norm_back(first_grad, resid * inv_one, inv_one, gain_one)
    shape = (batches, rows_local, width)
    grad_inputs = from_streams(resid_grad.astype(BF16).reshape(shape))

    in_sum = from_groups(in_sum)
    low_gains = gains.astype(BF16).astype(F32)
    gain_sum = jnp.stack(
        [
            jnp.sum(in_sum * attend_in.astype(BF16).astype(F32), axis=1),
            jnp.sum(expand_sum * expand.astype(BF16).astype(F32), axis=1),
        ]
    ) / low_gains

    out_fan = max(1, HEADS * HEAD_DIM // (stream // 8))
    new_in = adamw(attend_in, attend_in_first, attend_in_second, in_sum, RATE / math.sqrt(D))
    new_out = adamw(
        attend_out, attend_out_first, attend_out_second, out_sum, RATE / math.sqrt(out_fan)
    )
    new_gain = adamw(gains, gains_first, gains_second, gain_sum, GAIN_RATE)
    new_expand = adamw(expand, expand_first, expand_second, expand_sum, RATE / math.sqrt(D))
    new_contract = adamw(
        contract, contract_first, contract_second, contract_sum, RATE / math.sqrt(FF)
    )
    return (block_out, grad_inputs, *new_in, *new_out, *new_gain, *new_expand, *new_contract)


def solution(mesh):
    n_dp, n_ctx = mesh.shape["dp"], mesh.shape["ctx"]
    cut = jax.sharding.Mesh(
        mesh.devices.reshape(n_dp, 2, 2, n_ctx // 4), ("dp", "hi", "lo", "tp")
    )
    every = ("dp", "hi", "lo", "tp")
    rows = P(every, None)
    columns = P(None, every)
    tokens = P(None, every, None)
    return jax.shard_map(
        local,
        mesh=cut,
        in_specs=(tokens, columns, tokens, rows, rows, columns, rows, rows)
        + (rows,) * 4
        + (columns,) * 2
        + (rows,) * 4,
        out_specs=(tokens, tokens) + (rows,) * 6 + (columns,) * 3 + (rows,) * 6,
        check_vma=False,
    )
```

time: 2010 us -> 695 us (0.35)
  waiting for transfers between devices: 1390 us -> 213 us
  matrix products: 337 us -> 43.1 us
  Pallas kernels: 0 us -> 156 us
  starting transfers between devices: 0.5 us -> 86.2 us
  blocking collectives: 51.1 us -> 0 us
  local copies, waits for them, and re-layouts: 118 us -> 83.5 us
    reduce_scatter x5 -> x1, waiting for transfers between devices: 964 us -> 0.01 us  [local(): block_out = lax.psum_scatter(out_all, CTX, scatter_dimension=1, tiled=True)]
    all_gather x6 -> x2, waiting for transfers between devices: 331 us -> 50.3 us  [the longest x1 50.2 us: local(): lax.all_gather(attend_shard.astype(BF16), ('dp', 'hi', 'lo', 'tp'), axis=...]
    dot_general x18 -> x2, matrix products: 218 us -> 14 us  [product(): return jnp.dot(left, right, preferred_element_type=F32)]
    pallas_call x0 -> x8, Pallas kernels: none -> 156 us  [the longest x3 62.9 us: feed_forward(): pl.pallas_call(functools.partial(feed_kernel, parts, residual, fresh), gr...]
    ppermute x0 -> x44, waiting for transfers between devices: none -> 141 us  [the longest x30 108 us: exchange(): return lax.ppermute(value, axis, [(i, i ^ bit) for i in range(count)])]
    unnamed x13 -> x3, waiting for transfers between devices: 95 us -> 0.05 us
    ppermute x0 -> x44, starting transfers between devices: none -> 61.6 us  [the longest x6 22.5 us: shifted(): lax.ppermute(value, 'dp', [(i, (i + step) % count) for i in range(count)])]
    all_gather x2 -> x0, blocking collectives: 51.1 us -> none  [the longest x1 43 us: local(): lax.all_gather(gains.astype(jnp.bfloat16), ('dp', 'ctx'), axis=1, tiled=T...]
  transfers between devices with their start and end apart: 12 -> 51, of which waited for: 11 -> 18; matrix products, arithmetic and copies ran while one was open for 16% -> 27% of each run, Pallas kernels for 0% -> 19%
where the time goes in v1:
time: 695 us; the launch traced here: 687 us
  waiting for transfers between devices  213 us (31%)
  Pallas kernels  156 us (22%)
  other arithmetic  89.7 us (13%)
  starting transfers between devices  86.2 us (12%)
  local copies, waits for them, and re-layouts  83.5 us (12%)
  matrix products  43.1 us (6%)
  between operations  15.5 us (2%)
    ppermute x30, waiting for transfers between devices, exchange(): return lax.ppermute(value, axis, [(i, i ^ bit) for i in range(count)])  108 us
    pallas_call x3, Pallas kernels, feed_forward(): pl.pallas_call(functools.partial(feed_kernel, parts, residual, fresh), gr...  62.9 us
    all_gather x1, waiting for transfers between devices, local(): lax.all_gather(attend_shard.astype(BF16), ('dp', 'hi', 'lo', 'tp'), axis=...  50.2 us
    pallas_call x2, Pallas kernels, attention_backward(): pl.pallas_call(functools.partial(backward_kernel, block), grid=(steps,),...  32 us
    pallas_call x1, Pallas kernels, expand_grads(): pl.pallas_call(functools.partial(expand_grad_kernel, parts), grid_spec=pl...  26.4 us
    ppermute x6, starting transfers between devices, shifted(): lax.ppermute(value, 'dp', [(i, (i + step) % count) for i in range(count)])  22.5 us
    ppermute x30, starting transfers between devices, exchange(): return lax.ppermute(value, axis, [(i, i ^ bit) for i in range(count)])  21.1 us
    unnamed x120, local copies, waits for them, and re-layouts  20.5 us
  transfers between devices with their start and end apart: 51, of which 18 were waited for; matrix products, arithmetic and copies ran while one was open for 27% of the time, Pallas kernels for 19%

profile of v1, /device:TPU:0, one launch (start us, length us, event | category | flops | bytes accessed | tf_op | source)
XLA Modules:
  0.0 686.9 jit_solution(4168087085293307273)
XLA Ops:
  12.2 7.6 %collective-permute-start.1 = (bf16[1,128,1664]{2,1,0:T(8,128)(2,1)S(1)}, bf16[1,128,1664]{2,1,0:T(8,128)(2,1)S(1)}, u32[]{:S(2)}, u32[]{:S(2)}) collective-permute-start(bf16[1,128,1664]{2,1,0:T(8,128)(2,1)S(1)} %get-tuple-element.127), channel_id=1, source_target_pairs={{0,2},{1,4},{2,6},{3,0},{4,3},{5,5},{6,7},{7,1},{8,10},{9,12},{10,... | collective-permute-start | bytes 1277960 | tf_op jit(solution)/shard_map/ppermute | solution.py:225
  23.3 10.0 %collective-permute-done.1 = bf16[1,128,1664]{2,1,0:T(8,128)(2,1)S(1)} collective-permute-done((bf16[1,128,1664]{2,1,0:T(8,128)(2,1)S(1)}, bf16[1,128,1664]{2,1,0:T(8,128)(2,1)S(1)}, u32[]{:S(2)}, u32[]{:S(2)}) %collective-permute-start.1) | collective-permute-done | bytes 426016 | tf_op jit(solution)/shard_map/ppermute | solution.py:225
  33.3 6.2 collective-permute-done.2
  50.1 17.3 %all-to-all-done = bf16[8,48,1024]{2,1,0:T(8,128)(2,1)S(1)} async-done(((bf16[8,48,1024]{2,1,0:T(8,128)(2,1)}), bf16[8,48,1024]{2,1,0:T(8,128)(2,1)S(1)}, u32[]{:S(2)}, u32[]{:S(2)}) %all-to-all-start) | async-done | bytes 786464 | tf_op jit(solution)/shard_map/all_to_all | solution.py:207
  83.8 50.2 %all-gather.3.cloned.1.call-done = bf16[1536,4736]{1,0:T(8,128)(2,1)} async-done(((bf16[48,4736]{1,0:T(8,128)(2,1)}), bf16[1536,4736]{1,0:T(8,128)(2,1)}) %all-gather.3.cloned.1.call-update) | async-done | bytes 14549008 | tf_op jit(solution)/shard_map/all_gather | solution.py:695
  141.8 9.3 %fusion.7.joined_ref = bf16[1024,1536]{1,0:T(8,128)(2,1)} fusion(bf16[1024,1536]{1,0:T(8,128)(2,1)S(1)} %fusion.2, bf16[1536,4736]{1,0:T(8,128)(2,1)} %all-gather.3.cloned.1.call-done, s32[]{:T(128)S(6)} %select_n.292), kind=kOutput, calls=%fused_computation.14 | convolution fusion | flops 4833411072 | bytes 11010052 | tf_op jit(solution)/shard_map/dot_general | solution.py:47
  151.1 19.8 %attention_forward.1 = (bf16[1024,768]{1,0:T(8,128)(2,1)}, bf16[1024,2048]{1,0:T(8,128)(2,1)}, f32[2,1024,128]{2,1,0:T(8,128)}) custom-call(bf16[1024,1536]{1,0:T(8,128)(2,1)} %fusion.7.joined_ref, f32[1024,256]{1,0:T(8,128)} %concatenate.48.table_ref, s32[1024,1]{1,0:T(8,128)} %copy.109.start_ref, bf16[384,512]{1,0:T(8,128)(2,1)} %constant.561.clone.place_ref, ...), custom_call_target="tpu_custom_call" | custom-call | flops 1048576 | bytes 1048576 | tf_op jit(solution)/shard_map/attention_forward/pallas_call | solution.py:373
  193.4 44.4 %collective-permute-done.10.refs_0_.refs_6_ = bf16[512,1536]{1,0:T(8,128)(2,1)} collective-permute-done((bf16[512,1536]{1,0:T(8,128)(2,1)S(1)}, bf16[512,1536]{1,0:T(8,128)(2,1)}, u32[]{:S(2)}, u32[]{:S(2)}) %collective-permute-start.10) | collective-permute-done | bytes 1572896 | tf_op jit(solution)/shard_map/ppermute | solution.py:68
  246.6 11.9 %collective-permute-done.12.refs_2_.refs_8_ = bf16[512,768]{1,0:T(8,128)(2,1)} collective-permute-done((bf16[512,768]{1,0:T(8,128)(2,1)S(1)}, bf16[512,768]{1,0:T(8,128)(2,1)}, u32[]{:S(2)}, u32[]{:S(2)}) %collective-permute-start.12) | collective-permute-done | bytes 786464 | tf_op jit(solution)/shard_map/ppermute | solution.py:68
  265.9 22.4 %feed_forward.3 = (bf16[4,1024,1536]{2,1,0:T(8,128)(2,1)}, bf16[8,3,512,512]{3,2,1,0:T(8,128)(2,1)}, bf16[3,512,1536]{2,1,0:T(8,128)(2,1)}) custom-call(s32[3,3]{1,0:T(4,128)} %pad_add_fusion.1.places_ref, bf16[512,1536]{1,0:T(8,128)(2,1)} %collective-permute-done.14.refs_0_.refs_2_, bf16[512,1536]{1,0:T(8,128)(2,1)} %collective-permute-done.15.refs_1_.refs_3_, ...), custom_call_target="tpu_custom_call" | custom-call | flops 1048576 | bytes 1048576 | tf_op jit(solution)/shard_map/feed_forward/pallas_call | solution.py:515
  289.6 22.4 %feed_forward.4 = (bf16[4,1024,1536]{2,1,0:T(8,128)(2,1)}, bf16[8,3,512,512]{3,2,1,0:T(8,128)(2,1)}, bf16[3,512,1536]{2,1,0:T(8,128)(2,1)}) custom-call(s32[3,3]{1,0:T(4,128)} %pad_add_fusion.places_ref, bf16[512,1536]{1,0:T(8,128)(2,1)} %collective-permute-done.10.refs_0_.refs_6_, ...), custom_call_target="tpu_custom_call", output_to_operand_aliasing={{0}: (8, {}), {1}: (9, {})} | custom-call | flops 1048576 | bytes 1048576 | tf_op jit(solution)/shard_map/feed_forward/pallas_call | solution.py:515
  323.6 18.1 %feed_forward.5 = (bf16[4,1024,1536]{2,1,0:T(8,128)(2,1)}, bf16[8,3,512,512]{3,2,1,0:T(8,128)(2,1)}, bf16[2,512,1536]{2,1,0:T(8,128)(2,1)}) custom-call(s32[2,3]{1,0:T(2,128)} %pad_add_fusion.2.places_ref, bf16[512,1536]{1,0:T(8,128)(2,1)} %copy-done.8, bf16[512,1536]{1,0:T(8,128)(2,1)} %copy-done.9, ...), custom_call_target="tpu_custom_call", output_to_operand_aliasing={{0}: (7, {}), {1}: (8, {})} | custom-call | flops 1048576 | bytes 1048576 | tf_op jit(solution)/shard_map/feed_forward/pallas_call | solution.py:515
  343.3 14.8 %down_grads.1.refs_12_ = bf16[4,576,1024]{2,1,0:T(8,128)(2,1)} custom-call(s32[8,3]{1,0:T(8,128)} %stack.154.places_ref, bf16[4,1024,1536]{2,1,0:T(8,128)(2,1)} %all-gather.5.cloned.1.call-done.refs_4_.refs_2_.dy_ref, bf16[8,3,512,512]{3,2,1,0:T(8,128)(2,1)} %get-tuple-element.68.mixed_ref.refs_10_.refs_11_), custom_call_target="tpu_custom_call" | custom-call | flops 1048576 | bytes 1048576 | tf_op jit(solution)/shard_map/down_grads/pallas_call | solution.py:581
  363.6 26.4 %expand_grads.1 = bf16[4,576,1024]{2,1,0:T(8,128)(2,1)} custom-call(s32[8,3]{1,0:T(8,128)} %stack.154.places_ref, bf16[512,1536]{1,0:T(8,128)(2,1)} %copy-done.8, bf16[512,1536]{1,0:T(8,128)(2,1)} %copy-done.9, bf16[512,1536]{1,0:T(8,128)(2,1)} %collective-permute-done.14.refs_0_.refs_2_, ...), custom_call_target="tpu_custom_call", output_to_operand_aliasing={{}: (13, {})} | custom-call | flops 1048576 | bytes 1048576 | tf_op jit(solution)/shard_map/expand_grads/pallas_call | solution.py:610
  408.0 10.6 %collective-permute-start.28 = (bf16[576,1024]{1,0:T(8,128)(2,1)}, bf16[576,1024]{1,0:T(8,128)(2,1)}, u32[]{:S(2)}, u32[]{:S(2)}) collective-permute-start(bf16[576,1024]{1,0:T(8,128)(2,1)} %get-tuple-element.112), channel_id=1, source_target_pairs={{0,8},{8,16},{16,24},{24,0},{1,9},{9,17},{17,25},{25,1},{2,10},{10... | collective-permute-start | bytes 3538952 | tf_op jit(solution)/shard_map/ppermute | solution.py:73
  430.2 16.1 %attention_backward.2 = bf16[1024,768]{1,0:T(8,128)(2,1)} custom-call(bf16[1024,2048]{1,0:T(8,128)(2,1)} %get-tuple-element.76.kept_ref, f32[1024,256]{1,0:T(8,128)} %concatenate.48.table_ref, s32[1024,1]{1,0:T(8,128)} %copy.109.start_ref, f32[2,1024,128]{2,1,0:T(8,128)} %get-tuple-element.77.logsum_ref, bf16[1024,768]{1,0:T(8,128)(2,1)} %get-tuple-element.56.att_ref, ...), custom_call_target="tpu_custom_call" | custom-call | flops 1048576 | bytes 1048576 | tf_op jit(solution)/shard_map/attention_backward/pallas_call | solution.py:407
  466.1 15.9 %attention_backward.3 = bf16[1024,768]{1,0:T(8,128)(2,1)} custom-call(bf16[1024,2048]{1,0:T(8,128)(2,1)} %get-tuple-element.76.kept_ref, f32[1024,256]{1,0:T(8,128)} %concatenate.48.table_ref, s32[1024,1]{1,0:T(8,128)} %copy.109.start_ref, f32[2,1024,128]{2,1,0:T(8,128)} %get-tuple-element.77.logsum_ref, bf16[1024,768]{1,0:T(8,128)(2,1)} %get-tuple-element.56.att_ref, ...), custom_call_target="tpu_custom_call" | custom-call | flops 1048576 | bytes 1048576 | tf_op jit(solution)/shard_map/attention_backward/pallas_call | solution.py:407
  490.6 7.8 %fusion.10 = bf16[1024,1536]{1,0:T(8,128)(2,1)S(1)} fusion(bf16[1024,1536]{1,0:T(8,128)(2,1)S(1)} %pad_maximum_fusion.1, bf16[1536,4736]{1,0:T(8,128)(2,1)} %all-gather.3.cloned.1.call-done, s32[]{:T(128)S(6)} %select_n.292), kind=kOutput, calls=%fused_computation.15 | convolution fusion | flops 4833411072 | bytes 11010052 | tf_op jit(solution)/shard_map/dot_general | solution.py:39
  511.3 19.5 %collective-permute-done.38 = bf16[4,1,2,96,384]{4,3,2,1,0:T(8,128)(2,1)} collective-permute-done((bf16[4,1,2,96,384]{4,3,2,1,0:T(8,128)(2,1)}, bf16[4,1,2,96,384]{4,3,2,1,0:T(8,128)(2,1)}, u32[]{:S(2)}, u32[]{:S(2)}) %collective-permute-start.38) | collective-permute-done | bytes 589856 | tf_op jit(solution)/shard_map/ppermute | solution.py:68
  533.8 13.8 %collective-permute-done.29 = bf16[4,1,1,96,768]{4,3,2,1,0:T(8,128)(2,1)} collective-permute-done((bf16[4,1,1,96,768]{4,3,2,1,0:T(8,128)(2,1)}, bf16[4,1,1,96,768]{4,3,2,1,0:T(8,128)(2,1)}, u32[]{:S(2)}, u32[]{:S(2)}) %collective-permute-start.29) | collective-permute-done | bytes 589856 | tf_op jit(solution)/shard_map/ppermute | solution.py:68
  556.3 8.7 %collective-permute-done.32 = bf16[4,1,1,96,768]{4,3,0,2,1:T(8,128)(2,1)S(1)} collective-permute-done((bf16[4,1,1,96,768]{4,3,0,2,1:T(8,128)(2,1)S(1)}, bf16[4,1,1,96,768]{4,3,0,2,1:T(8,128)(2,1)S(1)}, u32[]{:S(2)}, u32[]{:S(2)}) %collective-permute-start.32) | collective-permute-done | bytes 589856 | tf_op jit(solution)/shard_map/ppermute | solution.py:68
  602.5 11.0 %collective-permute-done.35 = bf16[1,128,1536]{2,1,0:T(8,128)(2,1)S(1)} collective-permute-done((bf16[1,128,1536]{2,1,0:T(8,128)(2,1)}, bf16[1,128,1536]{2,1,0:T(8,128)(2,1)S(1)}, u32[]{:S(2)}, u32[]{:S(2)}) %collective-permute-start.35) | collective-permute-done | bytes 393248 | tf_op jit(solution)/shard_map/ppermute | solution.py:237
  648.8 12.3 %all-to-all-start.2 = ((bf16[4,96,768]{2,1,0:T(8,128)(2,1)}), bf16[4,96,768]{2,1,0:T(8,128)(2,1)S(1)}, u32[]{:S(2)}, u32[]{:S(2)}) async-start(bf16[4,96,768]{2,1,0:T(8,128)(2,1)} %pad_maximum_fusion.4), calls=%async_computation.3 | async-start | bytes 1179648 | tf_op jit(solution)/shard_map/all_to_all | solution.py:95
  667.7 5.8 multiply_subtract_fusion
  (358 shorter events, 268.9 us)
Async XLA Ops:
  7.2 126.9 %all-gather.3.cloned.1.call-start = ((), (), s32[]{:S(2)}) async-start(), calls=%async_computation.5 | async-start | bytes 15003648 | tf_op jit(solution)/shard_map/all_gather | solution.py:695
  10.2 254.6 %all-gather.5.cloned.1.call-start = ((), (), s32[]{:S(2)}) async-start(), calls=%async_computation.6 | async-start | bytes 14155776 | tf_op jit(solution)/shard_map/all_gather | solution.py:718
  47.4 632.7 %reduce-scatter.2.cloned.1.call-start = ((), (), s32[]{:S(2)}) async-start(), calls=%async_computation.7 | async-start | bytes 14155776 | tf_op jit(solution)/shard_map/reduce_scatter | solution.py:808
  134.1 36.8 %collective-permute-start.5 = (bf16[576,1024]{1,0:T(8,128)(2,1)}, bf16[576,1024]{1,0:T(8,128)(2,1)}, u32[]{:S(2)}, u32[]{:S(2)}) collective-permute-start(bf16[576,1024]{1,0:T(8,128)(2,1)} %pad_maximum_fusion.2), channel_id=1, source_target_pairs={{0,8},{8,16},{16,24},{24,0},{1,9},{9,17},{17,25},{25,1},{2,10},{10... | collective-permute-start | bytes 3538952 | tf_op jit(solution)/shard_map/ppermute | solution.py:73
  186.9 50.9 %collective-permute-start.10 = (bf16[512,1536]{1,0:T(8,128)(2,1)S(1)}, bf16[512,1536]{1,0:T(8,128)(2,1)}, u32[]{:S(2)}, u32[]{:S(2)}) collective-permute-start(bf16[512,1536]{1,0:T(8,128)(2,1)S(1)} %multiply_convert_fusion.refs_0_), channel_id=1, source_target_pairs={{0,2},{2,0},{1,3},{3,1},{4,6},{6,4},{5,7},{7,5},{8,10},{10,8},{9,1... | collective-permute-start | bytes 4718600 | tf_op jit(solution)/shard_map/ppermute | solution.py:68
  188.4 52.1 %collective-permute-start.11 = (bf16[512,1536]{1,0:T(8,128)(2,1)S(1)}, bf16[512,1536]{1,0:T(8,128)(2,1)}, u32[]{:S(2)}, u32[]{:S(2)}) collective-permute-start(bf16[512,1536]{1,0:T(8,128)(2,1)S(1)} %multiply_convert_fusion.refs_0_), channel_id=1, source_target_pairs={{0,4},{4,0},{1,5},{5,1},{2,6},{6,2},{3,7},{7,3},{8,12},{12,8},{9,1... | collective-permute-start | bytes 4718600 | tf_op jit(solution)/shard_map/ppermute | solution.py:68
  189.5 54.9 %collective-permute-start.8 = (bf16[576,1024]{1,0:T(8,128)(2,1)S(1)}, bf16[576,1024]{1,0:T(8,128)(2,1)}, u32[]{:S(2)}, u32[]{:S(2)}) collective-permute-start(bf16[576,1024]{1,0:T(8,128)(2,1)S(1)} %copy-done.20), channel_id=1, source_target_pairs={{0,16},{8,24},{16,0},{24,8},{1,17},{9,25},{17,1},{25,9},{2,18},{10... | collective-permute-start | bytes 3538952 | tf_op jit(solution)/shard_map/ppermute | solution.py:73
  191.3 71.0 %collective-permute-start.9 = (bf16[576,1024]{1,0:T(8,128)(2,1)S(1)}, bf16[576,1024]{1,0:T(8,128)(2,1)S(1)}, u32[]{:S(2)}, u32[]{:S(2)}) collective-permute-start(bf16[576,1024]{1,0:T(8,128)(2,1)S(1)} %copy-done.20), channel_id=1, source_target_pairs={{0,24},{8,0},{16,8},{24,16},{1,25},{9,1},{17,9},{25,17},{2,26},{10... | collective-permute-start | bytes 3538952 | tf_op jit(solution)/shard_map/ppermute | solution.py:73
  289.6 32.8 %collective-permute-start.7 = (bf16[512,1536]{1,0:T(8,128)(2,1)S(1)}, bf16[512,1536]{1,0:T(8,128)(2,1)S(1)}, u32[]{:S(2)}, u32[]{:S(2)}) collective-permute-start(bf16[512,1536]{1,0:T(8,128)(2,1)S(1)} %multiply_convert_fusion.refs_0_), channel_id=1, source_target_pairs={{0,1},{1,0},{2,3},{3,2},{4,5},{5,4},{6,7},{7,6},{8,9},{9,8},{10,11... | collective-permute-start | bytes 4718600 | tf_op jit(solution)/shard_map/ppermute | solution.py:68
  320.3 37.7 %collective-permute-start.22 = (bf16[2,512,768]{2,1,0:T(8,128)(2,1)}, bf16[2,512,768]{2,1,0:T(8,128)(2,1)}, u32[]{:S(2)}, u32[]{:S(2)}) collective-permute-start(bf16[2,512,768]{2,1,0:T(8,128)(2,1)} %get-tuple-element.115), channel_id=1, source_target_pairs={{0,4},{4,0},{1,5},{5,1},{2,6},{6,2},{3,7},{7,3},{8,12},{12,8},{9,1... | collective-permute-start | bytes 4718600 | tf_op jit(solution)/shard_map/ppermute | solution.py:68
  320.9 37.2 %collective-permute-start.20 = (bf16[2,512,768]{2,1,0:T(8,128)(2,1)}, bf16[2,512,768]{2,1,0:T(8,128)(2,1)}, u32[]{:S(2)}, u32[]{:S(2)}) collective-permute-start(bf16[2,512,768]{2,1,0:T(8,128)(2,1)} %get-tuple-element.116), channel_id=1, source_target_pairs={{0,2},{2,0},{1,3},{3,1},{4,6},{6,4},{5,7},{7,5},{8,10},{10,8},{9,1... | collective-permute-start | bytes 4718600 | tf_op jit(solution)/shard_map/ppermute | solution.py:68
  343.2 50.1 %collective-permute-start.19 = (bf16[512,1536]{1,0:T(8,128)(2,1)S(1)}, bf16[512,1536]{1,0:T(8,128)(2,1)}, u32[]{:S(2)}, u32[]{:S(2)}) collective-permute-start(bf16[512,1536]{1,0:T(8,128)(2,1)S(1)} %slice_bitcast_fusion), channel_id=1, source_target_pairs={{0,1},{1,0},{2,3},{3,2},{4,5},{5,4},{6,7},{7,6},{8,9},{9,8},{10,11... | collective-permute-start | bytes 4718600 | tf_op jit(solution)/shard_map/ppermute | solution.py:68
  360.3 29.7 %collective-permute-start.21 = (bf16[512,768]{1,0:T(8,128)(2,1)S(1)}, bf16[512,768]{1,0:T(8,128)(2,1)}, u32[]{:S(2)}, u32[]{:S(2)}) collective-permute-start(bf16[512,768]{1,0:T(8,128)(2,1)S(1)} %get-tuple-element.113), channel_id=1, source_target_pairs={{0,4},{4,0},{1,5},{5,1},{2,6},{6,2},{3,7},{7,3},{8,12},{12,8},{9,1... | collective-permute-start | bytes 2359304 | tf_op jit(solution)/shard_map/ppermute | solution.py:68
  408.0 95.0 %collective-permute-start.28 = (bf16[576,1024]{1,0:T(8,128)(2,1)}, bf16[576,1024]{1,0:T(8,128)(2,1)}, u32[]{:S(2)}, u32[]{:S(2)}) collective-permute-start(bf16[576,1024]{1,0:T(8,128)(2,1)} %get-tuple-element.112), channel_id=1, source_target_pairs={{0,8},{8,16},{16,24},{24,0},{1,9},{9,17},{17,25},{25,1},{2,10},{10... | collective-permute-start | bytes 3538952 | tf_op jit(solution)/shard_map/ppermute | solution.py:73
  418.6 132.0 %collective-permute-start.31 = (bf16[576,1024]{1,0:T(8,128)(2,1)}, bf16[576,1024]{1,0:T(8,128)(2,1)}, u32[]{:S(2)}, u32[]{:S(2)}) collective-permute-start(bf16[576,1024]{1,0:T(8,128)(2,1)} %get-tuple-element.111), channel_id=1, source_target_pairs={{0,16},{8,24},{16,0},{24,8},{1,17},{9,25},{17,1},{25,9},{2,18},{10... | collective-permute-start | bytes 3538952 | tf_op jit(solution)/shard_map/ppermute | solution.py:73
  455.2 48.5 %collective-permute-start.27 = (bf16[4,1,2,96,768]{4,3,2,1,0:T(8,128)(2,1)}, bf16[4,1,2,96,768]{4,3,2,1,0:T(8,128)(2,1)}, u32[]{:S(2)}, u32[]{:S(2)}) collective-permute-start(bf16[4,1,2,96,768]{4,3,2,1,0:T(8,128)(2,1)} %constant_dynamic-slice_fusion.9), channel_id=1, source_target_pairs={{0,4},{4,0},{1,5},{5,1},{2,6},{6,2},{3,7},{7,3},{8,12},{12,8},{9,1... | collective-permute-start | bytes 3538952 | tf_op jit(solution)/shard_map/ppermute | solution.py:68
  489.0 61.7 %collective-permute-start.30 = (bf16[4,2,1,96,768]{4,3,0,2,1:T(8,128)(2,1)}, bf16[4,2,1,96,768]{4,3,0,2,1:T(8,128)(2,1)}, u32[]{:S(2)}, u32[]{:S(2)}) collective-permute-start(bf16[4,2,1,96,768]{4,3,0,2,1:T(8,128)(2,1)} %copy.124), channel_id=1, source_target_pairs={{0,2},{2,0},{1,3},{3,1},{4,6},{6,4},{5,7},{7,5},{8,10},{10,8},{9,1... | collective-permute-start | bytes 3538952 | tf_op jit(solution)/shard_map/ppermute | solution.py:68
  499.8 53.0 %collective-permute-start.26 = (bf16[512,1536]{1,0:T(8,128)(2,1)}, bf16[512,1536]{1,0:T(8,128)(2,1)}, u32[]{:S(2)}, u32[]{:S(2)}) collective-permute-start(bf16[512,1536]{1,0:T(8,128)(2,1)} %dynamic-slice_bitcast_fusion), channel_id=1, source_target_pairs={{0,1},{1,0},{2,3},{3,2},{4,5},{5,4},{6,7},{7,6},{8,9},{9,8},{10,11... | collective-permute-start | bytes 4718600 | tf_op jit(solution)/shard_map/ppermute | solution.py:68
  507.7 40.0 %collective-permute-start.29 = (bf16[4,1,1,96,768]{4,3,2,1,0:T(8,128)(2,1)}, bf16[4,1,1,96,768]{4,3,2,1,0:T(8,128)(2,1)}, u32[]{:S(2)}, u32[]{:S(2)}) collective-permute-start(bf16[4,1,1,96,768]{4,3,2,1,0:T(8,128)(2,1)} %add_convert_fusion.6), channel_id=1, source_target_pairs={{0,2},{2,0},{1,3},{3,1},{4,6},{6,4},{5,7},{7,5},{8,10},{10,8},{9,1... | collective-permute-start | bytes 1769480 | tf_op jit(solution)/shard_map/ppermute | solution.py:68
  530.8 53.7 %collective-permute-start.40 = (bf16[4,2,1,96,384]{4,3,0,2,1:T(8,128)(2,1)}, bf16[4,2,1,96,384]{4,3,0,2,1:T(8,128)(2,1)}, u32[]{:S(2)}, u32[]{:S(2)}) collective-permute-start(bf16[4,2,1,96,384]{4,3,0,2,1:T(8,128)(2,1)} %copy.127), channel_id=1, source_target_pairs={{0,2},{2,0},{1,3},{3,1},{4,6},{6,4},{5,7},{7,5},{8,10},{10,8},{9,1... | collective-permute-start | bytes 1769480 | tf_op jit(solution)/shard_map/ppermute | solution.py:68
  547.6 43.8 %collective-permute-start.39 = (bf16[4,1,1,96,384]{4,3,2,1,0:T(8,128)(2,1)}, bf16[4,1,1,96,384]{4,3,2,1,0:T(8,128)(2,1)}, u32[]{:S(2)}, u32[]{:S(2)}) collective-permute-start(bf16[4,1,1,96,384]{4,3,2,1,0:T(8,128)(2,1)} %add_convert_fusion.10), channel_id=1, source_target_pairs={{0,2},{2,0},{1,3},{3,1},{4,6},{6,4},{5,7},{7,5},{8,10},{10,8},{9,1... | collective-permute-start | bytes 884744 | tf_op jit(solution)/shard_map/ppermute | solution.py:68
  567.4 46.1 %all-to-all-start.1 = ((bf16[4,96,1536]{2,1,0:T(8,128)(2,1)}), bf16[4,96,1536]{2,1,0:T(8,128)(2,1)}, u32[]{:S(2)}, u32[]{:S(2)}) async-start(bf16[4,96,1536]{2,1,0:T(8,128)(2,1)} %pad_maximum_fusion.3), calls=%async_computation.2 | async-start | bytes 2359296 | tf_op jit(solution)/shard_map/all_to_all | solution.py:95
  580.6 36.8 %collective-permute-start.43 = (bf16[576,1024]{1,0:T(8,128)(2,1)}, bf16[576,1024]{1,0:T(8,128)(2,1)}, u32[]{:S(2)}, u32[]{:S(2)}) collective-permute-start(bf16[576,1024]{1,0:T(8,128)(2,1)} %get-tuple-element.110), channel_id=1, source_target_pairs={{0,24},{8,0},{16,8},{24,16},{1,25},{9,1},{17,9},{25,17},{2,26},{10... | collective-permute-start | bytes 3538952 | tf_op jit(solution)/shard_map/ppermute | solution.py:73
  586.2 54.4 %collective-permute-start.41 = (bf16[4,1,1,96,384]{4,3,0,2,1:T(8,128)(2,1)}, bf16[4,1,1,96,384]{4,3,0,2,1:T(8,128)(2,1)}, u32[]{:S(2)}, u32[]{:S(2)}) collective-permute-start(bf16[4,1,1,96,384]{4,3,0,2,1:T(8,128)(2,1)} %add_convert_fusion.8), channel_id=1, source_target_pairs={{0,4},{4,0},{1,5},{5,1},{2,6},{6,2},{3,7},{7,3},{8,12},{12,8},{9,1... | collective-permute-start | bytes 884744 | tf_op jit(solution)/shard_map/ppermute | solution.py:68
  (84 other events, 996.2 us)
Sparse Core Ops, SparseCore 0:
  11.5 122.5 all-gather.2
  136.0 83.9 all-gather.4
  404.3 142.2 reduce-scatter.1

commit v2 on v1

--- a/solution.py
+++ b/solution.py
@@ -172,8 +172,10 @@
     return pieces
 
 
-def relative_sum(pieces):
+def relative_sum(pieces, arrived=False):
     pieces = list(pieces)
+    if arrived:
+        return total_of(pieces)
     bit = len(pieces) // 2
     while bit:
         for index in range(bit):
@@ -265,13 +267,14 @@
     return slice(first, first + SLOT)
 
 
-def forward_kernel(block, joined_ref, table_ref, start_ref, place_ref, back_ref,
-                   out_ref, kept_ref, logsum_ref):
-    length = joined_ref.shape[0]
+def forward_kernel(block, member_ref, input_ref, weight_ref, table_ref, start_ref, place_ref,
+                   back_ref, head_ref, out_ref, kept_ref, logsum_ref, part_ref, total_ref):
+    length = input_ref.shape[0]
     cosine = table_ref[:, :SLOT]
     sine = table_ref[:, SLOT:]
     for group in range(PAIR):
-        joined = joined_ref[:, group * JOINED : (group + 1) * JOINED]
+        weight = weight_ref[:, group * JOINED : (group + 1) * JOINED]
+        joined = product(input_ref[...], weight).astype(BF16)
         placed = product(joined, place_ref[...])
         for slot in range(SLOTS):
             part = placed[:, slot * SLOT : (slot + 1) * SLOT]
@@ -301,14 +304,28 @@
                     lane == group * GROUP + head, peak + jnp.log2(total), logsums
                 )
         logsum_ref[0, rows, :] = logsums
-        out_ref[rows, :] = product(jnp.concatenate(outs, axis=1), back_ref[...]).astype(BF16)
-
-
-def backward_kernel(block, kept_ref, table_ref, start_ref, logsum_ref, att_ref, grad_ref,
-                    place_ref, back_ref, out_ref):
+        compact = product(jnp.concatenate(outs, axis=1), back_ref[...]).astype(BF16)
+        out_ref[rows, :] = compact
+        part = product(compact, head_ref[...])
+
+        @pl.when(pl.program_id(0) == 0)
+        def _():
+            total_ref[rows, :] = part
+
+        @pl.when(pl.program_id(0) > 0)
+        def _():
+            total_ref[rows, :] += part
+
+    @pl.when(pl.program_id(0) == pl.num_programs(0) - 1)
+    def _():
+        part_ref[...] = total_ref[...].astype(BF16)
+
+
+def backward_kernel(block, kept_ref, table_ref, start_ref, logsum_ref, att_ref, branch_ref,
+                    head_ref, place_ref, back_ref, out_ref):
     length = kept_ref.shape[0]
     att = product(att_ref[...], place_ref[...])
-    grad = product(grad_ref[...], place_ref[...])
+    grad = product(against(branch_ref[...], head_ref[...]).astype(BF16), place_ref[...])
     both = att * grad
     grad_low = grad.astype(BF16)
     blocks = length // block
@@ -361,42 +378,50 @@
             ).astype(BF16)
 
 
-def attention_forward(joined, table, start):
-    length, width = joined.shape
-    steps = width // (PAIR * JOINED)
+def attention_forward(member, value, weights, table, start, heads):
+    length, width = value.shape
     out_width = PAIR * GROUP * HEAD_DIM
+    steps = heads.shape[0] // out_width
     kept_width = PAIR * SLOTS * SLOT
     place = jnp.asarray(placement(SLOTS), BF16)
     back = jnp.asarray(placement(PAIR * GROUP).T, BF16)
     block = min(256, length)
-    flops = steps * PAIR * GROUP * length * (length // 2 + block // 2) * SLOT * 4
+    whole = lambda s, m: (0, 0)
     return pl.pallas_call(
         functools.partial(forward_kernel, block),
-        grid=(steps,),
-        in_specs=[
-            pl.BlockSpec((length, PAIR * JOINED), lambda s: (0, s)),
-            pl.BlockSpec((length, 2 * SLOT), lambda s: (0, 0)),
-            pl.BlockSpec((length, 1), lambda s: (0, 0)),
-            pl.BlockSpec(place.shape, lambda s: (0, 0)),
-            pl.BlockSpec(back.shape, lambda s: (0, 0)),
-        ],
-        out_specs=[
-            pl.BlockSpec((length, out_width), lambda s: (0, s)),
-            pl.BlockSpec((length, kept_width), lambda s: (0, s)),
-            pl.BlockSpec((1, length, SLOT), lambda s: (s, 0, 0)),
-        ],
+        grid_spec=pltpu.PrefetchScalarGridSpec(
+            num_scalar_prefetch=1,
+            grid=(steps,),
+            in_specs=[
+                pl.BlockSpec((length, width), whole),
+                pl.BlockSpec((width, PAIR * JOINED), lambda s, m: (0, m[0] * steps + s)),
+                pl.BlockSpec((length, 2 * SLOT), whole),
+                pl.BlockSpec((length, 1), whole),
+                pl.BlockSpec(place.shape, whole),
+                pl.BlockSpec(back.shape, whole),
+                pl.BlockSpec((out_width, width), lambda s, m: (s, 0)),
+            ],
+            out_specs=[
+                pl.BlockSpec((length, out_width), lambda s, m: (0, s)),
+                pl.BlockSpec((length, kept_width), lambda s, m: (0, s)),
+                pl.BlockSpec((1, length, SLOT), lambda s, m: (s, 0, 0)),
+                pl.BlockSpec((length, width), whole),
+            ],
+            scratch_shapes=[pltpu.VMEM((length, width), F32)],
+        ),
         out_shape=[
             jax.ShapeDtypeStruct((length, steps * out_width), BF16),
             jax.ShapeDtypeStruct((length, steps * kept_width), BF16),
             jax.ShapeDtypeStruct((steps, length, SLOT), F32),
+            jax.ShapeDtypeStruct((length, width), BF16),
         ],
         compiler_params=pltpu.CompilerParams(vmem_limit_bytes=VMEM_LIMIT),
         cost_estimate=SMALL_COST,
         name="attention_forward",
-    )(joined, table, start, place, back)
-
-
-def attention_backward(kept, table, start, logsum, att, grad, first, steps):
+    )(member, value, weights, table, start, place, back, heads)
+
+
+def attention_backward(kept, table, start, logsum, att, branch, heads, first, steps):
     length = att.shape[0]
     out_width = PAIR * GROUP * HEAD_DIM
     kept_width = PAIR * SLOTS * SLOT
@@ -413,7 +438,8 @@
             pl.BlockSpec((length, 1), lambda s: (0, 0)),
             pl.BlockSpec((1, length, SLOT), lambda s: (s + first, 0, 0)),
             pl.BlockSpec((length, out_width), lambda s: (0, s + first)),
-            pl.BlockSpec((length, out_width), lambda s: (0, s)),
+            pl.BlockSpec(branch.shape, lambda s: (0, 0)),
+            pl.BlockSpec((out_width, branch.shape[1]), lambda s: (s + first, 0)),
             pl.BlockSpec(place.shape, lambda s: (0, 0)),
             pl.BlockSpec(back.shape, lambda s: (0, 0)),
         ],
@@ -422,20 +448,24 @@
         compiler_params=pltpu.CompilerParams(vmem_limit_bytes=VMEM_LIMIT),
         cost_estimate=SMALL_COST,
         name="attention_backward",
-    )(kept, table, start, logsum, att, grad, place, back)
+    )(kept, table, start, logsum, att, branch, heads, place, back)
 
 
 def fetched(parts, c_refs, c_ref, sems):
     step = pl.program_id(0)
 
     def copies(index):
-        first = sum(parts[:index])
-        column = 0
-        for part, ref in enumerate(c_refs[first : first + parts[index]]):
-            size = ref.shape[1]
-            target = c_ref.at[index % 2, :, pl.ds(column, size)]
-            yield pltpu.make_async_copy(ref, target, sems.at[index % 2, part])
-            column += size
+        ref_index = sum(sum(rows) for rows in parts[:index])
+        number = 0
+        for block, count in enumerate(parts[index]):
+            column = 0
+            for ref in c_refs[ref_index : ref_index + count]:
+                own, size = ref.shape
+                target = c_ref.at[index % 2, pl.ds(block * own, own), pl.ds(column, size)]
+                yield pltpu.make_async_copy(ref, target, sems.at[index % 2, number])
+                column += size
+                number += 1
+            ref_index += count
 
     for index in range(len(parts)):
 
@@ -453,8 +483,14 @@
     return c_ref[step % 2]
 
 
+def counted(c):
+    parts = tuple(tuple(len(block) for block in step) for step in c)
+    return parts, [part for step in c for block in step for part in block]
+
+
 def feed_kernel(parts, residual, fresh, places_ref, *refs):
-    c_refs, refs = refs[: sum(parts)], refs[sum(parts) :]
+    number = sum(sum(rows) for rows in parts)
+    c_refs, refs = refs[:number], refs[number:]
     (dy_ref, expand_ref, down_ref), refs = refs[:3], refs[3:]
     if residual:
         hidden_ref, refs = refs[0], refs[1:]
@@ -483,12 +519,13 @@
         out_ref[0] = out.astype(BF16)
 
 
-def c_scratch(own, width):
-    return [pltpu.VMEM((2, own, width), BF16), pltpu.SemaphoreType.DMA((2, 2))]
+def c_scratch(parts, rows, width):
+    number = max(sum(counts) for counts in parts)
+    return [pltpu.VMEM((2, rows, width), BF16), pltpu.SemaphoreType.DMA((2, number))]
 
 
 def feed_forward(places, c, dy, expand, down, blocks, before=None, hidden_res=None):
-    parts = tuple(len(block) for block in c)
+    parts, flat = counted([[block] for block in c])
     steps = len(c)
     own, width = dy.shape[1] // (blocks // 4), dy.shape[2]
     hidden = down.shape[0]
@@ -497,7 +534,6 @@
     single = pl.Buffered(1)
     whole = lambda s, p: (0, 0)
     token = pl.BlockSpec((1, own, width), lambda s, p: (p[s, 1], p[s, 2], 0))
-    flat = [part for block in c for part in block]
     operands = [places, *flat, dy, expand, down]
     in_specs = [pl.BlockSpec(memory_space=pl.ANY)] * len(flat) + [
         token,
@@ -523,7 +559,7 @@
                 pl.BlockSpec((1, 3, own, hidden), lambda s, p: (p[s, 0], 0, 0, 0)),
                 pl.BlockSpec((1, own, width), lambda s, p: (s, 0, 0)),
             ],
-            scratch_shapes=c_scratch(own, width),
+            scratch_shapes=c_scratch(parts, own, width),
         ),
         out_shape=[
             jax.ShapeDtypeStruct(dy.shape, BF16),
@@ -547,27 +583,35 @@
         total_ref[:, columns] += value
 
 
-def down_grad_kernel(rows, places_ref, dy_ref, mixed_ref, out_ref, total_ref):
-    accumulate(total_ref, tokens_product(mixed_ref[0, 0], dy_ref[0]))
+def down_grad_kernel(rows, count, places_ref, *refs):
+    dy_refs, (mixed_ref, out_ref, total_ref, dy_buffer) = refs[:count], refs[count:]
+    own, hidden = mixed_ref.shape[2], mixed_ref.shape[3]
+    for index in range(count):
+        dy_buffer[index * own : (index + 1) * own, :] = dy_refs[index][0]
+    mixed = mixed_ref[...].reshape(count * own, hidden)
+    accumulate(total_ref, tokens_product(mixed, dy_buffer[...]))
     width, columns = total_ref.shape[1], out_ref.shape[2]
 
     @pl.when(pl.program_id(0) == pl.num_programs(0) - 1)
     def _():
         for place in range(out_ref.shape[0]):
-            for to_row, count, to_column, row, column, size in pack_chunks(rows, width, columns):
+            for to_row, size_row, to_column, row, column, size in pack_chunks(rows, width, columns):
                 first = place * rows + row
-                out_ref[place, to_row : to_row + count, to_column : to_column + size] = total_ref[
-                    first : first + count, column : column + size
-                ].astype(BF16)
-
-
-def expand_grad_kernel(parts, places_ref, *refs):
-    c_refs, refs = refs[: sum(parts)], refs[sum(parts) :]
+                out_ref[place, to_row : to_row + size_row, to_column : to_column + size] = (
+                    total_ref[first : first + size_row, column : column + size].astype(BF16)
+                )
+
+
+def expand_grad_kernel(parts, *refs):
+    number = sum(sum(rows) for rows in parts)
+    c_refs, refs = refs[:number], refs[number:]
     dgate_ref, dup_ref, _, out_ref, total_ref, c_buffer, sems = refs
-    hidden = dgate_ref.shape[3]
+    count, _, own, hidden = dgate_ref.shape
     c = fetched(parts, c_refs, c_buffer, sems)
-    accumulate(total_ref, tokens_product(c, dgate_ref[0, 0]), slice(0, hidden))
-    accumulate(total_ref, tokens_product(c, dup_ref[0, 0]), slice(hidden, None))
+    dgate = dgate_ref[...].reshape(count * own, hidden)
+    dup = dup_ref[...].reshape(count * own, hidden)
+    accumulate(total_ref, tokens_product(c, dgate), slice(0, hidden))
+    accumulate(total_ref, tokens_product(c, dup), slice(hidden, None))
 
     @pl.when(pl.program_id(0) == pl.num_programs(0) - 1)
     def _():
@@ -576,59 +620,62 @@
 
 def down_grads(places, dy, terms, n_dp, rows_before):
     blocks, _, own, hidden = terms.shape
+    count = blocks // 4
     width = dy.shape[2]
     packed = hidden * width // (2 * hidden) // n_dp
+
+    def dy_spec(index):
+        return pl.BlockSpec((1, own, width), lambda s, p: (p[s, 0], p[s, 1] ^ index, 0))
+
     return pl.pallas_call(
-        functools.partial(down_grad_kernel, hidden // n_dp),
+        functools.partial(down_grad_kernel, hidden // n_dp, count),
         grid_spec=pltpu.PrefetchScalarGridSpec(
             num_scalar_prefetch=1,
-            grid=(blocks,),
-            in_specs=[
-                pl.BlockSpec((1, own, width), lambda s, p: (p[s, 1], p[s, 2], 0)),
-                pl.BlockSpec((1, 1, own, hidden), lambda s, p: (p[s, 0], 0, 0, 0)),
-            ],
+            grid=(4,),
+            in_specs=[dy_spec(index) for index in range(count)]
+            + [pl.BlockSpec((count, 1, own, hidden), lambda s, p: (s, 0, 0, 0))],
             out_specs=pl.BlockSpec(
                 (n_dp, packed, 2 * hidden),
                 lambda s, p: (0, rows_before // packed, 0),
                 pipeline_mode=pl.Buffered(1),
             ),
-            scratch_shapes=[pltpu.VMEM((hidden, width), F32)],
+            scratch_shapes=[
+                pltpu.VMEM((hidden, width), F32), pltpu.VMEM((count * own, width), BF16)
+            ],
         ),
         out_shape=jax.ShapeDtypeStruct((n_dp, rows_before + packed, 2 * hidden), BF16),
         compiler_params=pltpu.CompilerParams(vmem_limit_bytes=VMEM_LIMIT),
         cost_estimate=SMALL_COST,
         name="down_grads",
-    )(places, dy, terms)
-
-
-def expand_grads(places, c, terms, packed, rows):
-    parts = tuple(len(block) for block in c)
+    )(places, *([dy] * count), terms)
+
+
+def expand_grads(c, terms, packed, rows):
+    parts, flat = counted(c)
     blocks, _, own, hidden = terms.shape
+    count = blocks // 4
     n_dp = packed.shape[0]
     width = n_dp * rows
-    flat = [part for block in c for part in block]
     return pl.pallas_call(
         functools.partial(expand_grad_kernel, parts),
-        grid_spec=pltpu.PrefetchScalarGridSpec(
-            num_scalar_prefetch=1,
-            grid=(blocks,),
-            in_specs=[pl.BlockSpec(memory_space=pl.ANY)] * len(flat)
-            + [
-                pl.BlockSpec((1, 1, own, hidden), lambda s, p: (p[s, 0], 1, 0, 0)),
-                pl.BlockSpec((1, 1, own, hidden), lambda s, p: (p[s, 0], 2, 0, 0)),
-                pl.BlockSpec(memory_space=pl.ANY),
-            ],
-            out_specs=pl.BlockSpec(
-                (n_dp, rows, 2 * hidden), lambda s, p: (0, 0, 0), pipeline_mode=pl.Buffered(1)
-            ),
-            scratch_shapes=[pltpu.VMEM((width, 2 * hidden), F32)] + c_scratch(own, width),
+        grid=(4,),
+        in_specs=[pl.BlockSpec(memory_space=pl.ANY)] * len(flat)
+        + [
+            pl.BlockSpec((count, 1, own, hidden), lambda s: (s, 1, 0, 0)),
+            pl.BlockSpec((count, 1, own, hidden), lambda s: (s, 2, 0, 0)),
+            pl.BlockSpec(memory_space=pl.ANY),
+        ],
+        out_specs=pl.BlockSpec(
+            (n_dp, rows, 2 * hidden), lambda s: (0, 0, 0), pipeline_mode=pl.Buffered(1)
         ),
+        scratch_shapes=[pltpu.VMEM((width, 2 * hidden), F32)]
+        + c_scratch(parts, count * own, width),
         out_shape=jax.ShapeDtypeStruct(packed.shape, BF16),
-        input_output_aliases={1 + len(flat) + 2: 0},
+        input_output_aliases={len(flat) + 2: 0},
         compiler_params=pltpu.CompilerParams(vmem_limit_bytes=VMEM_LIMIT),
         cost_estimate=SMALL_COST,
         name="expand_grads",
-    )(places, *flat, terms, terms, packed)
+    )(*flat, terms, terms, packed)
 
 
 def local(
@@ -736,20 +783,21 @@
 
     inv_all = lax.rsqrt(jnp.mean(resid_all * resid_all, axis=-1, keepdims=True) + EPSILON)
     first_in = (resid_all * inv_all * gain_one).astype(BF16)
-    joined = product(first_in, in_low).astype(BF16)
-    att_low, kept, logsum = attention_forward(joined, table, start)
-    att_low = after(att_low, feed_pieces[0])
+    att_low, kept, logsum, hidden_part = attention_forward(
+        me[None].astype(jnp.int32), first_in, attend_all, table, start, out_low
+    )
+    hidden_part = after(hidden_part, feed_pieces[0])
 
     def own_sum(value):
         grid = value.reshape(n_tp, own, width)
         if n_tp != 2:
-            return lax.psum_scatter(grid, "tp", scatter_dimension=0, tiled=True)[0].astype(F32)
+            return lax.psum_scatter(grid, "tp", scatter_dimension=0, tiled=True)[0]
         came = exchange(lax.dynamic_index_in_dim(grid, 1 - me, 0, keepdims=False), "tp")
         mine = lax.dynamic_index_in_dim(grid, me, 0, keepdims=False)
         return mine.astype(F32) + came.astype(F32)
 
     resid = resid.astype(F32)
-    hidden_res = resid + own_sum(product(att_low, out_low).astype(BF16))
+    hidden_res = resid + own_sum(hidden_part)
     inv_two = lax.rsqrt(jnp.mean(hidden_res * hidden_res, axis=-1, keepdims=True) + EPSILON)
     normed_two = hidden_res * inv_two
     second_in = (normed_two * gain_two).astype(BF16)
@@ -771,41 +819,52 @@
         c = [pieces_of(relative, member) for relative, member in order]
         return feed_forward(rows, c, dy_all, expand_all, down_all, blocks, before, residual)
 
-    near_order = [(0, member) for member in range(n_tp)]
-    first_order = [(r, member) for member in range(1, n_tp) for r in (1, 2, 3)]
-    second_order = [(r, 0) for r in (1, 2, 3)]
-    out_all, terms, first_dc = feed_call(first_order)
+    def after_calls(*ready):
+        return lax.optimization_barrier((out_all, terms) + ready)[:2]
+
+    members = list(range(n_tp))
+    far_order = [(r, member) for member in members[1:] for r in (3, 1, 2)]
+    out_all, terms, first_dc = feed_call(far_order)
+    out_all, terms, corner_dc = feed_call([(3, 0)], (out_all, terms))
     first_dc = first_dc.reshape(n_tp - 1, 3, own, width)
-    first_sent = [first_dc[member] for member in range(n_tp - 1)]
-    out_all, terms, second_dc = feed_call(second_order, (out_all, terms))
-    far_sum = relative_sum([second_dc] + first_sent).astype(BF16)
+    first_came = list(first_dc)
+    if n_tp == 2:
+        first_came = [exchange(first_dc[0], "tp")]
+    corner = relative_sum([corner_dc[0]] + [value[0] for value in first_came], n_tp == 2).astype(BF16)
     middle = width // 2
-    left_sent, right_sent = far_sum[0::2, :, :middle], far_sum[1:, :, middle:]
+    corner = (corner[:, :middle], corner[:, middle:])
+    corner_left = exchange(corner[0], "lo")
+    corner_right = exchange(corner[1], "hi")
+    out_all, terms, second_dc = feed_call([(1, 0), (2, 0)], after_calls(*corner))
+    beside, across = relative_sum(
+        [second_dc] + [value[1:] for value in first_came], n_tp == 2
+    ).astype(BF16)
+    left_sent = jnp.stack(
+        [beside[:, :middle], total_of([beside[:, middle:], corner_right])]
+    ).astype(BF16)
+    right_sent = jnp.stack(
+        [across[:, middle:], total_of([across[:, :middle], corner_left])]
+    ).astype(BF16)
     out_all, terms, near_dc = feed_call(
-        near_order, lax.optimization_barrier((out_all, terms, left_sent, right_sent))[:2], hidden_res
-    )
-    every_order = near_order + first_order + second_order
-    every_rows = jnp.stack([place_row(relative, member) for relative, member in every_order])
-    packed = down_grads(every_rows, dy_all, terms, n_dp, rows_expand)
-    near = relative_sum([near_dc[member] for member in range(n_tp)])
+        [(0, member) for member in members], after_calls(left_sent, right_sent), hidden_res
+    )
+    near = relative_sum([near_dc[member] for member in members])
+    chip_rows = jnp.stack([place_row(relative, 0)[1:] for relative in range(4)])
+    packed = down_grads(chip_rows, dy_all, terms, n_dp, rows_expand)
     left_came = after(exchange(left_sent, "lo"), packed)
     right_came = after(exchange(right_sent, "hi"), packed)
-    left = total_of([far_sum[1, :, :middle], left_came[1]]).astype(BF16)
-    right = total_of([far_sum[0, :, middle:], right_came[1]]).astype(BF16)
     feed_terms = expand_grads(
-        every_rows,
-        [pieces_of(relative, member) for relative, member in every_order],
+        [[pieces_of(relative, member) for member in members] for relative in range(4)],
         terms,
-        after(packed, left, right),
+        after(packed, left_came, right_came),
         rows_expand,
     )
-    left = after(exchange(left, "hi"), feed_terms)
-    right = after(exchange(right, "lo"), feed_terms)
+    left_came, right_came = after(left_came, feed_terms), after(right_came, feed_terms)
     second_grad = near.astype(F32) + jnp.concatenate(
-        [total_of([left_came[0], left]), total_of([right_came[0], right])], axis=1
-    )
-    out_all, second_grad = lax.optimization_barrier((out_all, second_grad))
+        [total_of([left_came[0], right_came[1]]), total_of([left_came[1], right_came[0]])], axis=1
+    )
     block_out = lax.psum_scatter(out_all, CTX, scatter_dimension=1, tiled=True)
+    feed_sum = lax.psum_scatter(feed_terms, "dp", scatter_dimension=0, tiled=True)[0]
 
     upstream = lax.dynamic_slice(dy_all, (stream_place, me * own, 0), (1, own, width))[0]
     upstream = upstream.astype(F32)
@@ -813,7 +872,6 @@
     branch_all = group_gather(hidden_grad.astype(BF16))
     att_steps = logsum.shape[0]
     cuts = [0, att_steps // 2, att_steps] if att_steps > 1 else [0, 1]
-    heads_width = PAIR * GROUP * HEAD_DIM
     def plane_stage(terms, name):
         return axis_sum(terms, name, 1 if name == "hi" else 2)
 
@@ -825,22 +883,13 @@
 
     orders = (("hi", "lo"), ("lo", "hi"))
 
-    def heads_grad(index):
-        part = out_low[cuts[index] * heads_width : cuts[index + 1] * heads_width]
-        return against(branch_all, part).astype(BF16)
-
-    def heads_back(index, grad):
+    def heads_back(index, branch):
         begin, end = cuts[index], cuts[index + 1]
-        return attention_backward(kept, table, start, logsum, att_low, grad, begin, end - begin)
-
-    dp_place = lax.axis_index("dp")
-
-    def feed_piece(step):
-        return lax.dynamic_index_in_dim(feed_terms, (dp_place + step) % n_dp, 0, keepdims=False)
-
-    feed_came = [shifted(feed_piece(step), step) for step in range(1, n_dp)]
-
-    joined_parts = [heads_back(0, heads_grad(0))]
+        return attention_backward(
+            kept, table, start, logsum, att_low, branch, out_low, begin, end - begin
+        )
+
+    joined_parts = [heads_back(0, branch_all)]
     in_parts = [tokens_product(first_in, joined_parts[0]).astype(BF16)]
 
     branch_late = after(branch_all, joined_parts[0])
@@ -863,18 +912,24 @@
     out_parts = [out_term[:, :half], out_term[:, half:]]
 
     if len(cuts) > 2:
-        grad = after(heads_grad(1), in_parts[0], out_term)
-        joined_parts.append(heads_back(1, grad))
+        joined_parts.append(heads_back(1, after(branch_all, in_parts[0], out_term)))
     in_terms = [plane_stage(plane_grid(in_parts[0]), orders[0][0])]
-    in_terms[0][-1] = after(in_terms[0][-1], feed_came[0])
+    out_terms = [
+        plane_stage(plane_grid(part), order[0]) for part, order in zip(out_parts, orders)
+    ]
+    came = [terms[-1] for terms in out_terms]
+    came = [after(value, joined_parts[-1]) for value in came]
+    for terms, value in zip(out_terms, came):
+        terms[-1] = value
     if len(cuts) > 2:
-        in_parts.append(tokens_product(first_in, joined_parts[1]).astype(BF16))
+        late_in = after(first_in, *came)
+        in_parts.append(tokens_product(late_in, joined_parts[1]).astype(BF16))
         in_terms.append(plane_stage(plane_grid(in_parts[1]), orders[1][0]))
-        in_terms[-1][-1] = after(in_terms[-1][-1], feed_came[1])
-    out_terms = [
-        plane_stage(plane_grid(after(part, in_parts[-1])), order[0])
-        for part, order in zip(out_parts, orders)
-    ]
+    late = in_terms[-1][-1]
+    for terms in out_terms:
+        terms[-1] = after(terms[-1], late)
+    in_terms[0][-1] = after(in_terms[0][-1], late)
+    feed_sum = after(feed_sum, late)
     in_terms = [plane_stage(terms, order[1]) for terms, order in zip(in_terms, orders)]
     out_terms = [plane_stage(terms, order[1]) for terms, order in zip(out_terms, orders)]
     joined_all = after(jnp.concatenate(joined_parts, axis=1), in_parts[-1])
@@ -883,18 +938,14 @@
     ready = (first_part,) + tuple(terms[-1] for terms in in_terms)
     low = F32 if n_tp != 2 else BF16
 
-    def owned(terms):
-        rows = column_sum(terms).reshape(n_tp, row_in, -1)
-        return group_swap(rows.astype(low)).astype(F32).transpose(1, 0, 2).reshape(row_in, -1)
-
-    in_sum = owned(in_terms)
-    out_terms[-1][-1] = after(out_terms[-1][-1], in_sum)
-    out_sum = owned(out_terms)
-    feed_sum = total_of([feed_piece(0)] + [after(came, in_sum) for came in feed_came])
-    expand_rows = feed_sum[:rows_expand].astype(BF16).reshape(n_ctx, row_in, -1)
-    expand_sum = ctx_swap(after(expand_rows, in_sum)).reshape(n_ctx, row_in, 2, n_dp, row_down)
+    rows = column_sum(in_terms + out_terms).reshape(n_tp, row_in, -1)
+    rows = group_swap(rows.astype(low)).astype(F32).transpose(1, 0, 2)
+    in_sum = rows[:, :, :part_in].reshape(row_in, joined_width)
+    out_sum = rows[:, :, part_in:].reshape(row_in, width)
+    expand_rows = feed_sum[:rows_expand].reshape(n_ctx, row_in, -1)
+    expand_sum = ctx_swap(expand_rows).reshape(n_ctx, row_in, 2, n_dp, row_down)
     expand_sum = expand_sum.transpose(1, 2, 3, 0, 4).reshape(row_in, 2 * FF).astype(F32)
-    contract_sum = unpacked_rows(feed_sum[rows_expand:], row_down, width)
+    contract_sum = unpacked_rows(feed_sum[rows_expand:].astype(F32), row_down, width)
 
     inv_one = lax.rsqrt(jnp.mean(resid * resid, axis=-1, keepdims=True) + EPSILON)
     first_grad = own_sum(first_part)

time: 695 us -> 669 us (0.963)
  Pallas kernels: 156 us -> 183 us
  matrix products: 43.1 us -> 19.4 us
  local copies, waits for them, and re-layouts: 83.5 us -> 68.4 us
  other arithmetic: 89.7 us -> 81.1 us
  starting transfers between devices: 86.2 us -> 77.7 us
    ppermute x6 -> x3, starting transfers between devices: 22.5 us -> 4.43 us  [shifted(): lax.ppermute(value, 'dp', [(i, (i + step) % count) for i in range(count)])]
    pallas_call x3 -> x4, Pallas kernels: 62.9 us -> 77.7 us  [feed_forward(): pl.pallas_call(functools.partial(feed_kernel, parts, residual, fresh), gr...]
    dot_general x2 -> x0, matrix products: 14 us -> none  [product(): return jnp.dot(left, right, preferred_element_type=F32)]
    all_to_all x2 -> x1, starting transfers between devices: 16.7 us -> 28.1 us  [dp_sum(): came = lax.all_to_all(value, 'dp', split_axis=0, concat_axis=0, tiled=True)]
    all_to_all x2, waiting for transfers between devices: 17.3 us -> 26.8 us  [ctx_swap(): return lax.all_to_all(value, CTX, split_axis=0, concat_axis=0, tiled=True)]
    dot_general x3 -> x1, matrix products: 16.9 us -> 7.63 us  [against(): lax.dot_general(left, right, (((1,), (1,)), ((), ())), preferred_element_...]
    ppermute x30 -> x29, waiting for transfers between devices: 108 us -> 98.6 us  [exchange(): return lax.ppermute(value, axis, [(i, i ^ bit) for i in range(count)])]
    pallas_call x3, Pallas kernels: 61 us -> 69.8 us  [the longest x1 34.3 us: attention_forward(): pl.pallas_call(functools.partial(forward_kernel, block), grid_spec=pltpu....]
  transfers between devices with their start and end apart: 51 -> 47, of which waited for: 18 -> 22; matrix products, arithmetic and copies ran while one was open for 27% -> 23% of each run, Pallas kernels for 19% -> 20%
where the time goes in v2:
time: 669 us; the launch traced here: 664 us
  waiting for transfers between devices  219 us (33%)
  Pallas kernels  183 us (27%)
  other arithmetic  81.1 us (12%)
  starting transfers between devices  77.7 us (12%)
  local copies, waits for them, and re-layouts  68.4 us (10%)
  matrix products  19.4 us (3%)
  between operations  15.5 us (2%)
    ppermute x29, waiting for transfers between devices, exchange(): return lax.ppermute(value, axis, [(i, i ^ bit) for i in range(count)])  98.6 us
    pallas_call x4, Pallas kernels, feed_forward(): pl.pallas_call(functools.partial(feed_kernel, parts, residual, fresh), gr...  77.7 us
    all_gather x1, waiting for transfers between devices, local(): lax.all_gather(attend_shard.astype(BF16), ('dp', 'hi', 'lo', 'tp'), axis=...  50 us
    pallas_call x2, Pallas kernels, attention_backward(): pl.pallas_call(functools.partial(backward_kernel, block), grid=(steps,),...  36 us
    pallas_call x1, Pallas kernels, attention_forward(): pl.pallas_call(functools.partial(forward_kernel, block), grid_spec=pltpu....  34.3 us
    all_to_all x1, starting transfers between devices, dp_sum(): came = lax.all_to_all(value, 'dp', split_axis=0, concat_axis=0, tiled=True)  28.1 us
    all_to_all x2, waiting for transfers between devices, ctx_swap(): return lax.all_to_all(value, CTX, split_axis=0, concat_axis=0, tiled=True)  26.8 us
    ppermute x4, waiting for transfers between devices, from_streams(): piece = lax.ppermute(taken(value, (stream - step) % batches, 0), CTX, back)  23.4 us
  transfers between devices with their start and end apart: 47, of which 22 were waited for; matrix products, arithmetic and copies ran while one was open for 23% of the time, Pallas kernels for 20%

profile of v2, /device:TPU:0, one launch (start us, length us, event | category | flops | bytes accessed | tf_op | source)
XLA Modules:
  0.0 664.4 jit_solution(17144418798342851588)
XLA Ops:
  12.8 7.6 %collective-permute-start.1 = (bf16[1,128,1664]{2,1,0:T(8,128)(2,1)S(1)}, bf16[1,128,1664]{2,1,0:T(8,128)(2,1)S(1)}, u32[]{:S(2)}, u32[]{:S(2)}) collective-permute-start(bf16[1,128,1664]{2,1,0:T(8,128)(2,1)S(1)} %get-tuple-element.233), channel_id=1, source_target_pairs={{0,2},{1,4},{2,6},{3,0},{4,3},{5,5},{6,7},{7,1},{8,10},{9,12},{10,... | collective-permute-start | bytes 1277960 | tf_op jit(solution)/shard_map/ppermute | solution.py:227
  23.8 10.0 %collective-permute-done.1 = bf16[1,128,1664]{2,1,0:T(8,128)(2,1)S(1)} collective-permute-done((bf16[1,128,1664]{2,1,0:T(8,128)(2,1)S(1)}, bf16[1,128,1664]{2,1,0:T(8,128)(2,1)S(1)}, u32[]{:S(2)}, u32[]{:S(2)}) %collective-permute-start.1) | collective-permute-done | bytes 426016 | tf_op jit(solution)/shard_map/ppermute | solution.py:227
  33.9 6.2 collective-permute-done.2
  50.7 17.5 %all-to-all-done = bf16[8,48,1024]{2,1,0:T(8,128)(2,1)S(1)} async-done(((bf16[8,48,1024]{2,1,0:T(8,128)(2,1)}), bf16[8,48,1024]{2,1,0:T(8,128)(2,1)S(1)}, u32[]{:S(2)}, u32[]{:S(2)}) %all-to-all-start) | async-done | bytes 786464 | tf_op jit(solution)/shard_map/all_to_all | solution.py:209
  84.6 50.0 %all-gather.3.cloned.1.call-done.weight_ref = bf16[1536,4736]{1,0:T(8,128)(2,1)} async-done(((bf16[48,4736]{1,0:T(8,128)(2,1)}), bf16[1536,4736]{1,0:T(8,128)(2,1)}) %all-gather.3.cloned.1.call-update) | async-done | bytes 14549008 | tf_op jit(solution)/shard_map/all_gather | solution.py:742
  145.3 34.3 %attention_forward.1 = (bf16[1024,768]{1,0:T(8,128)(2,1)}, bf16[1024,2048]{1,0:T(8,128)(2,1)}, f32[2,1024,128]{2,1,0:T(8,128)}, bf16[1024,1536]{1,0:T(8,128)(2,1)}) custom-call(s32[1]{0:T(128)} %bitcast.1.member_ref, bf16[1024,1536]{1,0:T(8,128)(2,1)} %fusion.2.input_ref, bf16[1536,4736]{1,0:T(8,128)(2,1)} %all-gather.3.cloned.1.call-done.weight_ref, ...), custom_call_target="tpu_custom_call" | custom-call | flops 1048576 | bytes 1048576 | tf_op jit(solution)/shard_map/attention_forward/pallas_call | solution.py:390
  196.3 42.0 %collective-permute-done.10.refs_0_.refs_2_ = bf16[512,1536]{1,0:T(8,128)(2,1)} collective-permute-done((bf16[512,1536]{1,0:T(8,128)(2,1)S(1)}, bf16[512,1536]{1,0:T(8,128)(2,1)}, u32[]{:S(2)}, u32[]{:S(2)}) %collective-permute-start.10) | collective-permute-done | bytes 1572896 | tf_op jit(solution)/shard_map/ppermute | solution.py:68
  249.3 9.7 %collective-permute-done.12.refs_0_.refs_6_ = bf16[512,768]{1,0:T(8,128)(2,1)} collective-permute-done((bf16[512,768]{1,0:T(8,128)(2,1)S(1)}, bf16[512,768]{1,0:T(8,128)(2,1)}, u32[]{:S(2)}, u32[]{:S(2)}) %collective-permute-start.12) | collective-permute-done | bytes 786464 | tf_op jit(solution)/shard_map/ppermute | solution.py:68
  266.4 31.0 %feed_forward.4 = (bf16[4,1024,1536]{2,1,0:T(8,128)(2,1)}, bf16[8,3,512,512]{3,2,1,0:T(8,128)(2,1)}, bf16[3,512,1536]{2,1,0:T(8,128)(2,1)}) custom-call(s32[3,3]{1,0:T(4,128)} %pad_add_fusion.places_ref, bf16[512,768]{1,0:T(8,128)(2,1)} %collective-permute-done.14.refs_0_.refs_8_, bf16[512,768]{1,0:T(8,128)(2,1)} %collective-permute-done.15.refs_1_.refs_9_, ...), custom_call_target="tpu_custom_call" | custom-call | flops 1048576 | bytes 1048576 | tf_op jit(solution)/shard_map/feed_forward/pallas_call | solution.py:551
  299.3 11.4 %feed_forward.5 = (bf16[4,1024,1536]{2,1,0:T(8,128)(2,1)}, bf16[8,3,512,512]{3,2,1,0:T(8,128)(2,1)}, bf16[1,512,1536]{2,1,0:T(8,128)(2,1)}) custom-call(s32[1,3]{1,0:T(1,128)} %add_bitcast_fusion.6.places_ref, bf16[512,768]{1,0:T(8,128)(2,1)} %collective-permute-done.12.refs_0_.refs_6_, ...), custom_call_target="tpu_custom_call", output_to_operand_aliasing={{0}: (6, {}), {1}: (7, {})} | custom-call | flops 1048576 | bytes 1048576 | tf_op jit(solution)/shard_map/feed_forward/pallas_call | solution.py:551
  315.0 17.4 %feed_forward.6 = (bf16[4,1024,1536]{2,1,0:T(8,128)(2,1)}, bf16[8,3,512,512]{3,2,1,0:T(8,128)(2,1)}, bf16[2,512,1536]{2,1,0:T(8,128)(2,1)}) custom-call(s32[2,3]{1,0:T(2,128)} %pad_add_fusion.3.places_ref, bf16[512,1536]{1,0:T(8,128)(2,1)} %collective-permute-done.10.refs_0_.refs_2_, ...), custom_call_target="tpu_custom_call", output_to_operand_aliasing={{0}: (6, {}), {1}: (7, {})} | custom-call | flops 1048576 | bytes 1048576 | tf_op jit(solution)/shard_map/feed_forward/pallas_call | solution.py:551
  347.5 17.9 %feed_forward.7 = (bf16[4,1024,1536]{2,1,0:T(8,128)(2,1)}, bf16[8,3,512,512]{3,2,1,0:T(8,128)(2,1)}, bf16[2,512,1536]{2,1,0:T(8,128)(2,1)}) custom-call(s32[2,3]{1,0:T(2,128)} %pad_add_fusion.2.places_ref, bf16[512,1536]{1,0:T(8,128)(2,1)} %copy-done.9, bf16[512,1536]{1,0:T(8,128)(2,1)} %copy-done.12, ...), custom_call_target="tpu_custom_call", output_to_operand_aliasing={{0}: (7, {}), {1}: (8, {})} | custom-call | flops 1048576 | bytes 1048576 | tf_op jit(solution)/shard_map/feed_forward/pallas_call | solution.py:551
  365.3 12.8 %down_grads.1.refs_12_ = bf16[4,576,1024]{2,1,0:T(8,128)(2,1)} custom-call(s32[4,2]{1,0:T(4,128)} %pad_add_fusion.1.places_ref, bf16[4,1024,1536]{2,1,0:T(8,128)(2,1)} %all-gather.5.cloned.1.call-done.refs_4_.refs_2_.refs_0_.refs_1_, bf16[4,1024,1536]{2,1,0:T(8,128)(2,1)} %all-gather.5.cloned.1.call-done.refs_4_.refs_2_.refs_0_.refs_1_, ...), custom_call_target="tpu_custom_call" | custom-call | flops 1048576 | bytes 1048576 | tf_op jit(solution)/shard_map/down_grads/pallas_call | solution.py:630
  379.7 22.7 %expand_grads.1 = bf16[4,576,1024]{2,1,0:T(8,128)(2,1)} custom-call(bf16[512,1536]{1,0:T(8,128)(2,1)} %copy-done.9, bf16[512,1536]{1,0:T(8,128)(2,1)} %copy-done.12, bf16[512,1536]{1,0:T(8,128)(2,1)} %collective-permute-done.10.refs_0_.refs_2_, bf16[512,1536]{1,0:T(8,128)(2,1)} %collective-permute-done.16.refs_2_.refs_3_, ...), custom_call_target="tpu_custom_call", output_to_operand_aliasing={{}: (12, {})} | custom-call | flops 1048576 | bytes 1048576 | tf_op jit(solution)/shard_map/expand_grads/pallas_call | solution.py:659
  423.9 18.1 %attention_backward.2 = bf16[1024,768]{1,0:T(8,128)(2,1)} custom-call(bf16[1024,2048]{1,0:T(8,128)(2,1)} %get-tuple-element.81.kept_ref, f32[1024,256]{1,0:T(8,128)} %concatenate.42.table_ref, s32[1024,1]{1,0:T(8,128)} %copy.175.start_ref, f32[2,1024,128]{2,1,0:T(8,128)} %get-tuple-element.82.logsum_ref, bf16[1024,768]{1,0:T(8,128)(2,1)} %get-tuple-element.83.att_ref, ...), custom_call_target="tpu_custom_call" | custom-call | flops 1048576 | bytes 1048576 | tf_op jit(solution)/shard_map/attention_backward/pallas_call | solution.py:432
  461.2 17.9 %attention_backward.3 = bf16[1024,768]{1,0:T(8,128)(2,1)} custom-call(bf16[1024,2048]{1,0:T(8,128)(2,1)} %get-tuple-element.81.kept_ref, f32[1024,256]{1,0:T(8,128)} %concatenate.42.table_ref, s32[1024,1]{1,0:T(8,128)} %copy.175.start_ref, f32[2,1024,128]{2,1,0:T(8,128)} %get-tuple-element.82.logsum_ref, bf16[1024,768]{1,0:T(8,128)(2,1)} %get-tuple-element.83.att_ref, ...), custom_call_target="tpu_custom_call" | custom-call | flops 1048576 | bytes 1048576 | tf_op jit(solution)/shard_map/attention_backward/pallas_call | solution.py:432
  487.6 7.6 %fusion.5 = bf16[1024,1536]{1,0:T(8,128)(2,1)S(1)} fusion(bf16[1024,1536]{1,0:T(8,128)(2,1)S(1)} %pad_maximum_fusion.1, bf16[1536,4736]{1,0:T(8,128)(2,1)} %all-gather.3.cloned.1.call-done.weight_ref, s32[]{:T(128)S(6)} %select_n.266), kind=kOutput, calls=%fused_computation.12 | convolution fusion | flops 4833411072 | bytes 11010052 | tf_op jit(solution)/shard_map/dot_general | solution.py:39
  499.6 15.0 %collective-permute-done.30 = bf16[4,2,1,96,768]{4,3,0,2,1:T(8,128)(2,1)S(1)} collective-permute-done((bf16[4,2,1,96,768]{4,3,0,2,1:T(8,128)(2,1)}, bf16[4,2,1,96,768]{4,3,0,2,1:T(8,128)(2,1)S(1)}, u32[]{:S(2)}, u32[]{:S(2)}) %collective-permute-start.30) | collective-permute-done | bytes 1179680 | tf_op jit(solution)/shard_map/ppermute | solution.py:68
  537.9 9.4 %collective-permute-done.32 = bf16[4,1,1,96,768]{4,3,0,2,1:T(8,128)(2,1)S(1)} collective-permute-done((bf16[4,1,1,96,768]{4,3,0,2,1:T(8,128)(2,1)S(1)}, bf16[4,1,1,96,768]{4,3,0,2,1:T(8,128)(2,1)S(1)}, u32[]{:S(2)}, u32[]{:S(2)}) %collective-permute-start.32) | collective-permute-done | bytes 589856 | tf_op jit(solution)/shard_map/ppermute | solution.py:68
  549.0 28.1 %all-to-all-start.1 = ((bf16[4,96,2304]{2,1,0:T(8,128)(2,1)}), bf16[4,96,2304]{2,1,0:T(8,128)(2,1)S(1)}, u32[]{:S(2)}, u32[]{:S(2)}) async-start(bf16[4,96,2304]{2,1,0:T(8,128)(2,1)} %pad_maximum_fusion.2), calls=%async_computation.2 | async-start | bytes 3538944 | tf_op jit(solution)/shard_map/all_to_all | solution.py:95
  594.6 9.0 %collective-permute-done.34 = bf16[1,128,1536]{2,1,0:T(8,128)(2,1)S(1)} collective-permute-done((bf16[1,128,1536]{2,1,0:T(8,128)(2,1)}, bf16[1,128,1536]{2,1,0:T(8,128)(2,1)S(1)}, u32[]{:S(2)}, u32[]{:S(2)}) %collective-permute-start.34) | collective-permute-done | bytes 393248 | tf_op jit(solution)/shard_map/ppermute | solution.py:239
  604.4 14.4 %collective-permute-done.35 = bf16[1,128,1536]{2,1,0:T(8,128)(2,1)S(1)} collective-permute-done((bf16[1,128,1536]{2,1,0:T(8,128)(2,1)}, bf16[1,128,1536]{2,1,0:T(8,128)(2,1)S(1)}, u32[]{:S(2)}, u32[]{:S(2)}) %collective-permute-start.35) | collective-permute-done | bytes 393248 | tf_op jit(solution)/shard_map/ppermute | solution.py:239
  637.6 9.3 %all-to-all-done.2 = bf16[8,48,1024]{2,1,0:T(8,128)(2,1)S(1)} async-done(((bf16[8,48,1024]{2,1,0:T(8,128)(2,1)}), bf16[8,48,1024]{2,1,0:T(8,128)(2,1)S(1)}, u32[]{:S(2)}, u32[]{:S(2)}) %all-to-all-start.2) | async-done | bytes 786464 | tf_op jit(solution)/shard_map/all_to_all | solution.py:209
  649.5 5.8 multiply_subtract_fusion
  (359 shorter events, 223.7 us)
Async XLA Ops:
  7.2 127.4 %all-gather.3.cloned.1.call-start = ((), (), s32[]{:S(2)}) async-start(), calls=%async_computation.5 | async-start | bytes 15003648 | tf_op jit(solution)/shard_map/all_gather | solution.py:742
  10.8 254.5 %all-gather.5.cloned.1.call-start = ((), (), s32[]{:S(2)}) async-start(), calls=%async_computation.6 | async-start | bytes 14155776 | tf_op jit(solution)/shard_map/all_gather | solution.py:765
  42.3 26.9 %collective-permute-start.4 = (bf16[512,1664]{1,0:T(8,128)(2,1)S(1)}, bf16[512,1664]{1,0:T(8,128)(2,1)}, u32[]{:S(2)}, u32[]{:S(2)}) collective-permute-start(bf16[512,1664]{1,0:T(8,128)(2,1)S(1)} %bitcast.155), channel_id=1, source_target_pairs={{0,1},{1,0},{2,3},{3,2},{4,5},{5,4},{6,7},{7,6},{8,9},{9,8},{10,11... | collective-permute-start | bytes 5111816 | tf_op jit(solution)/shard_map/ppermute | solution.py:68
  44.4 23.7 %all-to-all-start = ((bf16[8,48,1024]{2,1,0:T(8,128)(2,1)}), bf16[8,48,1024]{2,1,0:T(8,128)(2,1)S(1)}, u32[]{:S(2)}, u32[]{:S(2)}) async-start(bf16[8,48,1024]{2,1,0:T(8,128)(2,1)} %reshape.227), calls=%async_computation | async-start | bytes 1572864 | tf_op jit(solution)/shard_map/all_to_all | solution.py:209
  48.0 579.2 %reduce-scatter.5.cloned.1.call-start = ((), (), s32[]{:S(2)}) async-start(), calls=%async_computation.8 | async-start | bytes 5898240 | tf_op jit(solution)/shard_map/reduce_scatter | solution.py:867
  134.6 45.0 %collective-permute-start.5 = (bf16[576,1024]{1,0:T(8,128)(2,1)}, bf16[576,1024]{1,0:T(8,128)(2,1)}, u32[]{:S(2)}, u32[]{:S(2)}) collective-permute-start(bf16[576,1024]{1,0:T(8,128)(2,1)} %pad_maximum_fusion.5), channel_id=1, source_target_pairs={{0,8},{8,16},{16,24},{24,0},{1,9},{9,17},{17,25},{25,1},{2,10},{10... | collective-permute-start | bytes 3538952 | tf_op jit(solution)/shard_map/ppermute | solution.py:73
  190.0 48.3 %collective-permute-start.10 = (bf16[512,1536]{1,0:T(8,128)(2,1)S(1)}, bf16[512,1536]{1,0:T(8,128)(2,1)}, u32[]{:S(2)}, u32[]{:S(2)}) collective-permute-start(bf16[512,1536]{1,0:T(8,128)(2,1)S(1)} %multiply_convert_fusion.refs_0_), channel_id=1, source_target_pairs={{0,2},{2,0},{1,3},{3,1},{4,6},{6,4},{5,7},{7,5},{8,10},{10,8},{9,1... | collective-permute-start | bytes 4718600 | tf_op jit(solution)/shard_map/ppermute | solution.py:68
  191.4 49.6 %collective-permute-start.11 = (bf16[512,1536]{1,0:T(8,128)(2,1)S(1)}, bf16[512,1536]{1,0:T(8,128)(2,1)}, u32[]{:S(2)}, u32[]{:S(2)}) collective-permute-start(bf16[512,1536]{1,0:T(8,128)(2,1)S(1)} %multiply_convert_fusion.refs_0_), channel_id=1, source_target_pairs={{0,4},{4,0},{1,5},{5,1},{2,6},{6,2},{3,7},{7,3},{8,12},{12,8},{9,1... | collective-permute-start | bytes 4718600 | tf_op jit(solution)/shard_map/ppermute | solution.py:68
  192.4 54.8 %collective-permute-start.8 = (bf16[576,1024]{1,0:T(8,128)(2,1)S(1)}, bf16[576,1024]{1,0:T(8,128)(2,1)}, u32[]{:S(2)}, u32[]{:S(2)}) collective-permute-start(bf16[576,1024]{1,0:T(8,128)(2,1)S(1)} %copy-done.18), channel_id=1, source_target_pairs={{0,16},{8,24},{16,0},{24,8},{1,17},{9,25},{17,1},{25,9},{2,18},{10... | collective-permute-start | bytes 3538952 | tf_op jit(solution)/shard_map/ppermute | solution.py:73
  193.9 69.0 %collective-permute-start.9 = (bf16[576,1024]{1,0:T(8,128)(2,1)S(1)}, bf16[576,1024]{1,0:T(8,128)(2,1)S(1)}, u32[]{:S(2)}, u32[]{:S(2)}) collective-permute-start(bf16[576,1024]{1,0:T(8,128)(2,1)S(1)} %copy-done.18), channel_id=1, source_target_pairs={{0,24},{8,0},{16,8},{24,16},{1,25},{9,1},{17,9},{25,17},{2,26},{10... | collective-permute-start | bytes 3538952 | tf_op jit(solution)/shard_map/ppermute | solution.py:73
  299.3 47.0 %collective-permute-start.7 = (bf16[512,1536]{1,0:T(8,128)(2,1)S(1)}, bf16[512,1536]{1,0:T(8,128)(2,1)S(1)}, u32[]{:S(2)}, u32[]{:S(2)}) collective-permute-start(bf16[512,1536]{1,0:T(8,128)(2,1)S(1)} %multiply_convert_fusion.refs_0_), channel_id=1, source_target_pairs={{0,1},{1,0},{2,3},{3,2},{4,5},{5,4},{6,7},{7,6},{8,9},{9,8},{10,11... | collective-permute-start | bytes 4718600 | tf_op jit(solution)/shard_map/ppermute | solution.py:68
  314.2 26.6 %collective-permute-start.20 = (bf16[512,768]{1,0:T(8,128)(2,1)}, bf16[512,768]{1,0:T(8,128)(2,1)}, u32[]{:S(2)}, u32[]{:S(2)}) collective-permute-start(bf16[512,768]{1,0:T(8,128)(2,1)} %get-tuple-element.240), channel_id=1, source_target_pairs={{0,2},{2,0},{1,3},{3,1},{4,6},{6,4},{5,7},{7,5},{8,10},{10,8},{9,1... | collective-permute-start | bytes 2359304 | tf_op jit(solution)/shard_map/ppermute | solution.py:68
  339.1 39.0 %collective-permute-start.22 = (bf16[2,512,768]{2,1,0:T(8,128)(2,1)}, bf16[2,512,768]{2,1,0:T(8,128)(2,1)}, u32[]{:S(2)}, u32[]{:S(2)}) collective-permute-start(bf16[2,512,768]{2,1,0:T(8,128)(2,1)} %pad_maximum_fusion.3), channel_id=1, source_target_pairs={{0,2},{2,0},{1,3},{3,1},{4,6},{6,4},{5,7},{7,5},{8,10},{10,8},{9,1... | collective-permute-start | bytes 4718600 | tf_op jit(solution)/shard_map/ppermute | solution.py:68
  343.4 36.3 %collective-permute-start.23 = (bf16[2,512,768]{2,1,0:T(8,128)(2,1)}, bf16[2,512,768]{2,1,0:T(8,128)(2,1)}, u32[]{:S(2)}, u32[]{:S(2)}) collective-permute-start(bf16[2,512,768]{2,1,0:T(8,128)(2,1)} %pad_maximum_fusion.4), channel_id=1, source_target_pairs={{0,4},{4,0},{1,5},{5,1},{2,6},{6,2},{3,7},{7,3},{8,12},{12,8},{9,1... | collective-permute-start | bytes 4718600 | tf_op jit(solution)/shard_map/ppermute | solution.py:68
  402.5 255.2 %reduce-scatter.3.cloned.1.call-start = ((), (), s32[]{:S(2)}) async-start(), calls=%async_computation.7 | async-start | bytes 14155776 | tf_op jit(solution)/shard_map/reduce_scatter | solution.py:866
  452.0 29.4 %collective-permute-start.27 = (bf16[4,2,1,96,384]{4,3,2,1,0:T(8,128)(2,1)}, bf16[4,2,1,96,384]{4,3,2,1,0:T(8,128)(2,1)S(1)}, u32[]{:S(2)}, u32[]{:S(2)}) collective-permute-start(bf16[4,2,1,96,384]{4,3,2,1,0:T(8,128)(2,1)} %constant_dynamic-slice_fusion.7), channel_id=1, source_target_pairs={{0,2},{2,0},{1,3},{3,1},{4,6},{6,4},{5,7},{7,5},{8,10},{10,8},{9,1... | collective-permute-start | bytes 1769480 | tf_op jit(solution)/shard_map/ppermute | solution.py:68
  452.9 28.5 %collective-permute-start.26 = (bf16[4,1,2,96,384]{4,3,2,1,0:T(8,128)(2,1)}, bf16[4,1,2,96,384]{4,3,2,1,0:T(8,128)(2,1)}, u32[]{:S(2)}, u32[]{:S(2)}) collective-permute-start(bf16[4,1,2,96,384]{4,3,2,1,0:T(8,128)(2,1)} %constant_dynamic-slice_fusion.8), channel_id=1, source_target_pairs={{0,4},{4,0},{1,5},{5,1},{2,6},{6,2},{3,7},{7,3},{8,12},{12,8},{9,1... | collective-permute-start | bytes 1769480 | tf_op jit(solution)/shard_map/ppermute | solution.py:68
  460.0 39.6 %collective-permute-start.29 = (bf16[4,1,2,96,768]{4,3,2,1,0:T(8,128)(2,1)}, bf16[4,1,2,96,768]{4,3,2,1,0:T(8,128)(2,1)}, u32[]{:S(2)}, u32[]{:S(2)}) collective-permute-start(bf16[4,1,2,96,768]{4,3,2,1,0:T(8,128)(2,1)} %constant_dynamic-slice_fusion.6), channel_id=1, source_target_pairs={{0,4},{4,0},{1,5},{5,1},{2,6},{6,2},{3,7},{7,3},{8,12},{12,8},{9,1... | collective-permute-start | bytes 3538952 | tf_op jit(solution)/shard_map/ppermute | solution.py:68
  486.4 28.1 %collective-permute-start.30 = (bf16[4,2,1,96,768]{4,3,0,2,1:T(8,128)(2,1)}, bf16[4,2,1,96,768]{4,3,0,2,1:T(8,128)(2,1)S(1)}, u32[]{:S(2)}, u32[]{:S(2)}) collective-permute-start(bf16[4,2,1,96,768]{4,3,0,2,1:T(8,128)(2,1)} %copy.197), channel_id=1, source_target_pairs={{0,2},{2,0},{1,3},{3,1},{4,6},{6,4},{5,7},{7,5},{8,10},{10,8},{9,1... | collective-permute-start | bytes 3538952 | tf_op jit(solution)/shard_map/ppermute | solution.py:68
  498.1 32.5 %collective-permute-start.28 = (bf16[512,1536]{1,0:T(8,128)(2,1)}, bf16[512,1536]{1,0:T(8,128)(2,1)}, u32[]{:S(2)}, u32[]{:S(2)}) collective-permute-start(bf16[512,1536]{1,0:T(8,128)(2,1)} %dynamic-slice_bitcast_fusion), channel_id=1, source_target_pairs={{0,1},{1,0},{2,3},{3,2},{4,5},{5,4},{6,7},{7,6},{8,9},{9,8},{10,11... | collective-permute-start | bytes 4718600 | tf_op jit(solution)/shard_map/ppermute | solution.py:68
  521.4 26.0 %collective-permute-start.32 = (bf16[4,1,1,96,768]{4,3,0,2,1:T(8,128)(2,1)S(1)}, bf16[4,1,1,96,768]{4,3,0,2,1:T(8,128)(2,1)S(1)}, u32[]{:S(2)}, u32[]{:S(2)}) collective-permute-start(bf16[4,1,1,96,768]{4,3,0,2,1:T(8,128)(2,1)S(1)} %add_convert_fusion.6), channel_id=1, source_target_pairs={{0,4},{4,0},{1,5},{5,1},{2,6},{6,2},{3,7},{7,3},{8,12},{12,8},{9,1... | collective-permute-start | bytes 1769480 | tf_op jit(solution)/shard_map/ppermute | solution.py:68
  549.0 70.6 %all-to-all-start.1 = ((bf16[4,96,2304]{2,1,0:T(8,128)(2,1)}), bf16[4,96,2304]{2,1,0:T(8,128)(2,1)S(1)}, u32[]{:S(2)}, u32[]{:S(2)}) async-start(bf16[4,96,2304]{2,1,0:T(8,128)(2,1)} %pad_maximum_fusion.2), calls=%async_computation.2 | async-start | bytes 3538944 | tf_op jit(solution)/shard_map/all_to_all | solution.py:95
  587.8 31.0 %collective-permute-start.35 = (bf16[1,128,1536]{2,1,0:T(8,128)(2,1)}, bf16[1,128,1536]{2,1,0:T(8,128)(2,1)S(1)}, u32[]{:S(2)}, u32[]{:S(2)}) collective-permute-start(bf16[1,128,1536]{2,1,0:T(8,128)(2,1)} %get-tuple-element.236), channel_id=1, source_target_pairs={{4,0},{6,1},{0,2},{2,3},{5,4},{7,5},{1,6},{3,7},{12,8},{14,9},{8,1... | collective-permute-start | bytes 1179656 | tf_op jit(solution)/shard_map/ppermute | solution.py:239
  589.8 30.2 %collective-permute-start.36 = (bf16[1,128,1536]{2,1,0:T(8,128)(2,1)}, bf16[1,128,1536]{2,1,0:T(8,128)(2,1)S(1)}, u32[]{:S(2)}, u32[]{:S(2)}) collective-permute-start(bf16[1,128,1536]{2,1,0:T(8,128)(2,1)} %get-tuple-element.235), channel_id=1, source_target_pairs={{6,0},{0,1},{2,2},{4,3},{7,4},{1,5},{3,6},{5,7},{14,8},{8,9},{10,1... | collective-permute-start | bytes 1179656 | tf_op jit(solution)/shard_map/ppermute | solution.py:239
  (76 other events, 827.2 us)
Sparse Core Ops, SparseCore 0:
  11.5 123.0 all-gather.2
  136.5 81.4 all-gather.4
  402.6 97.7 reduce-scatter.4
  504.4 123.6 reduce-scatter.2

commit v3 on v2

--- a/solution.py
+++ b/solution.py
@@ -495,8 +495,8 @@
     if residual:
         hidden_ref, refs = refs[0], refs[1:]
     if not fresh:
-        refs = refs[2:]
-    out_ref, terms_ref, dc_ref, c_buffer, sems = refs
+        refs = refs[3:]
+    out_ref, mixed_ref, both_ref, dc_ref, c_buffer, sems = refs
     hidden = down_ref.shape[0]
     c = fetched(parts, c_refs, c_buffer, sems)
     gate = product(c, expand_ref[:, :hidden])
@@ -507,10 +507,10 @@
     mixed = (active * up).astype(BF16)
     dgate = (dm * up * sigmoid * (1.0 + gate * (1.0 - sigmoid))).astype(BF16)
     dup = (dm * active).astype(BF16)
-    terms_ref[0, 0] = mixed
-    terms_ref[0, 1] = dgate
-    terms_ref[0, 2] = dup
-    dc = against(dgate, expand_ref[:, :hidden]) + against(dup, expand_ref[:, hidden:])
+    mixed_ref[0] = mixed
+    both_ref[0, :, :hidden] = dgate
+    both_ref[0, :, hidden:] = dup
+    dc = against(both_ref[0], expand_ref[...])
     dc_ref[0] = dc.astype(BF16)
     out = product(mixed, down_ref[...])
     if residual:
@@ -545,9 +545,9 @@
         in_specs.append(pl.BlockSpec((own, width), whole, pipeline_mode=single))
     aliases = {}
     if not fresh:
-        aliases = {len(operands): 0, len(operands) + 1: 1}
+        aliases = {len(operands) + index: index for index in range(3)}
         operands += list(before)
-        in_specs += [pl.BlockSpec(memory_space=pl.ANY)] * 2
+        in_specs += [pl.BlockSpec(memory_space=pl.ANY)] * 3
     return pl.pallas_call(
         functools.partial(feed_kernel, parts, residual, fresh),
         grid_spec=pltpu.PrefetchScalarGridSpec(
@@ -556,14 +556,16 @@
             in_specs=in_specs,
             out_specs=[
                 token,
-                pl.BlockSpec((1, 3, own, hidden), lambda s, p: (p[s, 0], 0, 0, 0)),
+                pl.BlockSpec((1, own, hidden), lambda s, p: (p[s, 0], 0, 0)),
+                pl.BlockSpec((1, own, 2 * hidden), lambda s, p: (p[s, 0], 0, 0)),
                 pl.BlockSpec((1, own, width), lambda s, p: (s, 0, 0)),
             ],
             scratch_shapes=c_scratch(parts, own, width),
         ),
         out_shape=[
             jax.ShapeDtypeStruct(dy.shape, BF16),
-            jax.ShapeDtypeStruct((blocks, 3, own, hidden), BF16),
+            jax.ShapeDtypeStruct((blocks, own, hidden), BF16),
+            jax.ShapeDtypeStruct((blocks, own, 2 * hidden), BF16),
             jax.ShapeDtypeStruct((steps, own, width), BF16),
         ],
         input_output_aliases=aliases,
@@ -573,19 +575,19 @@
     )(*operands)
 
 
-def accumulate(total_ref, value, columns=slice(None)):
+def accumulate(total_ref, value):
     @pl.when(pl.program_id(0) == 0)
     def _():
-        total_ref[:, columns] = value
+        total_ref[...] = value
 
     @pl.when(pl.program_id(0) > 0)
     def _():
-        total_ref[:, columns] += value
+        total_ref[...] += value
 
 
 def down_grad_kernel(rows, count, places_ref, *refs):
     dy_refs, (mixed_ref, out_ref, total_ref, dy_buffer) = refs[:count], refs[count:]
-    own, hidden = mixed_ref.shape[2], mixed_ref.shape[3]
+    _, own, hidden = mixed_ref.shape
     for index in range(count):
         dy_buffer[index * own : (index + 1) * own, :] = dy_refs[index][0]
     mixed = mixed_ref[...].reshape(count * own, hidden)
@@ -605,21 +607,18 @@
 def expand_grad_kernel(parts, *refs):
     number = sum(sum(rows) for rows in parts)
     c_refs, refs = refs[:number], refs[number:]
-    dgate_ref, dup_ref, _, out_ref, total_ref, c_buffer, sems = refs
-    count, _, own, hidden = dgate_ref.shape
+    both_ref, _, out_ref, total_ref, c_buffer, sems = refs
+    count, own, hidden_two = both_ref.shape
     c = fetched(parts, c_refs, c_buffer, sems)
-    dgate = dgate_ref[...].reshape(count * own, hidden)
-    dup = dup_ref[...].reshape(count * own, hidden)
-    accumulate(total_ref, tokens_product(c, dgate), slice(0, hidden))
-    accumulate(total_ref, tokens_product(c, dup), slice(hidden, None))
+    accumulate(total_ref, tokens_product(c, both_ref[...].reshape(count * own, hidden_two)))
 
     @pl.when(pl.program_id(0) == pl.num_programs(0) - 1)
     def _():
         out_ref[...] = total_ref[...].astype(BF16).reshape(out_ref.shape)
 
 
-def down_grads(places, dy, terms, n_dp, rows_before):
-    blocks, _, own, hidden = terms.shape
+def down_grads(places, dy, mixed, n_dp, rows_before):
+    blocks, own, hidden = mixed.shape
     count = blocks // 4
     width = dy.shape[2]
     packed = hidden * width // (2 * hidden) // n_dp
@@ -633,7 +632,7 @@
             num_scalar_prefetch=1,
             grid=(4,),
             in_specs=[dy_spec(index) for index in range(count)]
-            + [pl.BlockSpec((count, 1, own, hidden), lambda s, p: (s, 0, 0, 0))],
+            + [pl.BlockSpec((count, own, hidden), lambda s, p: (s, 0, 0))],
             out_specs=pl.BlockSpec(
                 (n_dp, packed, 2 * hidden),
                 lambda s, p: (0, rows_before // packed, 0),
@@ -647,12 +646,12 @@
         compiler_params=pltpu.CompilerParams(vmem_limit_bytes=VMEM_LIMIT),
         cost_estimate=SMALL_COST,
         name="down_grads",
-    )(places, *([dy] * count), terms)
-
-
-def expand_grads(c, terms, packed, rows):
+    )(places, *([dy] * count), mixed)
+
+
+def expand_grads(c, both, packed, rows):
     parts, flat = counted(c)
-    blocks, _, own, hidden = terms.shape
+    blocks, own, hidden_two = both.shape
     count = blocks // 4
     n_dp = packed.shape[0]
     width = n_dp * rows
@@ -661,21 +660,20 @@
         grid=(4,),
         in_specs=[pl.BlockSpec(memory_space=pl.ANY)] * len(flat)
         + [
-            pl.BlockSpec((count, 1, own, hidden), lambda s: (s, 1, 0, 0)),
-            pl.BlockSpec((count, 1, own, hidden), lambda s: (s, 2, 0, 0)),
+            pl.BlockSpec((count, own, hidden_two), lambda s: (s, 0, 0)),
             pl.BlockSpec(memory_space=pl.ANY),
         ],
         out_specs=pl.BlockSpec(
-            (n_dp, rows, 2 * hidden), lambda s: (0, 0, 0), pipeline_mode=pl.Buffered(1)
+            (n_dp, rows, hidden_two), lambda s: (0, 0, 0), pipeline_mode=pl.Buffered(1)
         ),
-        scratch_shapes=[pltpu.VMEM((width, 2 * hidden), F32)]
+        scratch_shapes=[pltpu.VMEM((width, hidden_two), F32)]
         + c_scratch(parts, count * own, width),
         out_shape=jax.ShapeDtypeStruct(packed.shape, BF16),
-        input_output_aliases={len(flat) + 2: 0},
+        input_output_aliases={len(flat) + 1: 0},
         compiler_params=pltpu.CompilerParams(vmem_limit_bytes=VMEM_LIMIT),
         cost_estimate=SMALL_COST,
         name="expand_grads",
-    )(*flat, terms, terms, packed)
+    )(*flat, both, packed)
 
 
 def local(
@@ -820,12 +818,12 @@
         return feed_forward(rows, c, dy_all, expand_all, down_all, blocks, before, residual)
 
     def after_calls(*ready):
-        return lax.optimization_barrier((out_all, terms) + ready)[:2]
+        return lax.optimization_barrier((out_all, mixed, both) + ready)[:3]
 
     members = list(range(n_tp))
     far_order = [(r, member) for member in members[1:] for r in (3, 1, 2)]
-    out_all, terms, first_dc = feed_call(far_order)
-    out_all, terms, corner_dc = feed_call([(3, 0)], (out_all, terms))
+    out_all, mixed, both, first_dc = feed_call(far_order)
+    out_all, mixed, both, corner_dc = feed_call([(3, 0)], (out_all, mixed, both))
     first_dc = first_dc.reshape(n_tp - 1, 3, own, width)
     first_came = list(first_dc)
     if n_tp == 2:
@@ -835,7 +833,7 @@
     corner = (corner[:, :middle], corner[:, middle:])
     corner_left = exchange(corner[0], "lo")
     corner_right = exchange(corner[1], "hi")
-    out_all, terms, second_dc = feed_call([(1, 0), (2, 0)], after_calls(*corner))
+    out_all, mixed, both, second_dc = feed_call([(1, 0), (2, 0)], after_calls(*corner))
     beside, across = relative_sum(
         [second_dc] + [value[1:] for value in first_came], n_tp == 2
     ).astype(BF16)
@@ -845,17 +843,17 @@
     right_sent = jnp.stack(
         [across[:, middle:], total_of([across[:, :middle], corner_left])]
     ).astype(BF16)
-    out_all, terms, near_dc = feed_call(
+    out_all, mixed, both, near_dc = feed_call(
         [(0, member) for member in members], after_calls(left_sent, right_sent), hidden_res
     )
     near = relative_sum([near_dc[member] for member in members])
     chip_rows = jnp.stack([place_row(relative, 0)[1:] for relative in range(4)])
-    packed = down_grads(chip_rows, dy_all, terms, n_dp, rows_expand)
+    packed = down_grads(chip_rows, dy_all, mixed, n_dp, rows_expand)
     left_came = after(exchange(left_sent, "lo"), packed)
     right_came = after(exchange(right_sent, "hi"), packed)
     feed_terms = expand_grads(
         [[pieces_of(relative, member) for member in members] for relative in range(4)],
-        terms,
+        both,
         after(packed, left_came, right_came),
         rows_expand,
     )
@@ -892,7 +890,14 @@
     joined_parts = [heads_back(0, branch_all)]
     in_parts = [tokens_product(first_in, joined_parts[0]).astype(BF16)]
 
-    branch_late = after(branch_all, joined_parts[0])
+    if len(cuts) > 2:
+        joined_parts.append(heads_back(1, after(branch_all, in_parts[0])))
+    in_terms = [plane_stage(plane_grid(in_parts[0]), orders[0][0])]
+    if len(cuts) > 2:
+        in_parts.append(tokens_product(first_in, joined_parts[1]).astype(BF16))
+        in_terms.append(plane_stage(plane_grid(in_parts[1]), orders[1][0]))
+
+    branch_late = after(branch_all, in_parts[-1])
     if n_tp == 2:
         heads_rows = qwidth // n_tp
 
@@ -911,25 +916,18 @@
     half = part_out // 2
     out_parts = [out_term[:, :half], out_term[:, half:]]
 
-    if len(cuts) > 2:
-        joined_parts.append(heads_back(1, after(branch_all, in_parts[0], out_term)))
-    in_terms = [plane_stage(plane_grid(in_parts[0]), orders[0][0])]
     out_terms = [
         plane_stage(plane_grid(part), order[0]) for part, order in zip(out_parts, orders)
     ]
-    came = [terms[-1] for terms in out_terms]
-    came = [after(value, joined_parts[-1]) for value in came]
-    for terms, value in zip(out_terms, came):
-        terms[-1] = value
-    if len(cuts) > 2:
-        late_in = after(first_in, *came)
-        in_parts.append(tokens_product(late_in, joined_parts[1]).astype(BF16))
-        in_terms.append(plane_stage(plane_grid(in_parts[1]), orders[1][0]))
-    late = in_terms[-1][-1]
+    feed_sum = after(feed_sum, in_parts[-1])
+    expand_rows = ctx_swap(feed_sum[:rows_expand].reshape(n_ctx, row_in, -1))
+    late = [in_terms[-1][-1]] + [terms[-1] for terms in out_terms]
+    in_terms[-1][-1] = after(*late, expand_rows)
     for terms in out_terms:
-        terms[-1] = after(terms[-1], late)
-    in_terms[0][-1] = after(in_terms[0][-1], late)
-    feed_sum = after(feed_sum, late)
+        terms[-1] = after(terms[-1], late[0])
+    in_terms[0][-1] = after(in_terms[0][-1], *late, expand_rows)
+    expand_sum = expand_rows.reshape(n_ctx, row_in, 2, n_dp, row_down)
+    expand_sum = expand_sum.transpose(1, 2, 3, 0, 4).reshape(row_in, 2 * FF).astype(F32)
     in_terms = [plane_stage(terms, order[1]) for terms, order in zip(in_terms, orders)]
     out_terms = [plane_stage(terms, order[1]) for terms, order in zip(out_terms, orders)]
     joined_all = after(jnp.concatenate(joined_parts, axis=1), in_parts[-1])
@@ -942,9 +940,6 @@
     rows = group_swap(rows.astype(low)).astype(F32).transpose(1, 0, 2)
     in_sum = rows[:, :, :part_in].reshape(row_in, joined_width)
     out_sum = rows[:, :, part_in:].reshape(row_in, width)
-    expand_rows = feed_sum[:rows_expand].reshape(n_ctx, row_in, -1)
-    expand_sum = ctx_swap(expand_rows).reshape(n_ctx, row_in, 2, n_dp, row_down)
-    expand_sum = expand_sum.transpose(1, 2, 3, 0, 4).reshape(row_in, 2 * FF).astype(F32)
     contract_sum = unpacked_rows(feed_sum[rows_expand:].astype(F32), row_down, width)
 
     inv_one = lax.rsqrt(jnp.mean(resid * resid, axis=-1, keepdims=True) + EPSILON)

time: 669 us -> 674 us (level)
  waiting for transfers between devices: 219 us -> 231 us
  Pallas kernels: 183 us -> 176 us
    ppermute x4, waiting for transfers between devices: 23.4 us -> 5.79 us  [from_streams(): piece = lax.ppermute(taken(value, (stream - step) % batches, 0), CTX, back)]
    all_to_all x2, waiting for transfers between devices: 26.8 us -> 37.4 us  [ctx_swap(): return lax.all_to_all(value, CTX, split_axis=0, concat_axis=0, tiled=True)]
    ppermute x29, waiting for transfers between devices: 98.6 us -> 108 us  [exchange(): return lax.ppermute(value, axis, [(i, i ^ bit) for i in range(count)])]
    all_to_all x1, waiting for transfers between devices: 0.01 us -> 9.07 us  [dp_sum(): came = lax.all_to_all(value, 'dp', split_axis=0, concat_axis=0, tiled=True)]
    pallas_call x4, Pallas kernels: 77.7 us -> 70.1 us  [feed_forward(): pl.pallas_call(functools.partial(feed_kernel, parts, residual, fresh), gr...]
    unnamed x116 -> x112, local copies, waits for them, and re-layouts: 18.9 us -> 14.2 us
where the time goes in v3:
time: 674 us; the launch traced here: 665 us
  waiting for transfers between devices  231 us (34%)
  Pallas kernels  176 us (26%)
  other arithmetic  81.7 us (12%)
  starting transfers between devices  73.3 us (11%)
  local copies, waits for them, and re-layouts  66.5 us (10%)
  matrix products  20.8 us (3%)
  between operations  15.8 us (2%)
    ppermute x29, waiting for transfers between devices, exchange(): return lax.ppermute(value, axis, [(i, i ^ bit) for i in range(count)])  108 us
    pallas_call x4, Pallas kernels, feed_forward(): pl.pallas_call(functools.partial(feed_kernel, parts, residual, fresh), gr...  70.1 us
    all_gather x1, waiting for transfers between devices, local(): lax.all_gather(attend_shard.astype(BF16), ('dp', 'hi', 'lo', 'tp'), axis=...  50 us
    all_to_all x2, waiting for transfers between devices, ctx_swap(): return lax.all_to_all(value, CTX, split_axis=0, concat_axis=0, tiled=True)  37.4 us
    pallas_call x2, Pallas kernels, attention_backward(): pl.pallas_call(functools.partial(backward_kernel, block), grid=(steps,),...  36.2 us
    pallas_call x1, Pallas kernels, attention_forward(): pl.pallas_call(functools.partial(forward_kernel, block), grid_spec=pltpu....  34.8 us
    all_to_all x1, starting transfers between devices, dp_sum(): came = lax.all_to_all(value, 'dp', split_axis=0, concat_axis=0, tiled=True)  24.2 us
    pallas_call x1, Pallas kernels, expand_grads(): pl.pallas_call(functools.partial(expand_grad_kernel, parts), grid=(4,), i...  22.3 us
  transfers between devices with their start and end apart: 47, of which 22 were waited for; matrix products, arithmetic and copies ran while one was open for 23% of the time, Pallas kernels for 20%

profile of v3, /device:TPU:0, one launch (start us, length us, event | category | flops | bytes accessed | tf_op | source)
XLA Modules:
  0.0 665.2 jit_solution(13201960619706295707)
XLA Ops:
  12.8 7.6 %collective-permute-start.1 = (bf16[1,128,1664]{2,1,0:T(8,128)(2,1)S(1)}, bf16[1,128,1664]{2,1,0:T(8,128)(2,1)S(1)}, u32[]{:S(2)}, u32[]{:S(2)}) collective-permute-start(bf16[1,128,1664]{2,1,0:T(8,128)(2,1)S(1)} %get-tuple-element.241), channel_id=1, source_target_pairs={{0,2},{1,4},{2,6},{3,0},{4,3},{5,5},{6,7},{7,1},{8,10},{9,12},{10,... | collective-permute-start | bytes 1277960 | tf_op jit(solution)/shard_map/ppermute | solution.py:227
  23.8 10.0 %collective-permute-done.1 = bf16[1,128,1664]{2,1,0:T(8,128)(2,1)S(1)} collective-permute-done((bf16[1,128,1664]{2,1,0:T(8,128)(2,1)S(1)}, bf16[1,128,1664]{2,1,0:T(8,128)(2,1)S(1)}, u32[]{:S(2)}, u32[]{:S(2)}) %collective-permute-start.1) | collective-permute-done | bytes 426016 | tf_op jit(solution)/shard_map/ppermute | solution.py:227
  33.9 6.2 collective-permute-done.2
  50.7 17.5 %all-to-all-done = bf16[8,48,1024]{2,1,0:T(8,128)(2,1)S(1)} async-done(((bf16[8,48,1024]{2,1,0:T(8,128)(2,1)}), bf16[8,48,1024]{2,1,0:T(8,128)(2,1)S(1)}, u32[]{:S(2)}, u32[]{:S(2)}) %all-to-all-start) | async-done | bytes 786464 | tf_op jit(solution)/shard_map/all_to_all | solution.py:209
  84.6 50.0 %all-gather.3.cloned.1.call-done.weight_ref = bf16[1536,4736]{1,0:T(8,128)(2,1)} async-done(((bf16[48,4736]{1,0:T(8,128)(2,1)}), bf16[1536,4736]{1,0:T(8,128)(2,1)}) %all-gather.3.cloned.1.call-update) | async-done | bytes 14549008 | tf_op jit(solution)/shard_map/all_gather | solution.py:740
  145.2 34.8 %attention_forward.1 = (bf16[1024,768]{1,0:T(8,128)(2,1)}, bf16[1024,2048]{1,0:T(8,128)(2,1)}, f32[2,1024,128]{2,1,0:T(8,128)}, bf16[1024,1536]{1,0:T(8,128)(2,1)}) custom-call(s32[1]{0:T(128)} %bitcast.1.member_ref, bf16[1024,1536]{1,0:T(8,128)(2,1)} %fusion.2.input_ref, bf16[1536,4736]{1,0:T(8,128)(2,1)} %all-gather.3.cloned.1.call-done.weight_ref, ...), custom_call_target="tpu_custom_call" | custom-call | flops 1048576 | bytes 1048576 | tf_op jit(solution)/shard_map/attention_forward/pallas_call | solution.py:390
  196.5 41.8 %collective-permute-done.10.refs_0_.refs_2_ = bf16[512,1536]{1,0:T(8,128)(2,1)} collective-permute-done((bf16[512,1536]{1,0:T(8,128)(2,1)S(1)}, bf16[512,1536]{1,0:T(8,128)(2,1)}, u32[]{:S(2)}, u32[]{:S(2)}) %collective-permute-start.10) | collective-permute-done | bytes 1572896 | tf_op jit(solution)/shard_map/ppermute | solution.py:68
  249.5 9.4 %collective-permute-done.12.refs_0_.refs_6_ = bf16[512,768]{1,0:T(8,128)(2,1)} collective-permute-done((bf16[512,768]{1,0:T(8,128)(2,1)S(1)}, bf16[512,768]{1,0:T(8,128)(2,1)}, u32[]{:S(2)}, u32[]{:S(2)}) %collective-permute-start.12) | collective-permute-done | bytes 786464 | tf_op jit(solution)/shard_map/ppermute | solution.py:68
  266.4 22.5 %feed_forward.4 = (bf16[4,1024,1536]{2,1,0:T(8,128)(2,1)}, bf16[8,512,512]{2,1,0:T(8,128)(2,1)}, bf16[8,512,1024]{2,1,0:T(8,128)(2,1)}, bf16[3,512,1536]{2,1,0:T(8,128)(2,1)}) custom-call(s32[3,3]{1,0:T(4,128)} %pad_add_fusion.places_ref, bf16[512,768]{1,0:T(8,128)(2,1)} %collective-permute-done.14.refs_0_.refs_8_, ...), custom_call_target="tpu_custom_call" | custom-call | flops 1048576 | bytes 1048576 | tf_op jit(solution)/shard_map/feed_forward/pallas_call | solution.py:551
  290.8 11.4 %feed_forward.5 = (bf16[4,1024,1536]{2,1,0:T(8,128)(2,1)}, bf16[8,512,512]{2,1,0:T(8,128)(2,1)}, bf16[8,512,1024]{2,1,0:T(8,128)(2,1)}, bf16[1,512,1536]{2,1,0:T(8,128)(2,1)}) custom-call(s32[1,3]{1,0:T(1,128)} %add_bitcast_fusion.6.places_ref, ...), custom_call_target="tpu_custom_call", output_to_operand_aliasing={{0}: (6, {}), {1}: (7, {}), {2}: (8, {})} | custom-call | flops 1048576 | bytes 1048576 | tf_op jit(solution)/shard_map/feed_forward/pallas_call | solution.py:551
  306.5 17.3 %feed_forward.6 = (bf16[4,1024,1536]{2,1,0:T(8,128)(2,1)}, bf16[8,512,512]{2,1,0:T(8,128)(2,1)}, bf16[8,512,1024]{2,1,0:T(8,128)(2,1)}, bf16[2,512,1536]{2,1,0:T(8,128)(2,1)}) custom-call(s32[2,3]{1,0:T(2,128)} %pad_add_fusion.3.places_ref, ...), custom_call_target="tpu_custom_call", output_to_operand_aliasing={{0}: (6, {}), {1}: (7, {}), {2}: (8, {})} | custom-call | flops 1048576 | bytes 1048576 | tf_op jit(solution)/shard_map/feed_forward/pallas_call | solution.py:551
  338.9 18.9 %feed_forward.7 = (bf16[4,1024,1536]{2,1,0:T(8,128)(2,1)}, bf16[8,512,512]{2,1,0:T(8,128)(2,1)}, bf16[8,512,1024]{2,1,0:T(8,128)(2,1)}, bf16[2,512,1536]{2,1,0:T(8,128)(2,1)}) custom-call(s32[2,3]{1,0:T(2,128)} %pad_add_fusion.2.places_ref, bf16[512,1536]{1,0:T(8,128)(2,1)} %copy-done.9, ...), custom_call_target="tpu_custom_call", output_to_operand_aliasing={{0}: (7, {}), {1}: (8, {}), {2}: (9, {})} | custom-call | flops 1048576 | bytes 1048576 | tf_op jit(solution)/shard_map/feed_forward/pallas_call | solution.py:551
  357.8 12.8 %down_grads.1.refs_11_ = bf16[4,576,1024]{2,1,0:T(8,128)(2,1)} custom-call(s32[4,2]{1,0:T(4,128)} %pad_add_fusion.1.places_ref, bf16[4,1024,1536]{2,1,0:T(8,128)(2,1)} %all-gather.5.cloned.1.call-done.refs_4_.refs_2_.refs_0_.refs_1_, bf16[4,1024,1536]{2,1,0:T(8,128)(2,1)} %all-gather.5.cloned.1.call-done.refs_4_.refs_2_.refs_0_.refs_1_, ...), custom_call_target="tpu_custom_call" | custom-call | flops 1048576 | bytes 1048576 | tf_op jit(solution)/shard_map/down_grads/pallas_call | solution.py:629
  371.1 22.3 %expand_grads.1 = bf16[4,576,1024]{2,1,0:T(8,128)(2,1)} custom-call(bf16[512,1536]{1,0:T(8,128)(2,1)} %copy-done.9, bf16[512,1536]{1,0:T(8,128)(2,1)} %copy-done.18, bf16[512,1536]{1,0:T(8,128)(2,1)} %collective-permute-done.10.refs_0_.refs_2_, bf16[512,1536]{1,0:T(8,128)(2,1)} %collective-permute-done.16.refs_2_.refs_3_, ...), custom_call_target="tpu_custom_call", output_to_operand_aliasing={{}: (11, {})} | custom-call | flops 1048576 | bytes 1048576 | tf_op jit(solution)/shard_map/expand_grads/pallas_call | solution.py:658
  414.2 18.1 %attention_backward.2 = bf16[1024,768]{1,0:T(8,128)(2,1)} custom-call(bf16[1024,2048]{1,0:T(8,128)(2,1)} %get-tuple-element.91.kept_ref, f32[1024,256]{1,0:T(8,128)} %concatenate.42.table_ref, s32[1024,1]{1,0:T(8,128)} %copy.178.start_ref, f32[2,1024,128]{2,1,0:T(8,128)} %get-tuple-element.92.logsum_ref, bf16[1024,768]{1,0:T(8,128)(2,1)} %get-tuple-element.93.att_ref, ...), custom_call_target="tpu_custom_call" | custom-call | flops 1048576 | bytes 1048576 | tf_op jit(solution)/shard_map/attention_backward/pallas_call | solution.py:432
  432.3 5.5 convolution_convert_fusion.1
  437.8 18.1 %attention_backward.3 = bf16[1024,768]{1,0:T(8,128)(2,1)} custom-call(bf16[1024,2048]{1,0:T(8,128)(2,1)} %get-tuple-element.91.kept_ref, f32[1024,256]{1,0:T(8,128)} %concatenate.42.table_ref, s32[1024,1]{1,0:T(8,128)} %copy.178.start_ref, f32[2,1024,128]{2,1,0:T(8,128)} %get-tuple-element.92.logsum_ref, bf16[1024,768]{1,0:T(8,128)(2,1)} %get-tuple-element.93.att_ref, ...), custom_call_target="tpu_custom_call" | custom-call | flops 1048576 | bytes 1048576 | tf_op jit(solution)/shard_map/attention_backward/pallas_call | solution.py:432
  464.9 7.6 %fusion.5 = bf16[1024,1536]{1,0:T(8,128)(2,1)S(1)} fusion(bf16[1024,1536]{1,0:T(8,128)(2,1)S(1)} %pad_maximum_fusion.1, bf16[1536,4736]{1,0:T(8,128)(2,1)} %all-gather.3.cloned.1.call-done.weight_ref, s32[]{:T(128)S(6)} %select_n.263), kind=kOutput, calls=%fused_computation.12 | convolution fusion | flops 4833411072 | bytes 11010052 | tf_op jit(solution)/shard_map/dot_general | solution.py:39
  498.1 7.1 %collective-permute-done.30 = bf16[4,2,1,96,384]{4,3,2,1,0:T(8,128)(2,1)} collective-permute-done((bf16[4,2,1,96,384]{4,3,2,1,0:T(8,128)(2,1)}, bf16[4,2,1,96,384]{4,3,2,1,0:T(8,128)(2,1)}, u32[]{:S(2)}, u32[]{:S(2)}) %collective-permute-start.30) | collective-permute-done | bytes 589856 | tf_op jit(solution)/shard_map/ppermute | solution.py:68
  513.1 13.6 %collective-permute-done.38 = bf16[4,1,1,96,384]{4,3,2,1,0:T(8,128)(2,1)S(1)} collective-permute-done((bf16[4,1,1,96,384]{4,3,2,1,0:T(8,128)(2,1)S(1)}, bf16[4,1,1,96,384]{4,3,2,1,0:T(8,128)(2,1)S(1)}, u32[]{:S(2)}, u32[]{:S(2)}) %collective-permute-start.38) | collective-permute-done | bytes 294944 | tf_op jit(solution)/shard_map/ppermute | solution.py:68
  535.7 20.0 %all-to-all-done.1 = bf16[8,48,1024]{2,1,0:T(8,128)(2,1)S(1)} async-done(((bf16[8,48,1024]{2,1,0:T(8,128)(2,1)}), bf16[8,48,1024]{2,1,0:T(8,128)(2,1)S(1)}, u32[]{:S(2)}, u32[]{:S(2)}) %all-to-all-start.1) | async-done | bytes 786464 | tf_op jit(solution)/shard_map/all_to_all | solution.py:209
  565.2 16.4 %collective-permute-done.31 = bf16[4,1,1,96,768]{4,3,2,1,0:T(8,128)(2,1)} collective-permute-done((bf16[4,1,1,96,768]{4,3,2,1,0:T(8,128)(2,1)}, bf16[4,1,1,96,768]{4,3,2,1,0:T(8,128)(2,1)}, u32[]{:S(2)}, u32[]{:S(2)}) %collective-permute-start.31) | collective-permute-done | bytes 589856 | tf_op jit(solution)/shard_map/ppermute | solution.py:68
  586.1 24.2 %all-to-all-start.2 = ((bf16[4,96,2304]{2,1,0:T(8,128)(2,1)}), bf16[4,96,2304]{2,1,0:T(8,128)(2,1)S(1)}, u32[]{:S(2)}, u32[]{:S(2)}) async-start(bf16[4,96,2304]{2,1,0:T(8,128)(2,1)} %pad_maximum_fusion.2), calls=%async_computation.4 | async-start | bytes 3538944 | tf_op jit(solution)/shard_map/all_to_all | solution.py:95
  638.6 9.1 %all-to-all-done.2 = bf16[4,96,2304]{2,1,0:T(8,128)(2,1)S(1)} async-done(((bf16[4,96,2304]{2,1,0:T(8,128)(2,1)}), bf16[4,96,2304]{2,1,0:T(8,128)(2,1)S(1)}, u32[]{:S(2)}, u32[]{:S(2)}) %all-to-all-start.2) | async-done | bytes 1769504 | tf_op jit(solution)/shard_map/all_to_all | solution.py:95
  (355 shorter events, 227.1 us)
Async XLA Ops:
  7.2 127.4 %all-gather.3.cloned.1.call-start = ((), (), s32[]{:S(2)}) async-start(), calls=%async_computation.5 | async-start | bytes 15003648 | tf_op jit(solution)/shard_map/all_gather | solution.py:740
  10.7 254.6 %all-gather.5.cloned.1.call-start = ((), (), s32[]{:S(2)}) async-start(), calls=%async_computation.6 | async-start | bytes 14155776 | tf_op jit(solution)/shard_map/all_gather | solution.py:763
  42.3 26.9 %collective-permute-start.4 = (bf16[512,1664]{1,0:T(8,128)(2,1)S(1)}, bf16[512,1664]{1,0:T(8,128)(2,1)}, u32[]{:S(2)}, u32[]{:S(2)}) collective-permute-start(bf16[512,1664]{1,0:T(8,128)(2,1)S(1)} %bitcast.155), channel_id=1, source_target_pairs={{0,1},{1,0},{2,3},{3,2},{4,5},{5,4},{6,7},{7,6},{8,9},{9,8},{10,11... | collective-permute-start | bytes 5111816 | tf_op jit(solution)/shard_map/ppermute | solution.py:68
  44.4 23.7 %all-to-all-start = ((bf16[8,48,1024]{2,1,0:T(8,128)(2,1)}), bf16[8,48,1024]{2,1,0:T(8,128)(2,1)S(1)}, u32[]{:S(2)}, u32[]{:S(2)}) async-start(bf16[8,48,1024]{2,1,0:T(8,128)(2,1)} %reshape.227), calls=%async_computation | async-start | bytes 1572864 | tf_op jit(solution)/shard_map/all_to_all | solution.py:209
  48.0 479.8 %reduce-scatter.5.cloned.1.call-start = ((), (), s32[]{:S(2)}) async-start(), calls=%async_computation.8 | async-start | bytes 5898240 | tf_op jit(solution)/shard_map/reduce_scatter | solution.py:865
  134.6 45.4 %collective-permute-start.5 = (bf16[576,1024]{1,0:T(8,128)(2,1)}, bf16[576,1024]{1,0:T(8,128)(2,1)}, u32[]{:S(2)}, u32[]{:S(2)}) collective-permute-start(bf16[576,1024]{1,0:T(8,128)(2,1)} %pad_maximum_fusion.5), channel_id=1, source_target_pairs={{0,8},{8,16},{16,24},{24,0},{1,9},{9,17},{17,25},{25,1},{2,10},{10... | collective-permute-start | bytes 3538952 | tf_op jit(solution)/shard_map/ppermute | solution.py:73
  190.4 47.9 %collective-permute-start.10 = (bf16[512,1536]{1,0:T(8,128)(2,1)S(1)}, bf16[512,1536]{1,0:T(8,128)(2,1)}, u32[]{:S(2)}, u32[]{:S(2)}) collective-permute-start(bf16[512,1536]{1,0:T(8,128)(2,1)S(1)} %multiply_convert_fusion.refs_0_), channel_id=1, source_target_pairs={{0,2},{2,0},{1,3},{3,1},{4,6},{6,4},{5,7},{7,5},{8,10},{10,8},{9,1... | collective-permute-start | bytes 4718600 | tf_op jit(solution)/shard_map/ppermute | solution.py:68
  191.8 49.2 %collective-permute-start.11 = (bf16[512,1536]{1,0:T(8,128)(2,1)S(1)}, bf16[512,1536]{1,0:T(8,128)(2,1)}, u32[]{:S(2)}, u32[]{:S(2)}) collective-permute-start(bf16[512,1536]{1,0:T(8,128)(2,1)S(1)} %multiply_convert_fusion.refs_0_), channel_id=1, source_target_pairs={{0,4},{4,0},{1,5},{5,1},{2,6},{6,2},{3,7},{7,3},{8,12},{12,8},{9,1... | collective-permute-start | bytes 4718600 | tf_op jit(solution)/shard_map/ppermute | solution.py:68
  192.6 54.8 %collective-permute-start.8 = (bf16[576,1024]{1,0:T(8,128)(2,1)S(1)}, bf16[576,1024]{1,0:T(8,128)(2,1)}, u32[]{:S(2)}, u32[]{:S(2)}) collective-permute-start(bf16[576,1024]{1,0:T(8,128)(2,1)S(1)} %copy-done.19), channel_id=1, source_target_pairs={{0,16},{8,24},{16,0},{24,8},{1,17},{9,25},{17,1},{25,9},{2,18},{10... | collective-permute-start | bytes 3538952 | tf_op jit(solution)/shard_map/ppermute | solution.py:73
  194.3 68.6 %collective-permute-start.9 = (bf16[576,1024]{1,0:T(8,128)(2,1)S(1)}, bf16[576,1024]{1,0:T(8,128)(2,1)S(1)}, u32[]{:S(2)}, u32[]{:S(2)}) collective-permute-start(bf16[576,1024]{1,0:T(8,128)(2,1)S(1)} %copy-done.19), channel_id=1, source_target_pairs={{0,24},{8,0},{16,8},{24,16},{1,25},{9,1},{17,9},{25,17},{2,26},{10... | collective-permute-start | bytes 3538952 | tf_op jit(solution)/shard_map/ppermute | solution.py:73
  243.5 21.8 %collective-permute-start.16 = (bf16[512,1536]{1,0:T(8,128)(2,1)}, bf16[512,1536]{1,0:T(8,128)(2,1)}, u32[]{:S(2)}, u32[]{:S(2)}) collective-permute-start(bf16[512,1536]{1,0:T(8,128)(2,1)} %collective-permute-done.10.refs_0_.refs_2_), channel_id=1, source_target_pairs={{0,1},{1,0},{2,3},{3,2},{4,5},{5,4},{6,7},{7,6},{8,9},{9,8},{10,11... | collective-permute-start | bytes 4718600 | tf_op jit(solution)/shard_map/ppermute | solution.py:68
  290.8 46.9 %collective-permute-start.7 = (bf16[512,1536]{1,0:T(8,128)(2,1)S(1)}, bf16[512,1536]{1,0:T(8,128)(2,1)S(1)}, u32[]{:S(2)}, u32[]{:S(2)}) collective-permute-start(bf16[512,1536]{1,0:T(8,128)(2,1)S(1)} %multiply_convert_fusion.refs_0_), channel_id=1, source_target_pairs={{0,1},{1,0},{2,3},{3,2},{4,5},{5,4},{6,7},{7,6},{8,9},{9,8},{10,11... | collective-permute-start | bytes 4718600 | tf_op jit(solution)/shard_map/ppermute | solution.py:68
  305.7 26.4 %collective-permute-start.20 = (bf16[512,768]{1,0:T(8,128)(2,1)}, bf16[512,768]{1,0:T(8,128)(2,1)}, u32[]{:S(2)}, u32[]{:S(2)}) collective-permute-start(bf16[512,768]{1,0:T(8,128)(2,1)} %get-tuple-element.248), channel_id=1, source_target_pairs={{0,2},{2,0},{1,3},{3,1},{4,6},{6,4},{5,7},{7,5},{8,10},{10,8},{9,1... | collective-permute-start | bytes 2359304 | tf_op jit(solution)/shard_map/ppermute | solution.py:68
  330.5 40.2 %collective-permute-start.22 = (bf16[2,512,768]{2,1,0:T(8,128)(2,1)}, bf16[2,512,768]{2,1,0:T(8,128)(2,1)}, u32[]{:S(2)}, u32[]{:S(2)}) collective-permute-start(bf16[2,512,768]{2,1,0:T(8,128)(2,1)} %pad_maximum_fusion.3), channel_id=1, source_target_pairs={{0,2},{2,0},{1,3},{3,1},{4,6},{6,4},{5,7},{7,5},{8,10},{10,8},{9,1... | collective-permute-start | bytes 4718600 | tf_op jit(solution)/shard_map/ppermute | solution.py:68
  334.7 36.3 %collective-permute-start.23 = (bf16[2,512,768]{2,1,0:T(8,128)(2,1)}, bf16[2,512,768]{2,1,0:T(8,128)(2,1)}, u32[]{:S(2)}, u32[]{:S(2)}) collective-permute-start(bf16[2,512,768]{2,1,0:T(8,128)(2,1)} %pad_maximum_fusion.4), channel_id=1, source_target_pairs={{0,4},{4,0},{1,5},{5,1},{2,6},{6,2},{3,7},{7,3},{8,12},{12,8},{9,1... | collective-permute-start | bytes 4718600 | tf_op jit(solution)/shard_map/ppermute | solution.py:68
  393.4 264.7 %reduce-scatter.3.cloned.1.call-start = ((), (), s32[]{:S(2)}) async-start(), calls=%async_computation.7 | async-start | bytes 14155776 | tf_op jit(solution)/shard_map/reduce_scatter | solution.py:864
  463.4 29.0 %collective-permute-start.27 = (bf16[4,2,1,96,768]{4,3,0,2,1:T(8,128)(2,1)}, bf16[4,2,1,96,768]{4,3,0,2,1:T(8,128)(2,1)S(1)}, u32[]{:S(2)}, u32[]{:S(2)}) collective-permute-start(bf16[4,2,1,96,768]{4,3,0,2,1:T(8,128)(2,1)} %copy.200), channel_id=1, source_target_pairs={{0,2},{2,0},{1,3},{3,1},{4,6},{6,4},{5,7},{7,5},{8,10},{10,8},{9,1... | collective-permute-start | bytes 3538952 | tf_op jit(solution)/shard_map/ppermute | solution.py:68
  473.9 34.1 %collective-permute-start.25 = (bf16[512,1536]{1,0:T(8,128)(2,1)}, bf16[512,1536]{1,0:T(8,128)(2,1)}, u32[]{:S(2)}, u32[]{:S(2)}) collective-permute-start(bf16[512,1536]{1,0:T(8,128)(2,1)} %dynamic-slice_bitcast_fusion), channel_id=1, source_target_pairs={{0,1},{1,0},{2,3},{3,2},{4,5},{5,4},{6,7},{7,6},{8,9},{9,8},{10,11... | collective-permute-start | bytes 4718600 | tf_op jit(solution)/shard_map/ppermute | solution.py:68
  477.6 27.6 %collective-permute-start.30 = (bf16[4,2,1,96,384]{4,3,2,1,0:T(8,128)(2,1)}, bf16[4,2,1,96,384]{4,3,2,1,0:T(8,128)(2,1)}, u32[]{:S(2)}, u32[]{:S(2)}) collective-permute-start(bf16[4,2,1,96,384]{4,3,2,1,0:T(8,128)(2,1)} %constant_dynamic-slice_fusion.5), channel_id=1, source_target_pairs={{0,2},{2,0},{1,3},{3,1},{4,6},{6,4},{5,7},{7,5},{8,10},{10,8},{9,1... | collective-permute-start | bytes 1769480 | tf_op jit(solution)/shard_map/ppermute | solution.py:68
  487.0 48.7 %collective-permute-start.26 = (bf16[4,1,2,96,768]{4,3,2,1,0:T(8,128)(2,1)}, bf16[4,1,2,96,768]{4,3,2,1,0:T(8,128)(2,1)}, u32[]{:S(2)}, u32[]{:S(2)}) collective-permute-start(bf16[4,1,2,96,768]{4,3,2,1,0:T(8,128)(2,1)} %constant_dynamic-slice_fusion.8), channel_id=1, source_target_pairs={{0,4},{4,0},{1,5},{5,1},{2,6},{6,2},{3,7},{7,3},{8,12},{12,8},{9,1... | collective-permute-start | bytes 3538952 | tf_op jit(solution)/shard_map/ppermute | solution.py:68
  529.9 25.8 %all-to-all-start.1 = ((bf16[8,48,1024]{2,1,0:T(8,128)(2,1)}), bf16[8,48,1024]{2,1,0:T(8,128)(2,1)S(1)}, u32[]{:S(2)}, u32[]{:S(2)}) async-start(bf16[8,48,1024]{2,1,0:T(8,128)(2,1)} %bitcast.52), calls=%async_computation.3 | async-start | bytes 1572864 | tf_op jit(solution)/shard_map/all_to_all | solution.py:209
  558.0 23.6 %collective-permute-start.31 = (bf16[4,1,1,96,768]{4,3,2,1,0:T(8,128)(2,1)}, bf16[4,1,1,96,768]{4,3,2,1,0:T(8,128)(2,1)}, u32[]{:S(2)}, u32[]{:S(2)}) collective-permute-start(bf16[4,1,1,96,768]{4,3,2,1,0:T(8,128)(2,1)} %add_convert_fusion.7), channel_id=1, source_target_pairs={{0,2},{2,0},{1,3},{3,1},{4,6},{6,4},{5,7},{7,5},{8,10},{10,8},{9,1... | collective-permute-start | bytes 1769480 | tf_op jit(solution)/shard_map/ppermute | solution.py:68
  559.4 23.9 %collective-permute-start.32 = (bf16[4,1,1,96,768]{4,3,0,2,1:T(8,128)(2,1)S(1)}, bf16[4,1,1,96,768]{4,3,0,2,1:T(8,128)(2,1)}, u32[]{:S(2)}, u32[]{:S(2)}) collective-permute-start(bf16[4,1,1,96,768]{4,3,0,2,1:T(8,128)(2,1)S(1)} %add_convert_fusion.6), channel_id=1, source_target_pairs={{0,4},{4,0},{1,5},{5,1},{2,6},{6,2},{3,7},{7,3},{8,12},{12,8},{9,1... | collective-permute-start | bytes 1769480 | tf_op jit(solution)/shard_map/ppermute | solution.py:68
  586.1 61.5 %all-to-all-start.2 = ((bf16[4,96,2304]{2,1,0:T(8,128)(2,1)}), bf16[4,96,2304]{2,1,0:T(8,128)(2,1)S(1)}, u32[]{:S(2)}, u32[]{:S(2)}) async-start(bf16[4,96,2304]{2,1,0:T(8,128)(2,1)} %pad_maximum_fusion.2), calls=%async_computation.4 | async-start | bytes 3538944 | tf_op jit(solution)/shard_map/all_to_all | solution.py:95
  (74 other events, 841.2 us)
Sparse Core Ops, SparseCore 0:
  11.5 123.0 all-gather.2
  136.5 81.1 all-gather.4
  393.5 97.9 reduce-scatter.4
  495.4 114.2 reduce-scatter.2
